TPU v7x, 32 devices: a whole 2x2x4 slice. The times are simulated.
32 devices in a mesh: dp: 16 (over z, y, x), tensor: 2 (over core).
Axes of the slice: x: 2, y: 2, z: 4, core: 2. Of those that a mesh axis runs over, the one named last changes fastest.
Arguments:
- tokens: bfloat16 [32, 680, 1024], P('dp', 'tensor'), may hold values from -40 to 40
- condition: bfloat16 [32, 1024], P('dp'), may hold values from -6 to 6
- scale_index: int32 [32, 680], P('dp'), may hold values from 0 to 9, never falling along the last dimension, each value on 1 to 256 neighbouring positions
- ada_weight: bfloat16 [1024, 6, 1024], P('tensor', None, 'dp'), may hold values from -0.1875 to 0.1875
- ada_bias: bfloat16 [6, 16, 64], P(None, 'tensor', 'dp'), may hold values from -3 to 3
- qkv_weight: bfloat16 [3, 1024, 1024], P(None, 'dp', 'tensor'), may hold values from -0.1875 to 0.1875
- query_bias: bfloat16 [16, 64], P('tensor', 'dp'), may hold values from -3 to 3
- value_bias: bfloat16 [16, 64], P('tensor', 'dp'), may hold values from -3 to 3
- head_scale: float32 [16], P('tensor'), may hold values from 2 to 3.2
- proj_weight: bfloat16 [1024, 1024], P('tensor', 'dp'), may hold values from -0.375 to 0.375
- proj_bias: bfloat16 [16, 64], P('tensor', 'dp'), may hold values from -2 to 2
- up_weight: bfloat16 [1024, 4096], P('dp', 'tensor'), may hold values from -0.1875 to 0.1875
- up_bias: bfloat16 [16, 256], P('tensor', 'dp'), may hold values from -3 to 3
- down_weight: bfloat16 [4096, 1024], P('tensor', 'dp'), may hold values from -0.09375 to 0.09375
- down_bias: bfloat16 [16, 64], P('tensor', 'dp'), may hold values from -2 to 2
- out_grad: bfloat16 [32, 680, 1024], P('dp', 'tensor'), may hold values from -6 to 6
Outputs:
- output: float32 [32, 680, 1024], P('dp', 'tensor')
- grad_tokens: float32 [32, 680, 1024], P('dp', 'tensor')
- grad_condition: float32 [32, 1024], P('dp', 'tensor')
- grad_ada_weight: float32 [1024, 6, 1024], P('tensor', None, 'dp')
- grad_ada_bias: float32 [6, 16, 64], P(None, 'tensor', 'dp')
- grad_qkv_weight: float32 [3, 1024, 1024], P(None, 'dp', 'tensor')
- grad_query_bias: float32 [16, 64], P('tensor', 'dp')
- grad_value_bias: float32 [16, 64], P('tensor', 'dp')
- grad_head_scale: float32 [16], P('tensor')
- grad_proj_weight: float32 [1024, 1024], P('tensor', 'dp')
- grad_proj_bias: float32 [16, 64], P('tensor', 'dp')
- grad_up_weight: float32 [1024, 4096], P('dp', 'tensor')
- grad_up_bias: float32 [16, 256], P('tensor', 'dp')
- grad_down_weight: float32 [4096, 1024], P('tensor', 'dp')
- grad_down_bias: float32 [16, 64], P('tensor', 'dp')
Inputs may be any that keep to these rules, and one draw needn't show every extreme that they name: `scale_index`: in each sequence the scale of a token never falls along its positions; each of the 10 scales has 1 to 256 tokens.
All inputs are finite; a program needn't handle non-finite values.
Results may differ from a plain program's by a relative error of at most 0.025.
Values may be sent and summed in bfloat16 or wider, within the bound.
A program may use at most 384 MiB of HBM per device.

v0:
```python
import jax
import jax.numpy as jnp
from jax import lax
from jax.sharding import PartitionSpec as P

NORM_EPS = 1e-06
HEAD_EPS = 1e-06
GELU_COEF = 0.7978845608028654
GELU_CUBE = 0.044715


def normalize(values):
    centred = values - jnp.mean(values, axis=-1, keepdims=True)
    inverse = lax.rsqrt(jnp.mean(centred * centred, axis=-1, keepdims=True) + NORM_EPS)
    return (centred * inverse, inverse)


def norm_back(grad_normed, normed, inverse):
    return inverse * (
        grad_normed
        - jnp.mean(grad_normed, axis=-1, keepdims=True)
        - normed * jnp.mean(grad_normed * normed, axis=-1, keepdims=True)
    )


def gelu_slope(hidden):
    inner = jnp.tanh(GELU_COEF * (hidden + GELU_CUBE * hidden * hidden * hidden))
    return 0.5 * (1.0 + inner) + 0.5 * hidden * (1.0 - inner * inner) * GELU_COEF * (
        1.0 + 3.0 * GELU_CUBE * hidden * hidden
    )


def masked_scores(query_unit, key_unit, scale_factor, scale_row):
    query_low = (query_unit * scale_factor).astype(jnp.bfloat16)
    key_low = key_unit.astype(jnp.bfloat16)
    scores = jnp.einsum("qhe,khe->hqk", query_low, key_low, preferred_element_type=jnp.float32)
    allowed = scale_row[None, :] <= scale_row[:, None]
    return (jnp.where(allowed[None, :, :], scores, -1e30), query_low, key_low)


def attention_core(mixed_all, qkv_full, query_bias_part, value_bias_part, head_scale, scale_row):
    part_width = qkv_full.shape[2]
    part_heads = head_scale.shape[0]
    head_dim = part_width // part_heads
    seq_len = scale_row.shape[0]
    projected = jnp.einsum("ld,jdc->jlc", mixed_all, qkv_full, preferred_element_type=jnp.float32)
    queries = (projected[0] + query_bias_part.reshape(part_width).astype(jnp.float32)).reshape(
        seq_len, part_heads, head_dim
    )
    keys_raw = projected[1].reshape(seq_len, part_heads, head_dim)
    values_low = (projected[2] + value_bias_part.reshape(part_width).astype(jnp.float32)).astype(
        jnp.bfloat16
    )
    values_low = values_low.reshape(seq_len, part_heads, head_dim)
    query_inverse = lax.rsqrt(jnp.sum(queries * queries, axis=-1, keepdims=True) + HEAD_EPS)
    key_inverse = lax.rsqrt(jnp.sum(keys_raw * keys_raw, axis=-1, keepdims=True) + HEAD_EPS)
    query_unit = queries * query_inverse
    key_unit = keys_raw * key_inverse
    scale_factor = jnp.exp(head_scale)[:, None]
    scores, query_low, key_low = masked_scores(query_unit, key_unit, scale_factor, scale_row)
    row_max = jnp.max(scores, axis=-1, keepdims=True)
    weights_exp = jnp.exp(scores - row_max)
    row_total = jnp.sum(weights_exp, axis=-1, keepdims=True)
    attn_prob = weights_exp / row_total
    log_norm = row_max + jnp.log(row_total)
    attended = jnp.einsum(
        "hqk,khe->qhe",
        attn_prob.astype(jnp.bfloat16),
        values_low,
        preferred_element_type=jnp.float32,
    )
    attended = attended.reshape(seq_len, part_width).astype(jnp.bfloat16)
    return (attended, (query_unit, key_unit, query_inverse, key_inverse, values_low, log_norm))


def forward_step(weights, token_rows, condition_row, scale_row, head_scale):
    (
        ada_full,
        ada_bias_part,
        qkv_full,
        query_bias_part,
        value_bias_part,
        proj_full,
        proj_bias_part,
        up_full,
        up_bias_part,
        down_full,
        down_bias_part,
    ) = weights
    width = token_rows.shape[1]
    part_width = qkv_full.shape[2]
    col_start = lax.axis_index("tensor") * part_width
    cond_rows = lax.dynamic_slice_in_dim(
        condition_row.astype(jnp.float32), col_start, part_width, 0
    )
    silu_rows = jax.nn.silu(cond_rows).astype(jnp.bfloat16)
    mod_terms = jnp.einsum("r,rjc->jc", silu_rows, ada_full, preferred_element_type=jnp.float32)
    own_cols = jnp.concatenate(
        [
            ada_bias_part.reshape(6, part_width),
            proj_bias_part.reshape(1, part_width),
            down_bias_part.reshape(1, part_width),
        ],
        axis=0,
    ).astype(jnp.float32)
    placed = lax.dynamic_update_slice(jnp.zeros((8, width), jnp.float32), own_cols, (0, col_start))
    local_mod = placed + jnp.concatenate([mod_terms, jnp.zeros((2, width), jnp.float32)], axis=0)
    modulation = lax.psum(local_mod, "tensor")
    inputs = token_rows.astype(jnp.float32)
    normed_attn, inverse_attn = normalize(inputs)
    mixed_attn = (normed_attn * (1.0 + modulation[2]) + modulation[4]).astype(jnp.bfloat16)
    mixed_all = lax.all_gather(mixed_attn, "tensor", axis=0, tiled=True)
    attended, attn_kept = attention_core(
        mixed_all, qkv_full, query_bias_part, value_bias_part, head_scale, scale_row
    )
    branch_attn = (
        lax.psum_scatter(
            jnp.dot(attended, proj_full, preferred_element_type=jnp.float32).astype(jnp.bfloat16),
            "tensor",
            scatter_dimension=0,
            tiled=True,
        ).astype(jnp.float32)
        + modulation[6]
    )
    middle = inputs + modulation[0] * branch_attn
    normed_mlp, inverse_mlp = normalize(middle)
    mixed_mlp = (normed_mlp * (1.0 + modulation[3]) + modulation[5]).astype(jnp.bfloat16)
    mlp_all = lax.all_gather(mixed_mlp, "tensor", axis=0, tiled=True)
    hidden = jnp.dot(mlp_all, up_full, preferred_element_type=jnp.float32) + up_bias_part.reshape(
        -1
    ).astype(jnp.float32)
    activated = jax.nn.gelu(hidden, approximate=True).astype(jnp.bfloat16)
    branch_mlp = (
        lax.psum_scatter(
            jnp.dot(activated, down_full, preferred_element_type=jnp.float32).astype(jnp.bfloat16),
            "tensor",
            scatter_dimension=0,
            tiled=True,
        ).astype(jnp.float32)
        + modulation[7]
    )
    output = middle + modulation[1] * branch_mlp
    query_unit, key_unit, query_inverse, key_inverse, values_low, log_norm = attn_kept
    kept = (
        modulation,
        normed_attn,
        inverse_attn,
        mixed_all,
        query_unit,
        key_unit,
        query_inverse,
        key_inverse,
        values_low,
        log_norm,
        attended,
        branch_attn,
        normed_mlp,
        inverse_mlp,
        mlp_all,
        hidden,
        activated,
        branch_mlp,
    )
    return (output, kept)


def backward_step(weights, kept, token_grad, condition_row, scale_row, head_scale):
    (
        ada_full,
        ada_bias_part,
        qkv_full,
        query_bias_part,
        value_bias_part,
        proj_full,
        proj_bias_part,
        up_full,
        up_bias_part,
        down_full,
        down_bias_part,
    ) = weights
    (
        modulation,
        normed_attn,
        inverse_attn,
        mixed_all,
        query_unit,
        key_unit,
        query_inverse,
        key_inverse,
        values_low,
        log_norm,
        attended,
        branch_attn,
        normed_mlp,
        inverse_mlp,
        mlp_all,
        hidden,
        activated,
        branch_mlp,
    ) = kept
    part_width = qkv_full.shape[2]
    part_heads = head_scale.shape[0]
    head_dim = part_width // part_heads
    seq_len = scale_row.shape[0]
    scale_factor = jnp.exp(head_scale)[:, None]
    grad_rows = token_grad.astype(jnp.float32)
    grad_branch_mlp = grad_rows * modulation[1]
    grad_gamma_mlp = jnp.sum(grad_rows * branch_mlp, axis=0)
    grad_down_bias = jnp.sum(grad_branch_mlp, axis=0)
    grad_mlp_all = lax.all_gather(
        grad_branch_mlp.astype(jnp.bfloat16), "tensor", axis=0, tiled=True
    )
    grad_down = jnp.einsum("lf,ld->fd", activated, grad_mlp_all, preferred_element_type=jnp.float32)
    grad_act = jnp.einsum("ld,fd->lf", grad_mlp_all, down_full, preferred_element_type=jnp.float32)
    grad_hidden = grad_act * gelu_slope(hidden)
    grad_up_bias = jnp.sum(grad_hidden, axis=0)
    hidden_low = grad_hidden.astype(jnp.bfloat16)
    grad_up = jnp.einsum("ld,lf->df", mlp_all, hidden_low, preferred_element_type=jnp.float32)
    grad_mixed_mlp = lax.psum_scatter(
        jnp.einsum("lf,df->ld", hidden_low, up_full, preferred_element_type=jnp.float32).astype(
            jnp.bfloat16
        ),
        "tensor",
        scatter_dimension=0,
        tiled=True,
    ).astype(jnp.float32)
    grad_scale_mlp = jnp.sum(grad_mixed_mlp * normed_mlp, axis=0)
    grad_shift_mlp = jnp.sum(grad_mixed_mlp, axis=0)
    grad_middle = grad_rows + norm_back(
        grad_mixed_mlp * (1.0 + modulation[3]), normed_mlp, inverse_mlp
    )
    grad_branch_attn = grad_middle * modulation[0]
    grad_gamma_attn = jnp.sum(grad_middle * branch_attn, axis=0)
    grad_proj_bias = jnp.sum(grad_branch_attn, axis=0)
    grad_attn_all = lax.all_gather(
        grad_branch_attn.astype(jnp.bfloat16), "tensor", axis=0, tiled=True
    )
    grad_proj = jnp.einsum("lc,ld->cd", attended, grad_attn_all, preferred_element_type=jnp.float32)
    grad_attended = jnp.einsum(
        "ld,cd->lc", grad_attn_all, proj_full, preferred_element_type=jnp.float32
    )
    grad_attended = grad_attended.astype(jnp.bfloat16).reshape(seq_len, part_heads, head_dim)
    scores, query_low, key_low = masked_scores(query_unit, key_unit, scale_factor, scale_row)
    attn_prob = jnp.exp(scores - log_norm)
    grad_prob = jnp.einsum(
        "qhe,khe->hqk", grad_attended, values_low, preferred_element_type=jnp.float32
    )
    row_dot = jnp.sum(attn_prob * grad_prob, axis=-1, keepdims=True)
    grad_scores = (attn_prob * (grad_prob - row_dot)).astype(jnp.bfloat16)
    grad_values = jnp.einsum(
        "hqk,qhe->khe",
        attn_prob.astype(jnp.bfloat16),
        grad_attended,
        preferred_element_type=jnp.float32,
    )
    grad_query_scaled = jnp.einsum(
        "hqk,khe->qhe", grad_scores, key_low, preferred_element_type=jnp.float32
    )
    grad_key_unit = jnp.einsum(
        "hqk,qhe->khe", grad_scores, query_low, preferred_element_type=jnp.float32
    )
    grad_head_scale = jnp.sum(grad_query_scaled * query_unit, axis=(0, 2)) * jnp.exp(head_scale)
    grad_query_unit = grad_query_scaled * scale_factor
    grad_queries = query_inverse * (
        grad_query_unit - query_unit * jnp.sum(grad_query_unit * query_unit, axis=-1, keepdims=True)
    )
    grad_keys = key_inverse * (
        grad_key_unit - key_unit * jnp.sum(grad_key_unit * key_unit, axis=-1, keepdims=True)
    )
    grad_query_bias = jnp.sum(grad_queries, axis=0)
    grad_value_bias = jnp.sum(grad_values, axis=0)
    grad_projected = (
        jnp.stack([grad_queries, grad_keys, grad_values])
        .reshape(3, seq_len, part_width)
        .astype(jnp.bfloat16)
    )
    grad_qkv = jnp.einsum(
        "ld,jlc->jdc", mixed_all, grad_projected, preferred_element_type=jnp.float32
    )
    grad_mixed_attn = lax.psum_scatter(
        jnp.einsum(
            "jlc,jdc->ld", grad_projected, qkv_full, preferred_element_type=jnp.float32
        ).astype(jnp.bfloat16),
        "tensor",
        scatter_dimension=0,
        tiled=True,
    ).astype(jnp.float32)
    grad_scale_attn = jnp.sum(grad_mixed_attn * normed_attn, axis=0)
    grad_shift_attn = jnp.sum(grad_mixed_attn, axis=0)
    grad_inputs = grad_middle + norm_back(
        grad_mixed_attn * (1.0 + modulation[2]), normed_attn, inverse_attn
    )
    mod_rows = jnp.stack(
        [
            grad_gamma_attn,
            grad_gamma_mlp,
            grad_scale_attn,
            grad_scale_mlp,
            grad_shift_attn,
            grad_shift_mlp,
            grad_proj_bias,
            grad_down_bias,
        ]
    )
    grad_modulation = lax.psum(mod_rows.astype(jnp.bfloat16), "tensor").astype(jnp.float32)
    col_start = lax.axis_index("tensor") * part_width
    cond_rows = lax.dynamic_slice_in_dim(
        condition_row.astype(jnp.float32), col_start, part_width, 0
    )
    silu_rows = jax.nn.silu(cond_rows).astype(jnp.bfloat16)
    mod_low = grad_modulation[:6].astype(jnp.bfloat16)
    grad_ada = jnp.einsum("r,jc->rjc", silu_rows, mod_low, preferred_element_type=jnp.float32)
    grad_silu = jnp.einsum("jc,rjc->r", mod_low, ada_full, preferred_element_type=jnp.float32)
    sigmoid_rows = jax.nn.sigmoid(cond_rows)
    grad_condition = grad_silu * sigmoid_rows * (1.0 + cond_rows * (1.0 - sigmoid_rows))
    own_cols = lax.dynamic_slice_in_dim(grad_modulation, col_start, part_width, 1)
    increments = (
        grad_ada,
        own_cols[:6].reshape(6, part_heads, head_dim),
        grad_qkv,
        grad_query_bias,
        grad_value_bias,
        grad_head_scale,
        grad_proj,
        own_cols[6].reshape(part_heads, head_dim),
        grad_up,
        grad_up_bias.reshape(part_heads, -1),
        grad_down,
        own_cols[7].reshape(part_heads, head_dim),
    )
    return (increments, grad_inputs, grad_condition)


def on_device(
    tokens,
    condition,
    scale_index,
    ada_weight,
    ada_bias,
    qkv_weight,
    query_bias,
    value_bias,
    head_scale,
    proj_weight,
    proj_bias,
    up_weight,
    up_bias,
    down_weight,
    down_bias,
    out_grad,
):

    def fetch_weights():
        return (
            lax.all_gather(ada_weight, "dp", axis=2, tiled=True),
            lax.all_gather(ada_bias, "dp", axis=2, tiled=True),
            lax.all_gather(qkv_weight, "dp", axis=1, tiled=True),
            lax.all_gather(query_bias, "dp", axis=1, tiled=True),
            lax.all_gather(value_bias, "dp", axis=1, tiled=True),
            lax.all_gather(proj_weight, "dp", axis=1, tiled=True),
            lax.all_gather(proj_bias, "dp", axis=1, tiled=True),
            lax.all_gather(up_weight, "dp", axis=0, tiled=True),
            lax.all_gather(up_bias, "dp", axis=1, tiled=True),
            lax.all_gather(down_weight, "dp", axis=1, tiled=True),
            lax.all_gather(down_bias, "dp", axis=1, tiled=True),
        )

    def forward_scan(carried, step_in):
        token_rows, condition_row, scale_row = step_in
        weights_now = fetch_weights()
        output, kept = forward_step(weights_now, token_rows, condition_row, scale_row, head_scale)
        return (carried, (output, kept))

    unused_carry, (outputs, kept_all) = lax.scan(
        forward_scan, jnp.zeros((), jnp.int32), (tokens, condition, scale_index)
    )
    width = tokens.shape[2]
    part_width = qkv_weight.shape[2]
    part_heads = head_scale.shape[0]
    head_dim = part_width // part_heads
    part_ff = up_weight.shape[1]
    zero_grads = (
        jnp.zeros((part_width, 6, width), jnp.float32),
        jnp.zeros((6, part_heads, head_dim), jnp.float32),
        jnp.zeros((3, width, part_width), jnp.float32),
        jnp.zeros((part_heads, head_dim), jnp.float32),
        jnp.zeros((part_heads, head_dim), jnp.float32),
        jnp.zeros((part_heads,), jnp.float32),
        jnp.zeros((part_width, width), jnp.float32),
        jnp.zeros((part_heads, head_dim), jnp.float32),
        jnp.zeros((width, part_ff), jnp.float32),
        jnp.zeros((part_heads, part_ff // part_heads), jnp.float32),
        jnp.zeros((part_ff, width), jnp.float32),
        jnp.zeros((part_heads, head_dim), jnp.float32),
    )

    def backward_scan(totals, step_in):
        kept, token_grad, condition_row, scale_row = step_in
        weights_now = fetch_weights()
        increments, grad_inputs, grad_condition = backward_step(
            weights_now, kept, token_grad, condition_row, scale_row, head_scale
        )
        totals = tuple((running + increment for running, increment in zip(totals, increments)))
        return (totals, (grad_inputs, grad_condition))

    totals, (grad_tokens, grad_condition) = lax.scan(
        backward_scan, zero_grads, (kept_all, out_grad, condition, scale_index), reverse=True
    )
    scale_total = lax.psum(totals[5], "dp")
    reduced = (
        lax.psum_scatter(
            totals[0].astype(jnp.bfloat16), "dp", scatter_dimension=2, tiled=True
        ).astype(jnp.float32),
        lax.psum_scatter(
            totals[1].astype(jnp.bfloat16), "dp", scatter_dimension=2, tiled=True
        ).astype(jnp.float32),
        lax.psum_scatter(
            totals[2].astype(jnp.bfloat16), "dp", scatter_dimension=1, tiled=True
        ).astype(jnp.float32),
        lax.psum_scatter(
            totals[3].astype(jnp.bfloat16), "dp", scatter_dimension=1, tiled=True
        ).astype(jnp.float32),
        lax.psum_scatter(
            totals[4].astype(jnp.bfloat16), "dp", scatter_dimension=1, tiled=True
        ).astype(jnp.float32),
        lax.psum_scatter(
            totals[6].astype(jnp.bfloat16), "dp", scatter_dimension=1, tiled=True
        ).astype(jnp.float32),
        lax.psum_scatter(
            totals[7].astype(jnp.bfloat16), "dp", scatter_dimension=1, tiled=True
        ).astype(jnp.float32),
        lax.psum_scatter(
            totals[8].astype(jnp.bfloat16), "dp", scatter_dimension=0, tiled=True
        ).astype(jnp.float32),
        lax.psum_scatter(
            totals[9].astype(jnp.bfloat16), "dp", scatter_dimension=1, tiled=True
        ).astype(jnp.float32),
        lax.psum_scatter(
            totals[10].astype(jnp.bfloat16), "dp", scatter_dimension=1, tiled=True
        ).astype(jnp.float32),
        lax.psum_scatter(
            totals[11].astype(jnp.bfloat16), "dp", scatter_dimension=1, tiled=True
        ).astype(jnp.float32),
    )
    return (
        outputs,
        grad_tokens,
        grad_condition,
        reduced[0],
        reduced[1],
        reduced[2],
        reduced[3],
        reduced[4],
        scale_total,
        reduced[5],
        reduced[6],
        reduced[7],
        reduced[8],
        reduced[9],
        reduced[10],
    )


def solution(mesh):
    in_specs = (
        P("dp", "tensor", None),
        P("dp", None),
        P("dp", None),
        P("tensor", None, "dp"),
        P(None, "tensor", "dp"),
        P(None, "dp", "tensor"),
        P("tensor", "dp"),
        P("tensor", "dp"),
        P("tensor"),
        P("tensor", "dp"),
        P("tensor", "dp"),
        P("dp", "tensor"),
        P("tensor", "dp"),
        P("tensor", "dp"),
        P("tensor", "dp"),
        P("dp", "tensor", None),
    )
    out_specs = (
        P("dp", "tensor", None),
        P("dp", "tensor", None),
        P("dp", "tensor"),
        P("tensor", None, "dp"),
        P(None, "tensor", "dp"),
        P(None, "dp", "tensor"),
        P("tensor", "dp"),
        P("tensor", "dp"),
        P("tensor"),
        P("tensor", "dp"),
        P("tensor", "dp"),
        P("dp", "tensor"),
        P("tensor", "dp"),
        P("tensor", "dp"),
        P("tensor", "dp"),
    )
    return jax.shard_map(
        on_device, mesh=mesh, in_specs=in_specs, out_specs=out_specs, check_vma=False
    )
```

profile of v0, /device:TPU:0, one launch (start us, length us, event | category | flops | bytes accessed | tf_op | source)
XLA Modules:
  0.0 2518.0 jit_solution(15394075223387883404)
XLA Ops:
  15.2 1009.9 %while.89 = (s32[]{:T(128)}, f32[2,340,1024]{2,0,1:T(2,128)}, f32[2,8,1024]{2,1,0:T(8,128)}, f32[2,340,1024]{2,1,0:T(8,128)}, f32[2,340,1]{1,2,0:T(1,128)}, /*in...) while((s32[]{:T(128)}, f32[2,340,1024]{2,0,1:T(2,128)}, ...), condition=%wide.region_12.13_spmd, body=%wide.region_0.12_spmd.sunk | while | flops 9601629184 | bytes 367439008 | solution.py:374
  16.1 43.7 %all_gather.145 = bf16[6,8,64]{1,0,2:T(8,128)(2,1)S(1)} all-gather(bf16[6,8,4]{1,0,2:T(8,128)(2,1)S(1)} %get-tuple-element.2717), channel_id=1, replica_groups=mesh['dp'=16,'tensor'=2] {'dp'}, dimensions={2}, use_global_device_ids=true | all-gather | bytes 6528 | tf_op jit(solution)/shard_map/while/body/eval_jaxpr/all_gather | solution.py:356
  60.0 35.9 %all-gather.20 = bf16[16,4,8]{2,1,0:T(4,128)(2,1)S(1)} all-gather(bf16[1,4,8]{2,1,0:T(4,128)(2,1)S(1)} %bitcast.612), channel_id=1, replica_groups=mesh['dp'=16,'tensor'=2] {'dp'}, dimensions={0}, use_global_device_ids=true | all-gather | bytes 1088 | tf_op jit(solution)/shard_map/while/body/eval_jaxpr/all_gather | solution.py:365
  96.1 37.7 %all-gather.21 = bf16[16,4,8]{2,1,0:T(4,128)(2,1)S(1)} all-gather(bf16[1,4,8]{2,1,0:T(4,128)(2,1)S(1)} %bitcast.611), channel_id=1, replica_groups=mesh['dp'=16,'tensor'=2] {'dp'}, dimensions={0}, use_global_device_ids=true | all-gather | bytes 1088 | tf_op jit(solution)/shard_map/while/body/eval_jaxpr/all_gather | solution.py:361
  182.9 37.9 %all-gather.25 = bf16[16,4,8]{2,1,0:T(4,128)(2,1)S(1)} all-gather(bf16[1,4,8]{2,1,0:T(4,128)(2,1)} %bitcast.475), channel_id=1, replica_groups=mesh['dp'=16,'tensor'=2] {'dp'}, dimensions={0}, use_global_device_ids=true | all-gather | bytes 1088 | tf_op jit(solution)/shard_map/while/body/eval_jaxpr/all_gather | solution.py:359
  305.5 38.9 %all-gather.22 = bf16[16,16,8]{1,2,0:T(8,128)(2,1)S(1)} all-gather(bf16[1,16,8]{1,2,0:T(8,128)(2,1)} %bitcast.460), channel_id=1, replica_groups=mesh['dp'=16,'tensor'=2] {'dp'}, dimensions={0}, use_global_device_ids=true | all-gather | bytes 4352 | tf_op jit(solution)/shard_map/while/body/eval_jaxpr/all_gather | solution.py:363
  400.5 69.6 %all-gather.46.cloned.1.call-done = bf16[2048,1024]{0,1:T(8,128)(2,1)} async-done(((bf16[2048,64]{0,1:T(8,128)(2,1)}), bf16[2048,1024]{0,1:T(8,128)(2,1)}) %all-gather.46.cloned.1.call-update) | async-done | bytes 4194320 | tf_op jit(solution)/shard_map/while/body/eval_jaxpr/all_gather | solution.py:364
  523.2 39.5 %all_gather.145 = bf16[6,8,64]{1,0,2:T(8,128)(2,1)S(1)} all-gather(bf16[6,8,4]{1,0,2:T(8,128)(2,1)S(1)} %get-tuple-element.2717), channel_id=1, replica_groups=mesh['dp'=16,'tensor'=2] {'dp'}, dimensions={2}, use_global_device_ids=true | all-gather | bytes 6528 | tf_op jit(solution)/shard_map/while/body/eval_jaxpr/all_gather | solution.py:356
  598.8 37.9 %all-gather.21 = bf16[16,4,8]{2,1,0:T(4,128)(2,1)S(1)} all-gather(bf16[1,4,8]{2,1,0:T(4,128)(2,1)S(1)} %bitcast.611), channel_id=1, replica_groups=mesh['dp'=16,'tensor'=2] {'dp'}, dimensions={0}, use_global_device_ids=true | all-gather | bytes 1088 | tf_op jit(solution)/shard_map/while/body/eval_jaxpr/all_gather | solution.py:361
  685.8 37.9 %all-gather.25 = bf16[16,4,8]{2,1,0:T(4,128)(2,1)S(1)} all-gather(bf16[1,4,8]{2,1,0:T(4,128)(2,1)} %bitcast.475), channel_id=1, replica_groups=mesh['dp'=16,'tensor'=2] {'dp'}, dimensions={0}, use_global_device_ids=true | all-gather | bytes 1088 | tf_op jit(solution)/shard_map/while/body/eval_jaxpr/all_gather | solution.py:359
  808.3 38.9 %all-gather.22 = bf16[16,16,8]{1,2,0:T(8,128)(2,1)S(1)} all-gather(bf16[1,16,8]{1,2,0:T(8,128)(2,1)} %bitcast.460), channel_id=1, replica_groups=mesh['dp'=16,'tensor'=2] {'dp'}, dimensions={0}, use_global_device_ids=true | all-gather | bytes 4352 | tf_op jit(solution)/shard_map/while/body/eval_jaxpr/all_gather | solution.py:363
  903.5 69.3 %all-gather.46.cloned.1.call-done = bf16[2048,1024]{0,1:T(8,128)(2,1)} async-done(((bf16[2048,64]{0,1:T(8,128)(2,1)}), bf16[2048,1024]{0,1:T(8,128)(2,1)}) %all-gather.46.cloned.1.call-update) | async-done | bytes 4194320 | tf_op jit(solution)/shard_map/while/body/eval_jaxpr/all_gather | solution.py:364
  1027.5 901.3 %while.90 = (s32[]{:T(128)}, f32[512,6,1024]{2,1,0:T(8,128)}, f32[6,8,64]{2,1,0:T(8,128)S(1)}, f32[3,1024,512]{1,2,0:T(8,128)}, f32[8,64]{1,0:T(8,128)S(1)}, /*i...) while((s32[]{:T(128)}, f32[512,6,1024]{2,1,0:T(8,128)}, ...), condition=%wide.region_36.37_spmd.clone, body=%wide.region_13.36_spmd.clone.sunk | while | flops 19610910720 | bytes 585873984 | solution.py:406
  1064.6 78.3 %all-gather.62.cloned.1.call-done = bf16[2048,1024]{0,1:T(8,128)(2,1)} async-done(((bf16[2048,64]{0,1:T(8,128)(2,1)}), bf16[2048,1024]{0,1:T(8,128)(2,1)}) %all-gather.62.cloned.1.call-update) | async-done | bytes 4194320 | tf_op jit(solution)/shard_map/while/body/eval_jaxpr/all_gather | solution.py:364
  1152.8 67.4 %all-gather.58.cloned.1.call-done = bf16[1024,2048]{1,0:T(8,128)(2,1)} async-done(((bf16[64,2048]{1,0:T(8,128)(2,1)}), bf16[1024,2048]{1,0:T(8,128)(2,1)}) %all-gather.58.cloned.1.call-update) | async-done | bytes 4194320 | tf_op jit(solution)/shard_map/while/body/eval_jaxpr/all_gather | solution.py:362
  1437.7 37.6 %all-gather.70.cloned.1.call-done = bf16[512,6,1024]{0,2,1:T(8,128)(2,1)} async-done(((bf16[512,6,64]{0,2,1:T(8,128)(2,1)}), bf16[512,6,1024]{0,2,1:T(8,128)(2,1)}) %all-gather.70.cloned.1.call-update) | async-done | bytes 6291472 | tf_op jit(solution)/shard_map/while/body/eval_jaxpr/all_gather | solution.py:355
  1499.0 78.4 %all-gather.62.cloned.1.call-done = bf16[2048,1024]{0,1:T(8,128)(2,1)} async-done(((bf16[2048,64]{0,1:T(8,128)(2,1)}), bf16[2048,1024]{0,1:T(8,128)(2,1)}) %all-gather.62.cloned.1.call-update) | async-done | bytes 4194320 | tf_op jit(solution)/shard_map/while/body/eval_jaxpr/all_gather | solution.py:364
  1587.4 67.4 %all-gather.58.cloned.1.call-done = bf16[1024,2048]{1,0:T(8,128)(2,1)} async-done(((bf16[64,2048]{1,0:T(8,128)(2,1)}), bf16[1024,2048]{1,0:T(8,128)(2,1)}) %all-gather.58.cloned.1.call-update) | async-done | bytes 4194320 | tf_op jit(solution)/shard_map/while/body/eval_jaxpr/all_gather | solution.py:362
  1964.4 39.6 %psum.29 = f32[8]{0:T(128)} all-reduce(f32[8]{0:T(128)S(1)} %get-tuple-element.1283), channel_id=1, replica_groups=mesh['dp'=16,'tensor'=2] {'dp'}, use_global_device_ids=true, to_apply=%region_42.43 | all-reduce | flops 8 | bytes 64 | tf_op jit(solution)/shard_map/psum | solution.py:409
  2005.9 74.1 %all-reduce.14 = (bf16[6,8,64]{1,2,0:T(8,128)(2,1)S(1)}, bf16[8,64]{0,1:T(8,128)(2,1)S(1)}, bf16[8,64]{0,1:T(8,128)(2,1)S(1)}, bf16[8,64]{0,1:T(8,128)(2,1)S(1)}, bf16[8,64]{0,1:T(8,128)(2,1)S(1)}) all-reduce(bf16[6,8,64]{1,2,0:T(8,128)(2,1)S(1)} %copy.162, ...), channel_id=7, replica_groups=mesh['dp'=16,'tensor'=2] {'dp'}, use_global_device_ids=true, to_apply=%region_38.39.clone | all-reduce | flops 5120 | bytes 20480
  2084.6 80.7 %reduce-scatter.20.cloned.1.call-done = bf16[3,64,512]{2,1,0:T(8,128)(2,1)} async-done(((bf16[3,1024,512]{2,1,0:T(8,128)(2,1)}), bf16[3,64,512]{2,1,0:T(8,128)(2,1)}) %reduce-scatter.20.cloned.1.call-update) | async-done | bytes 196624 | tf_op jit(solution)/shard_map/reduce_scatter | solution.py:417
  2167.1 92.8 %reduce-scatter.24.cloned.1.call-done = bf16[64,2048]{1,0:T(8,128)(2,1)} async-done(((bf16[1024,2048]{1,0:T(8,128)(2,1)}), bf16[64,2048]{1,0:T(8,128)(2,1)}) %reduce-scatter.24.cloned.1.call-update) | async-done | bytes 262160 | tf_op jit(solution)/shard_map/reduce_scatter | solution.py:432
  2261.7 95.2 %reduce-scatter.26.cloned.1.call-done = bf16[2048,64]{0,1:T(8,128)(2,1)} async-done(((bf16[2048,1024]{0,1:T(8,128)(2,1)}), bf16[2048,64]{0,1:T(8,128)(2,1)}) %reduce-scatter.26.cloned.1.call-update) | async-done | bytes 262160 | tf_op jit(solution)/shard_map/reduce_scatter | solution.py:438
  2358.6 149.8 %reduce-scatter.18.cloned.1.call-done = bf16[512,6,64]{0,2,1:T(8,128)(2,1)} async-done(((bf16[512,6,1024]{0,2,1:T(8,128)(2,1)}), bf16[512,6,64]{0,2,1:T(8,128)(2,1)}) %reduce-scatter.18.cloned.1.call-update) | async-done | bytes 393232 | tf_op jit(solution)/shard_map/reduce_scatter | solution.py:411
  (687 shorter events, 1121.3 us)
Async XLA Ops:
  15.2 119.3 %all-gather.44.cloned.1.call-start = ((), (), s32[]{:S(2)}) async-start(), calls=%async_computation.12 | async-start | bytes 6684672 | tf_op jit(solution)/shard_map/while/body/eval_jaxpr/all_gather | solution.py:355
  15.9 204.9 %all-gather.48.cloned.1.call-start = ((), (), s32[]{:S(2)}) async-start(), calls=%async_computation.14 | async-start | bytes 2113536 | tf_op jit(solution)/shard_map/while/body/eval_jaxpr/all_gather | solution.py:112
  144.5 133.8 %all-gather.52.cloned.1.call-start = ((), (), s32[]{:S(2)}) async-start(), calls=%async_computation.16 | async-start | bytes 1114112 | tf_op jit(solution)/shard_map/while/body/eval_jaxpr/all_gather | solution.py:360
  145.1 222.5 %all-gather.54.cloned.1.call-start = ((), (), s32[]{:S(2)}) async-start(), calls=%async_computation.17 | async-start | bytes 2113536 | tf_op jit(solution)/shard_map/while/body/eval_jaxpr/all_gather | solution.py:128
  304.7 165.3 %all-gather.46.cloned.1.call-start = ((), (), s32[]{:S(2)}) async-start(), calls=%async_computation.13 | async-start | bytes 4456448 | tf_op jit(solution)/shard_map/while/body/eval_jaxpr/all_gather | solution.py:364
  522.2 115.1 %all-gather.44.cloned.1.call-start = ((), (), s32[]{:S(2)}) async-start(), calls=%async_computation.12 | async-start | bytes 6684672 | tf_op jit(solution)/shard_map/while/body/eval_jaxpr/all_gather | solution.py:355
  523.0 200.7 %all-gather.48.cloned.1.call-start = ((), (), s32[]{:S(2)}) async-start(), calls=%async_computation.14 | async-start | bytes 2113536 | tf_op jit(solution)/shard_map/while/body/eval_jaxpr/all_gather | solution.py:112
  647.2 133.9 %all-gather.52.cloned.1.call-start = ((), (), s32[]{:S(2)}) async-start(), calls=%async_computation.16 | async-start | bytes 1114112 | tf_op jit(solution)/shard_map/while/body/eval_jaxpr/all_gather | solution.py:360
  648.0 222.4 %all-gather.54.cloned.1.call-start = ((), (), s32[]{:S(2)}) async-start(), calls=%async_computation.17 | async-start | bytes 2113536 | tf_op jit(solution)/shard_map/while/body/eval_jaxpr/all_gather | solution.py:128
  807.7 165.2 %all-gather.46.cloned.1.call-start = ((), (), s32[]{:S(2)}) async-start(), calls=%async_computation.13 | async-start | bytes 4456448 | tf_op jit(solution)/shard_map/while/body/eval_jaxpr/all_gather | solution.py:364
  1055.2 165.0 %all-gather.58.cloned.1.call-start = ((), (), s32[]{:S(2)}) async-start(), calls=%async_computation.19 | async-start | bytes 4456448 | tf_op jit(solution)/shard_map/while/body/eval_jaxpr/all_gather | solution.py:362
  1055.8 218.8 %all-gather.66.cloned.1.call-start = ((), (), s32[]{:S(2)}) async-start(), calls=%async_computation.23 | async-start | bytes 2113536 | tf_op jit(solution)/shard_map/while/body/eval_jaxpr/all_gather | solution.py:235
  1243.5 135.9 %all-gather.64.cloned.1.call-start = ((), (), s32[]{:S(2)}) async-start(), calls=%async_computation.22 | async-start | bytes 3342336 | tf_op jit(solution)/shard_map/while/body/eval_jaxpr/all_gather | solution.py:357
  1244.0 231.2 %all-gather.70.cloned.1.call-start = ((), (), s32[]{:S(2)}) async-start(), calls=%async_computation.25 | async-start | bytes 6684672 | tf_op jit(solution)/shard_map/while/body/eval_jaxpr/all_gather | solution.py:355
  1490.0 164.8 %all-gather.58.cloned.1.call-start = ((), (), s32[]{:S(2)}) async-start(), calls=%async_computation.19 | async-start | bytes 4456448 | tf_op jit(solution)/shard_map/while/body/eval_jaxpr/all_gather | solution.py:362
  1490.6 221.0 %all-gather.66.cloned.1.call-start = ((), (), s32[]{:S(2)}) async-start(), calls=%async_computation.23 | async-start | bytes 2113536 | tf_op jit(solution)/shard_map/while/body/eval_jaxpr/all_gather | solution.py:235
  1678.0 135.9 %all-gather.64.cloned.1.call-start = ((), (), s32[]{:S(2)}) async-start(), calls=%async_computation.22 | async-start | bytes 3342336 | tf_op jit(solution)/shard_map/while/body/eval_jaxpr/all_gather | solution.py:357
  1678.5 231.3 %all-gather.70.cloned.1.call-start = ((), (), s32[]{:S(2)}) async-start(), calls=%async_computation.25 | async-start | bytes 6684672 | tf_op jit(solution)/shard_map/while/body/eval_jaxpr/all_gather | solution.py:355
  1928.8 153.0 %reduce-scatter.28.cloned.1.call-start = ((), (), s32[]{:S(2)}) async-start(), calls=%async_computation.11 | async-start | bytes 69632
  1929.6 153.6 %reduce-scatter.22.cloned.1.call-start = ((), (), s32[]{:S(2)}) async-start(), calls=%async_computation.8 | async-start | bytes 1114112 | tf_op jit(solution)/shard_map/reduce_scatter | solution.py:426
  1932.2 233.2 %reduce-scatter.20.cloned.1.call-start = ((), (), s32[]{:S(2)}) async-start(), calls=%async_computation.7 | async-start | bytes 3342336 | tf_op jit(solution)/shard_map/reduce_scatter | solution.py:417
  1937.7 322.2 %reduce-scatter.24.cloned.1.call-start = ((), (), s32[]{:S(2)}) async-start(), calls=%async_computation.9 | async-start | bytes 4456448 | tf_op jit(solution)/shard_map/reduce_scatter | solution.py:432
  1943.8 413.0 %reduce-scatter.26.cloned.1.call-start = ((), (), s32[]{:S(2)}) async-start(), calls=%async_computation.10 | async-start | bytes 4456448 | tf_op jit(solution)/shard_map/reduce_scatter | solution.py:438
  1951.3 557.1 %reduce-scatter.18.cloned.1.call-start = ((), (), s32[]{:S(2)}) async-start(), calls=%async_computation.6 | async-start | bytes 6684672 | tf_op jit(solution)/shard_map/reduce_scatter | solution.py:411
  (119 other events, 2002.5 us)
Sparse Core Ops, SparseCore 0:
  18.8 97.2 all-gather.43
  152.4 68.8 all-gather.49
  223.9 54.3 all-gather.51
  304.3 8.3 all-gather.53
  315.3 77.2 all-gather.55
  395.3 74.6 all-gather.45
  525.9 93.1 all-gather.43
  655.1 68.8 all-gather.49
  726.7 54.3 all-gather.51
  807.1 8.3 all-gather.53
  818.2 77.2 all-gather.55
  898.2 74.6 all-gather.45
  1054.7 8.1 all-gather.59
  1065.5 77.2 all-gather.61
  1145.4 74.6 all-gather.57
  1253.8 56.4 all-gather.67
  1312.9 66.4 all-gather.63
  1382.2 93.0 all-gather.69
  1500.2 77.2 all-gather.61
  1580.1 74.6 all-gather.57
  1677.5 8.1 all-gather.65
  1688.3 56.4 all-gather.67
  1747.4 66.4 all-gather.63
  1816.6 93.1 all-gather.69
  (4 shorter events, 27.2 us)
Sparse Core Ops, SparseCore 1:
  1932.0 74.2 reduce-scatter.27
  2008.5 74.3 reduce-scatter.21
  2085.0 80.3 reduce-scatter.19
  2167.7 92.2 reduce-scatter.23
  2262.2 94.6 reduce-scatter.25
  2362.1 146.3 reduce-scatter.17
where the time goes:
time: 2550 us; the launch traced here: 2520 us
  waiting for transfers between devices  1120 us (44%)
  blocking collectives  621 us (24%)
  matrix products  288 us (11%)
  local copies, waits for them, and re-layouts  265 us (10%)
  other arithmetic  153 us (6%)
  loops' own time  31.4 us (1%)
    all_gather x4, waiting for transfers between devices, fetch_weights(): lax.all_gather(down_weight, 'dp', axis=1, tiled=True)  296 us
    all_gather x4, waiting for transfers between devices, fetch_weights(): lax.all_gather(up_weight, 'dp', axis=0, tiled=True)  182 us
    reduce_scatter x1, waiting for transfers between devices, on_device(): lax.psum_scatter(totals[0].astype(jnp.bfloat16), 'dp', scatter_dimension=...  150 us
    dynamic_update_slice x22, local copies, waits for them, and re-layouts, on_device(): lax.scan(forward_scan, jnp.zeros((), jnp.int32), (tokens, condition, scal...  125 us
    all_gather x4, waiting for transfers between devices, fetch_weights(): lax.all_gather(proj_weight, 'dp', axis=1, tiled=True)  100 us
    reduce_scatter x1, waiting for transfers between devices, on_device(): lax.psum_scatter(totals[10].astype(jnp.bfloat16), 'dp', scatter_dimension...  95.2 us
    reduce_scatter x1, waiting for transfers between devices, on_device(): lax.psum_scatter(totals[8].astype(jnp.bfloat16), 'dp', scatter_dimension=...  92.8 us
    all_gather x2, blocking collectives, fetch_weights(): lax.all_gather(ada_bias, 'dp', axis=2, tiled=True)  83.2 us
  transfers between devices with their start and end apart: 42, of which 22 were waited for; matrix products, arithmetic and copies ran while one was open for 20% of the time, Pallas kernels for 0%

commit v1 on v0

--- a/solution.py
+++ b/solution.py
@@ -1,6 +1,10 @@
+import functools
+
 import jax
 import jax.numpy as jnp
 from jax import lax
+from jax.experimental import pallas as pl
+from jax.experimental.pallas import tpu as pltpu
 from jax.sharding import PartitionSpec as P
 
 NORM_EPS = 1e-06
@@ -461,6 +465,595 @@
     )
 
 
+GRIDS = {(16, 2): (4, 2, 2)}
+MESH_ID = pl.DeviceIdType.MESH
+ANY = pl.ANY
+F32 = jnp.float32
+BF16 = jnp.bfloat16
+
+
+def place():
+    return (lax.axis_index("dp"), lax.axis_index("tensor"))
+
+
+def coords(grid):
+    chip, core = place()
+    nz, ny, nx = grid
+    return (chip // (ny * nx), (chip // nx) % ny, chip % nx, core)
+
+
+def greet_all(count):
+    chip, core = place()
+    me = chip * 2 + core
+    barrier = pltpu.get_barrier_semaphore()
+    for k in range(1, count):
+        peer = (me + k) % count
+        pl.semaphore_signal(barrier, inc=1, device_id=(peer // 2, peer % 2), device_id_type=MESH_ID)
+    pl.semaphore_wait(barrier, count - 1)
+
+
+def remote(src, dst, send_sem, recv_sem, device):
+    return pltpu.make_async_remote_copy(
+        src_ref=src,
+        dst_ref=dst,
+        send_sem=send_sem,
+        recv_sem=recv_sem,
+        device_id=device,
+        device_id_type=MESH_ID,
+    )
+
+
+def swap_kernel(count, to_all, src_ref, dst_ref, local_sem, send_sem, recv_sem):
+    chip, core = place()
+    me = chip * 2 + core
+    greet_all(count)
+    own = pltpu.make_async_copy(src_ref if to_all else src_ref.at[me], dst_ref.at[me], local_sem)
+    own.start()
+    copies = []
+    for k in range(1, count):
+        peer = (me + k) % count
+        copy = remote(
+            src_ref if to_all else src_ref.at[peer],
+            dst_ref.at[me],
+            send_sem.at[k - 1],
+            recv_sem.at[k - 1],
+            (peer // 2, peer % 2),
+        )
+        copy.start()
+        copies.append(copy)
+    own.wait()
+    for copy in copies:
+        copy.wait()
+
+
+def swap(values, count, to_all, collective_id, name):
+    block = values.shape if to_all else values.shape[1:]
+    return pl.pallas_call(
+        functools.partial(swap_kernel, count, to_all),
+        out_shape=jax.ShapeDtypeStruct((count,) + block, values.dtype),
+        in_specs=[pl.BlockSpec(memory_space=pltpu.VMEM)],
+        out_specs=pl.BlockSpec(memory_space=pltpu.VMEM),
+        scratch_shapes=[
+            pltpu.SemaphoreType.DMA,
+            pltpu.SemaphoreType.DMA((count - 1,)),
+            pltpu.SemaphoreType.DMA((count - 1,)),
+        ],
+        compiler_params=pltpu.CompilerParams(collective_id=collective_id, has_side_effects=True),
+        name=name,
+    )(values)
+
+
+def gather_kernel(
+    grid, chunks, shard_ref, tok_ref, grad_ref, full_ref, tok_out, grad_out, local_sem, z_send, z_recv, p_send, p_recv, t_send, t_recv
+):
+    nz, ny, nx = grid
+    half = nz // 2
+    z, y, x, core = coords(grid)
+
+    def dev(z_at, y_at, x_at):
+        return ((z_at * ny + y_at) * nx + x_at, core)
+
+    x_peer = dev(z, y, 1 - x)
+    y_peer = dev(z, 1 - y, x)
+    sibling = (place()[0], 1 - core)
+    greet_all(nz * ny * nx * 2)
+    swaps = []
+    for i, (src, dst) in enumerate(((tok_ref, tok_out), (grad_ref, grad_out))):
+        own = pltpu.make_async_copy(src, dst.at[core], local_sem.at[chunks + i])
+        own.start()
+        copy = remote(src, dst.at[core], t_send.at[i], t_recv.at[i], sibling)
+        copy.start()
+        swaps += [own, copy]
+
+    def own_copy(c):
+        return pltpu.make_async_copy(shard_ref.at[c], full_ref.at[c, z, y, x], local_sem.at[c])
+
+    def z_copies(c):
+        return [
+            remote(
+                shard_ref.at[c],
+                full_ref.at[c, z, y, x],
+                z_send.at[c, k - 1],
+                z_recv.at[c, k - 1],
+                dev((z + k) % nz, y, x),
+            )
+            for k in range(1, nz)
+        ]
+
+    def first_copies(c):
+        low = full_ref.at[c, pl.ds(0, half), y, x]
+        high = full_ref.at[c, pl.ds(half, half), y, x]
+        return [
+            remote(low, low, p_send.at[c, 0], p_recv.at[c, 0], x_peer),
+            remote(high, high, p_send.at[c, 1], p_recv.at[c, 1], y_peer),
+        ]
+
+    def second_copies(c):
+        low = full_ref.at[c, pl.ds(0, half), y]
+        high = full_ref.at[c, pl.ds(half, half), :, x]
+        return [
+            remote(low, low, p_send.at[c, 2], p_recv.at[c, 2], y_peer),
+            remote(high, high, p_send.at[c, 3], p_recv.at[c, 3], x_peer),
+        ]
+
+    ahead = 2
+    for t in range(-ahead, chunks + 2):
+        if 0 <= t + ahead < chunks:
+            c = t + ahead
+            own_copy(c).start()
+            for copy in z_copies(c):
+                copy.start()
+        if 0 <= t < chunks:
+            own_copy(t).wait()
+            for copy in z_copies(t):
+                copy.wait_recv()
+            for copy in first_copies(t):
+                copy.start()
+        if 0 <= t - 1 < chunks:
+            for copy in first_copies(t - 1):
+                copy.wait_recv()
+            for copy in second_copies(t - 1):
+                copy.start()
+        if 0 <= t - 2 < chunks:
+            for copy in second_copies(t - 2):
+                copy.wait_recv()
+    for c in range(chunks):
+        for copy in z_copies(c) + first_copies(c) + second_copies(c):
+            copy.wait_send()
+    for copy in swaps:
+        copy.wait()
+
+
+def gather_weights(grid, shard, tok, grad, collective_id):
+    nz, ny, nx = grid
+    chunks = shard.shape[0]
+    return pl.pallas_call(
+        functools.partial(gather_kernel, grid, chunks),
+        out_shape=[
+            jax.ShapeDtypeStruct((chunks, nz, ny, nx) + shard.shape[1:], shard.dtype),
+            jax.ShapeDtypeStruct((2,) + tok.shape, tok.dtype),
+            jax.ShapeDtypeStruct((2,) + grad.shape, grad.dtype),
+        ],
+        in_specs=[pl.BlockSpec(memory_space=ANY)] * 3,
+        out_specs=[pl.BlockSpec(memory_space=ANY)] * 3,
+        scratch_shapes=[
+            pltpu.SemaphoreType.DMA((chunks + 2,)),
+            pltpu.SemaphoreType.DMA((chunks, nz - 1)),
+            pltpu.SemaphoreType.DMA((chunks, nz - 1)),
+            pltpu.SemaphoreType.DMA((chunks, 4)),
+            pltpu.SemaphoreType.DMA((chunks, 4)),
+            pltpu.SemaphoreType.DMA((2,)),
+            pltpu.SemaphoreType.DMA((2,)),
+        ],
+        compiler_params=pltpu.CompilerParams(collective_id=collective_id, has_side_effects=True),
+        name="gather_weights",
+    )(shard, tok, grad)
+
+
+def reduce_kernel(
+    grid,
+    chunks,
+    full_ref,
+    out_ref,
+    keep_low,
+    keep_high,
+    got_low,
+    got_high,
+    next_low,
+    next_high,
+    column,
+    got_z,
+    local_sem,
+    p_send,
+    p_recv,
+    z_send,
+    z_recv,
+):
+    nz, ny, nx = grid
+    half = nz // 2
+    z, y, x, core = coords(grid)
+
+    def dev(z_at, y_at, x_at):
+        return ((z_at * ny + y_at) * nx + x_at, core)
+
+    x_peer = dev(z, y, 1 - x)
+    y_peer = dev(z, 1 - y, x)
+    greet_all(nz * ny * nx * 2)
+
+    def own_copies(c):
+        return [
+            pltpu.make_async_copy(full_ref.at[c, pl.ds(0, half), y], keep_low.at[c], local_sem.at[c, 0]),
+            pltpu.make_async_copy(
+                full_ref.at[c, pl.ds(half, half), :, x], keep_high.at[c], local_sem.at[c, 1]
+            ),
+        ]
+
+    def first_copies(c):
+        return [
+            remote(
+                full_ref.at[c, pl.ds(0, half), 1 - y], got_low.at[c], p_send.at[c, 0], p_recv.at[c, 0], y_peer
+            ),
+            remote(
+                full_ref.at[c, pl.ds(half, half), :, 1 - x],
+                got_high.at[c],
+                p_send.at[c, 1],
+                p_recv.at[c, 1],
+                x_peer,
+            ),
+        ]
+
+    def second_copies(c):
+        return [
+            remote(keep_low.at[c, :, 1 - x], next_low.at[c], p_send.at[c, 2], p_recv.at[c, 2], x_peer),
+            remote(keep_high.at[c, :, 1 - y], next_high.at[c], p_send.at[c, 3], p_recv.at[c, 3], y_peer),
+        ]
+
+    def z_copies(c):
+        return [
+            remote(
+                column.at[c, (z + k) % nz],
+                got_z.at[c, k - 1],
+                z_send.at[c, k - 1],
+                z_recv.at[c, k - 1],
+                dev((z + k) % nz, y, x),
+            )
+            for k in range(1, nz)
+        ]
+
+    def add(a, b):
+        return (a.astype(F32) + b.astype(F32)).astype(BF16)
+
+    ahead = 2
+    for t in range(-ahead, chunks + 2):
+        if 0 <= t + ahead < chunks:
+            c = t + ahead
+            for copy in first_copies(c) + own_copies(c):
+                copy.start()
+        if 0 <= t < chunks:
+            for copy in own_copies(t):
+                copy.wait()
+            for copy in first_copies(t):
+                copy.wait_recv()
+            keep_low[t] = add(keep_low[t], got_low[t])
+            keep_high[t] = add(keep_high[t], got_high[t])
+            for copy in second_copies(t):
+                copy.start()
+        if 0 <= t - 1 < chunks:
+            c = t - 1
+            for copy in second_copies(c):
+                copy.wait_recv()
+            column[c, 0:half] = add(keep_low[c, :, x], next_low[c])
+            column[c, half:nz] = add(keep_high[c, :, y], next_high[c])
+            for copy in z_copies(c):
+                copy.start()
+        if 0 <= t - 2 < chunks:
+            c = t - 2
+            for copy in z_copies(c):
+                copy.wait_recv()
+            total = column[c, z].astype(F32)
+            for k in range(nz - 1):
+                total = total + got_z[c, k].astype(F32)
+            out_ref[c] = total
+    for c in range(chunks):
+        for copy in first_copies(c) + second_copies(c) + z_copies(c):
+            copy.wait_send()
+
+
+def reduce_weights(grid, full, collective_id):
+    nz, ny, nx = grid
+    half = nz // 2
+    chunks = full.shape[0]
+    block = full.shape[4:]
+    return pl.pallas_call(
+        functools.partial(reduce_kernel, grid, chunks),
+        out_shape=jax.ShapeDtypeStruct((chunks,) + block, F32),
+        in_specs=[pl.BlockSpec(memory_space=ANY)],
+        out_specs=pl.BlockSpec(memory_space=pltpu.VMEM),
+        scratch_shapes=[
+            pltpu.VMEM((chunks, half, nx) + block, BF16),
+            pltpu.VMEM((chunks, half, ny) + block, BF16),
+            pltpu.VMEM((chunks, half, nx) + block, BF16),
+            pltpu.VMEM((chunks, half, ny) + block, BF16),
+            pltpu.VMEM((chunks, half) + block, BF16),
+            pltpu.VMEM((chunks, half) + block, BF16),
+            pltpu.VMEM((chunks, nz) + block, BF16),
+            pltpu.VMEM((chunks, nz - 1) + block, BF16),
+            pltpu.SemaphoreType.DMA((chunks, 2)),
+            pltpu.SemaphoreType.DMA((chunks, 4)),
+            pltpu.SemaphoreType.DMA((chunks, 4)),
+            pltpu.SemaphoreType.DMA((chunks, nz - 1)),
+            pltpu.SemaphoreType.DMA((chunks, nz - 1)),
+        ],
+        compiler_params=pltpu.CompilerParams(
+            collective_id=collective_id, has_side_effects=True, vmem_limit_bytes=48 * 2**20
+        ),
+        name="reduce_weights",
+    )(full)
+
+
+def sibling_swap(values):
+    return lax.ppermute(values, "tensor", [(0, 1), (1, 0)])
+
+
+def pad_rows(values, rows):
+    count, length = values.shape
+    return jnp.pad(values, ((0, 0), (0, rows * 128 - length))).reshape(count, rows, 128)
+
+
+def fast_device(
+    grid,
+    tokens,
+    condition,
+    scale_index,
+    ada_weight,
+    ada_bias,
+    qkv_weight,
+    query_bias,
+    value_bias,
+    head_scale,
+    proj_weight,
+    proj_bias,
+    up_weight,
+    up_bias,
+    down_weight,
+    down_bias,
+    out_grad,
+):
+    nz, ny, nx = grid
+    dp = nz * ny * nx
+    count = dp * 2
+    seqs, own_len, width = tokens.shape
+    seq_len = own_len * 2
+    part = qkv_weight.shape[2]
+    heads = head_scale.shape[0]
+    head_dim = part // heads
+    own_rows = qkv_weight.shape[1]
+    ff_chunks = up_weight.shape[1] // part
+    chip, core = place()
+
+    shard = jnp.concatenate(
+        [
+            qkv_weight,
+            proj_weight.T[None],
+            up_weight.reshape(own_rows, ff_chunks, part).transpose(1, 0, 2),
+            down_weight.T.reshape(own_rows, ff_chunks, part).transpose(1, 0, 2),
+        ],
+        axis=0,
+    )
+    full, tok_all, grad_all = gather_weights(
+        grid, shard, tokens.transpose(1, 0, 2), out_grad.transpose(1, 0, 2), 0
+    )
+    full = full.reshape(-1, width, part)
+    inputs = tok_all.reshape(seq_len, seqs, width).transpose(1, 0, 2).astype(F32)
+    grad_rows = grad_all.reshape(seq_len, seqs, width).transpose(1, 0, 2).astype(F32)
+
+    pieces = [condition, ada_bias, query_bias, value_bias, proj_bias, up_bias, down_bias]
+    small = jnp.concatenate([piece.reshape(1, -1) for piece in pieces], axis=1)
+    small_rows = -(-small.shape[1] // (16 * 128)) * 16
+    every = swap(pad_rows(small, small_rows)[0], count, True, 1, "gather_small")
+    every = every.reshape(dp, 2, small_rows * 128)
+    parts, at = [], 0
+    for piece in pieces:
+        parts.append(every[:, :, at : at + piece.size].reshape((dp, 2) + piece.shape).astype(F32))
+        at += piece.size
+    cond_all = parts[0][:, 0].reshape(dp * seqs, width)
+    own_of = lambda values: lax.dynamic_index_in_dim(values, core, 1, keepdims=False)
+    spread = lambda values: values.transpose(1, 0, 2).reshape(-1)
+    both = lambda values: values.transpose(1, 2, 0, 3).reshape(-1)
+    ada_bias_full = parts[1].transpose(2, 1, 3, 0, 4).reshape(6, width)
+    query_bias_own = spread(own_of(parts[2]))
+    value_bias_own = spread(own_of(parts[3]))
+    proj_bias_full = both(parts[4])
+    up_bias_own = spread(own_of(parts[5]))
+    down_bias_full = both(parts[6])
+
+    cond_half = lax.dynamic_slice_in_dim(cond_all, core * part, part, 1)
+    silu_half = jax.nn.silu(cond_half).astype(BF16)
+    mod_part = jnp.einsum("sr,rjc->sjc", silu_half, ada_weight, preferred_element_type=F32)
+    cols = mod_part.shape[2]
+    mod_send = jnp.repeat(pad_rows(mod_part.reshape(dp, seqs * 6 * cols), 8), 2, axis=0)
+    mod_got = swap(mod_send, count, False, 2, "swap_modulation")
+    mod_got = mod_got.reshape(dp, 2, -1)[:, :, : seqs * 6 * cols].sum(axis=1)
+    modulation = mod_got.reshape(dp, seqs, 6, cols).transpose(1, 2, 0, 3).reshape(seqs, 6, width)
+    modulation = modulation + ada_bias_full
+    mod = [modulation[:, j][:, None, :] for j in range(6)]
+
+    normed_attn, inverse_attn = normalize(inputs)
+    mixed_attn = (normed_attn * (1.0 + mod[2]) + mod[4]).astype(BF16)
+    projected = jnp.einsum("sld,jdc->jslc", mixed_attn, full[:3], preferred_element_type=F32)
+    split = lambda values: values.reshape(seqs, seq_len, heads, head_dim)
+    queries = split(projected[0] + query_bias_own)
+    keys_raw = split(projected[1])
+    values_low = split((projected[2] + value_bias_own).astype(BF16))
+    query_inverse = lax.rsqrt(jnp.sum(queries * queries, axis=-1, keepdims=True) + HEAD_EPS)
+    key_inverse = lax.rsqrt(jnp.sum(keys_raw * keys_raw, axis=-1, keepdims=True) + HEAD_EPS)
+    query_unit = queries * query_inverse
+    key_unit = keys_raw * key_inverse
+    scale_factor = jnp.exp(head_scale)[:, None]
+    query_low = (query_unit * scale_factor).astype(BF16)
+    key_low = key_unit.astype(BF16)
+    scores = jnp.einsum("sqhe,skhe->shqk", query_low, key_low, preferred_element_type=F32)
+    allowed = (scale_index[:, None, :] <= scale_index[:, :, None])[:, None]
+    scores = jnp.where(allowed, scores, -1e30)
+    row_max = jnp.max(scores, axis=-1, keepdims=True)
+    weights_exp = jnp.exp(scores - row_max)
+    attn_prob = weights_exp / jnp.sum(weights_exp, axis=-1, keepdims=True)
+    prob_low = attn_prob.astype(BF16)
+    attended = jnp.einsum("shqk,skhe->sqhe", prob_low, values_low, preferred_element_type=F32)
+    attended = attended.reshape(seqs, seq_len, part).astype(BF16)
+    branch_part = jnp.einsum("slc,dc->sld", attended, full[3], preferred_element_type=F32).astype(BF16)
+    branch_attn = branch_part.astype(F32) + sibling_swap(branch_part).astype(F32) + proj_bias_full
+    middle = inputs + mod[0] * branch_attn
+    normed_mlp, inverse_mlp = normalize(middle)
+    mixed_mlp = (normed_mlp * (1.0 + mod[3]) + mod[5]).astype(BF16)
+    up = full[4 : 4 + ff_chunks]
+    down = full[4 + ff_chunks :]
+    hidden = jnp.einsum("sld,jdf->jslf", mixed_mlp, up, preferred_element_type=F32)
+    hidden = hidden + up_bias_own.reshape(ff_chunks, 1, 1, part)
+    activated = jax.nn.gelu(hidden, approximate=True).astype(BF16)
+    mlp_part = jnp.einsum("jslf,jdf->sld", activated, down, preferred_element_type=F32).astype(BF16)
+    branch_mlp = mlp_part.astype(F32) + sibling_swap(mlp_part).astype(F32) + down_bias_full
+    output = middle + mod[1] * branch_mlp
+
+    grad_gamma_mlp = jnp.sum(grad_rows * branch_mlp, axis=1)
+    grad_branch_mlp = grad_rows * mod[1]
+    grad_down_bias = jnp.sum(grad_branch_mlp, axis=(0, 1))
+    dm_low = grad_branch_mlp.astype(BF16)
+    grad_down = jnp.einsum("sld,jslf->jdf", dm_low, activated, preferred_element_type=F32).astype(BF16)
+    grad_act = jnp.einsum("sld,jdf->jslf", dm_low, down, preferred_element_type=F32)
+    grad_hidden = grad_act * gelu_slope(hidden)
+    grad_up_bias = jnp.sum(grad_hidden, axis=(1, 2)).reshape(-1)
+    hidden_low = grad_hidden.astype(BF16)
+    grad_up = jnp.einsum("sld,jslf->jdf", mixed_mlp, hidden_low, preferred_element_type=F32).astype(BF16)
+    gm_part = jnp.einsum("jslf,jdf->sld", hidden_low, up, preferred_element_type=F32).astype(BF16)
+    grad_mixed_mlp = gm_part.astype(F32) + sibling_swap(gm_part).astype(F32)
+    grad_scale_mlp = jnp.sum(grad_mixed_mlp * normed_mlp, axis=1)
+    grad_shift_mlp = jnp.sum(grad_mixed_mlp, axis=1)
+    grad_middle = grad_rows + norm_back(grad_mixed_mlp * (1.0 + mod[3]), normed_mlp, inverse_mlp)
+    grad_gamma_attn = jnp.sum(grad_middle * branch_attn, axis=1)
+    grad_branch_attn = grad_middle * mod[0]
+    grad_proj_bias = jnp.sum(grad_branch_attn, axis=(0, 1))
+    da_low = grad_branch_attn.astype(BF16)
+    grad_proj = jnp.einsum("sld,slc->dc", da_low, attended, preferred_element_type=F32).astype(BF16)
+    grad_attended = split(
+        jnp.einsum("sld,dc->slc", da_low, full[3], preferred_element_type=F32).astype(BF16)
+    )
+    grad_prob = jnp.einsum("sqhe,skhe->shqk", grad_attended, values_low, preferred_element_type=F32)
+    row_dot = jnp.sum(attn_prob * grad_prob, axis=-1, keepdims=True)
+    grad_scores = (attn_prob * (grad_prob - row_dot)).astype(BF16)
+    grad_values = jnp.einsum("shqk,sqhe->skhe", prob_low, grad_attended, preferred_element_type=F32)
+    grad_query_scaled = jnp.einsum("shqk,skhe->sqhe", grad_scores, key_low, preferred_element_type=F32)
+    grad_key_unit = jnp.einsum("shqk,sqhe->skhe", grad_scores, query_low, preferred_element_type=F32)
+    grad_head_scale = jnp.sum(grad_query_scaled * query_unit, axis=(0, 1, 3)) * jnp.exp(head_scale)
+    grad_query_unit = grad_query_scaled * scale_factor
+    grad_queries = query_inverse * (
+        grad_query_unit - query_unit * jnp.sum(grad_query_unit * query_unit, axis=-1, keepdims=True)
+    )
+    grad_keys = key_inverse * (
+        grad_key_unit - key_unit * jnp.sum(grad_key_unit * key_unit, axis=-1, keepdims=True)
+    )
+    grad_query_bias = jnp.sum(grad_queries, axis=(0, 1)).reshape(-1)
+    grad_value_bias = jnp.sum(grad_values, axis=(0, 1)).reshape(-1)
+    qkv_low = jnp.stack([grad_queries, grad_keys, grad_values]).reshape(3, seqs, seq_len, part)
+    qkv_low = qkv_low.astype(BF16)
+    grad_qkv = jnp.einsum("sld,jslc->jdc", mixed_attn, qkv_low, preferred_element_type=F32).astype(BF16)
+    ga_part = jnp.einsum("jslc,jdc->sld", qkv_low, full[:3], preferred_element_type=F32).astype(BF16)
+    grad_mixed_attn = ga_part.astype(F32) + sibling_swap(ga_part).astype(F32)
+    grad_scale_attn = jnp.sum(grad_mixed_attn * normed_attn, axis=1)
+    grad_shift_attn = jnp.sum(grad_mixed_attn, axis=1)
+    grad_inputs = grad_middle + norm_back(
+        grad_mixed_attn * (1.0 + mod[2]), normed_attn, inverse_attn
+    )
+
+    grad_mod = jnp.stack(
+        [
+            grad_gamma_attn,
+            grad_gamma_mlp,
+            grad_scale_attn,
+            grad_scale_mlp,
+            grad_shift_attn,
+            grad_shift_mlp,
+        ],
+        axis=1,
+    )
+    twice = lambda values: jnp.repeat(values[:, None], 2, axis=1)
+    to_owner = lambda values: values.reshape(heads, dp, -1).transpose(1, 0, 2).reshape(dp, -1)
+    to_both = lambda values: (
+        values.reshape(2, heads, dp, -1).transpose(2, 0, 1, 3).reshape(dp, 2, -1)
+    )
+    send = jnp.concatenate(
+        [
+            twice(grad_mod.reshape(seqs, 6, dp, cols).transpose(2, 0, 1, 3).reshape(dp, -1)),
+            twice(to_owner(grad_query_bias)),
+            twice(to_owner(grad_value_bias)),
+            twice(to_owner(grad_up_bias)),
+            to_both(grad_proj_bias),
+            to_both(grad_down_bias),
+            jnp.broadcast_to(grad_head_scale, (dp, 2, heads)),
+        ],
+        axis=2,
+    )
+    rows = -(-send.shape[2] // (8 * 128)) * 8
+    got = swap(pad_rows(send.reshape(count, -1), rows), count, False, 3, "swap_grads")
+    got = own_of(got.reshape(dp, 2, -1))
+    n_mod = seqs * 6 * cols
+    mod_low = got[:, :n_mod].reshape(dp * seqs, 6, cols)
+    grad_ada_bias_cols = jnp.sum(mod_low, axis=0)
+    mod_low = mod_low.astype(BF16)
+    sums = jnp.sum(got[:, n_mod:], axis=0)
+    owned, at = [], 0
+    for shape in (query_bias.shape, value_bias.shape, up_bias.shape, proj_bias.shape, down_bias.shape):
+        size = shape[0] * shape[1]
+        owned.append(sums[at : at + size].reshape(shape))
+        at += size
+    scale_total = sums[at : at + heads]
+    grad_ada = jnp.einsum("sr,sjc->rjc", silu_half, mod_low, preferred_element_type=F32)
+    cond_part = jnp.einsum("sjc,rjc->sr", mod_low, ada_weight, preferred_element_type=F32)
+    return_send = jnp.repeat(cond_part.reshape(dp, seqs * part // 128, 128), 2, axis=0)
+    ada_bias_send = jnp.broadcast_to(
+        jnp.pad(grad_ada_bias_cols.reshape(1, -1), ((0, 0), (0, 1024 - 6 * cols))).reshape(1, 8, 128),
+        (count, 8, 128),
+    )
+    last = swap(
+        jnp.concatenate([return_send, ada_bias_send], axis=1), count, False, 4, "swap_condition"
+    )
+    last = own_of(last.reshape(dp, 2, -1))
+    grad_silu = jnp.sum(last[:, : seqs * part], axis=0).reshape(seqs, part)
+    cond_own = lax.dynamic_slice_in_dim(condition.astype(F32), core * part, part, 1)
+    sigmoid = jax.nn.sigmoid(cond_own)
+    grad_condition = grad_silu * sigmoid * (1.0 + cond_own * (1.0 - sigmoid))
+    ada_cols = last[:, seqs * part : seqs * part + 6 * cols].reshape(dp, 6, cols)
+    ada_rows = lax.dynamic_slice_in_dim(ada_cols, core * heads, heads, 0).transpose(1, 0, 2)
+    grad_ada_bias = lax.dynamic_slice_in_dim(ada_rows, chip * ada_bias.shape[2], ada_bias.shape[2], 2)
+
+    reduced = reduce_weights(
+        grid,
+        jnp.concatenate([grad_qkv, grad_proj[None], grad_up, grad_down], axis=0).reshape(
+            (-1,) + grid + (own_rows, part)
+        ),
+        5,
+    )
+    wide = lambda values: values.transpose(1, 0, 2).reshape(own_rows, -1)
+    own_half = lambda values: lax.dynamic_slice_in_dim(values, core * own_len, own_len, 1)
+    return (
+        own_half(output),
+        own_half(grad_inputs),
+        grad_condition,
+        grad_ada,
+        grad_ada_bias,
+        reduced[:3],
+        owned[0],
+        owned[1],
+        scale_total,
+        reduced[3].T,
+        owned[3],
+        wide(reduced[4 : 4 + ff_chunks]),
+        owned[2],
+        wide(reduced[4 + ff_chunks :]).T,
+        owned[4],
+    )
+
+
 def solution(mesh):
     in_specs = (
         P("dp", "tensor", None),
@@ -497,6 +1090,8 @@
         P("tensor", "dp"),
         P("tensor", "dp"),
     )
+    grid = GRIDS.get((mesh.shape["dp"], mesh.shape["tensor"]))
+    body = on_device if grid is None else functools.partial(fast_device, grid)
     return jax.shard_map(
-        on_device, mesh=mesh, in_specs=in_specs, out_specs=out_specs, check_vma=False
-    )
+        body, mesh=mesh, in_specs=in_specs, out_specs=out_specs, check_vma=False
+    )

time: 2550 us -> 848 us (0.33); the launches traced: 2520 us -> 842 us
  waiting for transfers between devices: 1120 us -> 0.01 us
  blocking collectives: 621 us -> 0 us
  Pallas kernels: 0 us -> 368 us
  local copies, waits for them, and re-layouts: 265 us -> 134 us
  matrix products: 288 us -> 221 us
  other arithmetic: 153 us -> 116 us
  loops' own time: 31.4 us -> 0 us
    all_gather x28 -> x0, waiting for transfers between devices: 693 us -> none  [the longest x4 296 us: fetch_weights(): lax.all_gather(down_weight, 'dp', axis=1, tiled=True)]
    all_gather x12 -> x0, blocking collectives: 456 us -> none  [the longest x2 83.2 us: fetch_weights(): lax.all_gather(ada_bias, 'dp', axis=2, tiled=True)]
    reduce_scatter x5 -> x0, waiting for transfers between devices: 418 us -> none  [the longest x1 150 us: on_device(): lax.psum_scatter(totals[0].astype(jnp.bfloat16), 'dp', scatter_dimension=...]
    pallas_call x0 -> x6, Pallas kernels: none -> 368 us  [the longest x1 199 us: gather_weights(): pl.pallas_call(functools.partial(gather_kernel, grid, chunks), out_shape=...]
    dynamic_update_slice x24 -> x0, local copies, waits for them, and re-layouts: 125 us -> none  [the longest x22 125 us: on_device(): lax.scan(forward_scan, jnp.zeros((), jnp.int32), (tokens, condition, scal...]
    dot_general x42 -> x19, matrix products: 288 us -> 182 us  [the longest x1 25.9 us: fast_device(): jnp.einsum('sqhe,skhe->shqk', grad_attended, values_low, preferred_elemen...]
    while x212 -> x0, local copies, waits for them, and re-layouts: 85.9 us -> none
    unnamed x1 -> x0, blocking collectives: 74.1 us -> none
  transfers between devices with their start and end apart: 42 -> 4, of which waited for: 22 -> 0; matrix products, arithmetic and copies ran while one was open for 20% -> 8% of each run, Pallas kernels for 0% -> 14%
where the time goes in v1:
time: 848 us; the launch traced here: 842 us
  Pallas kernels  368 us (43%)
  matrix products  221 us (26%)
  local copies, waits for them, and re-layouts  134 us (16%)
  other arithmetic  116 us (14%)
    pallas_call x1, Pallas kernels, gather_weights(): pl.pallas_call(functools.partial(gather_kernel, grid, chunks), out_shape=...  199 us
    pallas_call x1, Pallas kernels, reduce_weights(): pl.pallas_call(functools.partial(reduce_kernel, grid, chunks), out_shape=...  121 us
    pallas_call x4, Pallas kernels, swap(): pl.pallas_call(functools.partial(swap_kernel, count, to_all), out_shape=j...  48.1 us
    unnamed x158, local copies, waits for them, and re-layouts  30.5 us
    convert_element_type x1, other arithmetic, fast_device(): grad_scores = (attn_prob * (grad_prob - row_dot)).astype(BF16)  28.5 us
    dot_general x1, matrix products, fast_device(): jnp.einsum('sqhe,skhe->shqk', grad_attended, values_low, preferred_elemen...  25.9 us
    mul x1, matrix products, fast_device(): key_unit * jnp.sum(grad_key_unit * key_unit, axis=-1, keepdims=True)  21.4 us
    dot_general x1, matrix products, fast_device(): jnp.einsum('sld,jdf->jslf', dm_low, down, preferred_element_type=F32)  17.7 us
  transfers between devices with their start and end apart: 4, of which 0 were waited for; matrix products, arithmetic and copies ran while one was open for 8% of the time, Pallas kernels for 14%

profile of v1, /device:TPU:0, one launch (start us, length us, event | category | flops | bytes accessed | tf_op | source)
XLA Modules:
  0.0 841.8 jit_solution(6417972158617991774)
XLA Ops:
  7.3 13.7 %gather_small.1 = bf16[32,32,128]{2,1,0:T(8,128)(2,1)} custom-call(bf16[32,128]{1,0:T(8,128)(2,1)} %bitcast.391), custom_call_target="tpu_custom_call" | custom-call | tf_op jit(solution)/shard_map/gather_small/pallas_call | solution.py:531
  27.2 198.7 %gather_weights.1 = (bf16[12,4,2,2,64,512]{5,4,3,2,1,0:T(8,128)(2,1)}, bf16[2,340,2,1024]{3,2,1,0:T(2,128)(2,1)}, bf16[2,340,2,1024]{3,2,1,0:T(2,128)(2,1)}) custom-call(bf16[12,64,512]{2,1,0:T(8,128)(2,1)} %pad_maximum_fusion.4.shard_ref, bf16[340,2,1024]{2,1,0:T(2,128)(2,1)} %bitcast.352, bf16[340,2,1024]{2,1,0:T(2,128)(2,1)} %bitcast.353), custom_call_target="tpu_custom_call" | custom-call | tf_op jit(solution)/shard_map/gather_weights/pallas_call | solution.py:630
  253.1 10.0 %swap_modulation.1 = f32[32,8,128]{2,1,0:T(8,128)} custom-call(f32[32,8,128]{2,1,0:T(8,128)} %bitcast.363), custom_call_target="tpu_custom_call" | custom-call | tf_op jit(solution)/shard_map/swap_modulation/pallas_call | solution.py:531
  311.4 17.2 %fusion.99 = (f32[2,8,680]{2,1,0:T(8,128)}, f32[2,8,680,680]{2,3,1,0:T(8,128)}) fusion(pred[2,680,680]{1,2,0:T(8,128)(4,1)} %broadcast_compare_fusion, f32[2,680,8,64]{1,3,2,0:T(8,128)} %bitcast.332, f32[2,680,8]{1,2,0:T(8,128)} %add_rsqrt_fusion, f32[2,680,8,64]{1,3,2,0:T(8,128)S(1)} %bitcast.327, f32[8]{0:T(128)S(1)} %copy-done.49, ...), kind=kOutput, calls=%fused_computation.206 | convolution fusion | flops 973369024 | bytes 36221600 | tf_op jit(solution)/shard_map/sub | solution.py:899
  328.7 15.9 %fusion.62 = bf16[2,8,64,680]{3,2,1,0:T(8,128)(2,1)} fusion(f32[2,680,8,64]{1,3,2,0:T(8,128)} %bitcast.345, f32[8,64]{1,0:T(8,128)} %copy.272, f32[2,8,680,680]{2,3,1,0:T(8,128)} %get-tuple-element.140, f32[2,8,680]{2,1,0:T(8,128)} %get-tuple-element.139), kind=kOutput, calls=%fused_computation.116 | convolution fusion | flops 963880960 | bytes 33817088 | tf_op jit(solution)/shard_map/shqk,skhe->sqhe/dot_general | solution.py:902
  372.2 9.9 %fusion.88 = f32[4,512,2,680]{1,3,2,0:T(8,128)} fusion(bf16[4,1024,512,1]{2,1,3,0:T(8,128)(2,1)S(1)} %bitcast.341, f32[2,680,1024]{2,1,0:T(8,128)S(1)} %get-tuple-element.112, f32[2,1024]{1,0:T(2,128)S(1)} %copy-done.52, f32[2,1024]{1,0:T(2,128)S(1)} %copy-done.33, f32[2,680]{1,0:T(2,128)S(1)} %add_rsqrt_fusion.2, f32[2,680]{1,0:T(2,128)S(1)} %broadcast_multiply_fusion.4), kind=kOutput, calls=%fused_computation.199 | convolution fusion | flops 5711216640 | bytes 20933248 | tf_op jit(solution)/shard_map/sld,jdf->jslf/dot_general | solution.py:911
  382.1 15.5 %fusion.40 = bf16[4,1024,512]{1,2,0:T(8,128)(2,1)} fusion(f32[680,2,1024]{2,1,0:T(2,128)S(1)} %bitcast_convert_fusion.7, f32[2,1024]{1,0:T(2,128)S(1)} %copy-done.32, f32[4,512,2,680]{1,3,2,0:T(8,128)} %fusion.88, f32[4,512]{1,0:T(4,128)S(1)} %add.256), kind=kOutput, calls=%fused_computation.75 | convolution fusion | flops 5736988672 | bytes 20922368 | tf_op jit(solution)/shard_map/sld,jslf->jdf/dot_general | solution.py:922
  397.6 17.7 %fusion.100 = (f32[4,512]{1,0:T(4,128)S(1)}, bf16[4,2,680,512]{3,2,1,0:T(8,128)(2,1)}) fusion(f32[4,512,2,680]{1,3,2,0:T(8,128)} %fusion.88, f32[4,512]{1,0:T(4,128)S(1)} %add.256, bf16[4,1024,512,1]{2,1,3,0:T(8,128)(2,1)S(1)} %bitcast.340, f32[680,2,1024]{2,1,0:T(2,128)S(1)} %bitcast_convert_fusion.7, f32[2,1024]{1,0:T(2,128)S(1)} %copy-done.32), kind=kOutput, calls=%fused_computation.207 | convolution fusion | flops 5765527552 | bytes 26501120 | tf_op jit(solution)/shard_map/sld,jdf->jslf/dot_general | solution.py:923
  415.3 9.9 %bitcast_convert_fusion.4 = bf16[2,680,1024]{2,1,0:T(8,128)(2,1)} fusion(bf16[4,1024,512,1]{2,1,3,0:T(8,128)(2,1)S(1)} %bitcast.342, bf16[4,2,680,512]{3,2,1,0:T(8,128)(2,1)} %get-tuple-element.147), kind=kOutput, calls=%fused_computation.41 | convolution fusion | flops 5705646080 | bytes 12550144 | tf_op jit(solution)/shard_map/jslf,jdf->sld/dot_general | solution.py:928
  433.1 12.5 %bitcast_convert_fusion.5 = bf16[2,680,1024]{2,1,0:T(8,128)(2,1)} fusion(bf16[4,1024,512,1]{2,1,3,0:T(8,128)(2,1)} %bitcast.339, f32[4,512,2,680]{1,3,2,0:T(8,128)} %fusion.88, f32[4,512]{1,0:T(4,128)S(1)} %add.256), kind=kOutput, calls=%fused_computation.46 | convolution fusion | flops 5733498880 | bytes 18128896 | tf_op jit(solution)/shard_map/jslf,jdf->sld/dot_general | solution.py:914
  445.6 11.2 %fusion.39 = bf16[4,1024,512]{1,2,0:T(8,128)(2,1)} fusion(bf16[4,2,680,512]{3,2,1,0:T(8,128)(2,1)} %get-tuple-element.147, f32[2,680,1024]{2,1,0:T(8,128)S(1)} %bitcast.323, f32[2,1024]{1,0:T(2,128)S(1)} %copy-done.52, f32[2,1024]{1,0:T(2,128)S(1)} %copy-done.33, f32[2,680]{1,0:T(2,128)S(1)} %add_rsqrt_fusion.2, f32[2,680]{1,0:T(2,128)S(1)} %broadcast_multiply_fusion.4), kind=kOutput, calls=%fused_computation.74 | convolution fusion | flops 5713313792 | bytes 15362688 | tf_op jit(solution)/shard_map/sld,jslf->jdf/dot_general | solution.py:927
  463.1 7.2 multiply_reduce_fusion.1
  470.4 13.8 %multiply_reduce_fusion.8 = (f32[1024]{0:T(1024)}, f32[2,1024]{1,0:T(2,128)}, f32[2,680,1024]{2,1,0:T(8,128)S(1)}, f32[2,1024]{1,0:T(2,128)}, f32[2,680,1024]{2,1,0:T(8,128)}, /*index=5*/f32[1024]{0:T(1024)S(1)}) fusion(f32[2,1024]{1,0:T(2,128)S(1)} %copy-done.30, f32[1024]{0:T(1024)S(1)} %reshape.396, bf16[2,680,1024]{2,1,0:T(8,128)(2,1)} %collective-permute-done, ...), kind=kLoop, calls=%fused_computation.66 | loop fusion | flops 37595136 | bytes 39073024 | tf_op jit(solution)/shard_map/reduce_sum | solution.py:935
  489.9 16.2 %bitcast_convert_fusion.6 = (bf16[2,680,8,64]{1,3,2,0:T(8,128)(2,1)}, f32[2,8,64,680]{3,2,1,0:T(8,128)}) fusion(bf16[2,680,8,64]{1,3,2,0:T(8,128)(2,1)} %bitcast.349, f32[2,8,680,680]{2,3,1,0:T(8,128)} %get-tuple-element.140, f32[2,8,680]{2,1,0:T(8,128)} %get-tuple-element.139), kind=kOutput, calls=%fused_computation.80 | convolution fusion | flops 962488320 | bytes 35207680 | tf_op jit(solution)/shard_map/shqk,sqhe->skhe/dot_general | solution.py:944
  506.1 25.9 %multiply_reduce_fusion = (f32[2,8,680]{2,1,0:T(8,128)}, f32[2,8,680,680]{2,3,1,0:T(8,128)}) fusion(f32[2,8,680,680]{2,3,1,0:T(8,128)} %get-tuple-element.140, f32[2,8,680]{2,1,0:T(8,128)} %get-tuple-element.139, bf16[2,680,8,64]{1,3,2,0:T(8,128)(2,1)} %bitcast.350, f32[2,680,8,64]{1,3,2,0:T(8,128)S(1)} %bitcast.346, f32[8,64]{1,0:T(8,128)S(1)} %copy-done.53), kind=kOutput, calls=%fused_computation.4 | convolution fusion | flops 970572160 | bytes 63454208 | tf_op jit(solution)/shard_map/sqhe,skhe->shqk/dot_general | solution.py:941
  532.0 28.5 %multiply_convert_fusion = bf16[2,8,680,680]{2,3,1,0:T(8,128)(2,1)} fusion(f32[2,8,680,680]{2,3,1,0:T(8,128)} %get-tuple-element.142, f32[2,8,680]{2,1,0:T(8,128)} %get-tuple-element.141, f32[2,8,680,680]{2,3,1,0:T(8,128)} %get-tuple-element.140, f32[2,8,680]{2,1,0:T(8,128)} %get-tuple-element.139), kind=kLoop, calls=%fused_computation.3 | loop fusion | flops 29593600 | bytes 74071040 | tf_op jit(solution)/shard_map/convert_element_type | solution.py:943
  560.5 21.4 %fusion.43 = bf16[2,680,8,64]{1,3,2,0:T(8,128)(2,1)} fusion(f32[2,680,8,64]{1,3,2,0:T(8,128)} %bitcast.333, f32[2,680,8]{1,2,0:T(8,128)} %add_rsqrt_fusion, bf16[2,8,680,680]{2,3,1,0:T(8,128)(2,1)} %multiply_convert_fusion, f32[2,680,8,64]{1,3,2,0:T(8,128)S(1)} %bitcast.328, f32[8]{0:T(128)} %exp.15, f32[2,680,8]{1,2,0:T(8,128)} %add_rsqrt_fusion.1, ...), kind=kOutput, calls=%fused_computation.84 | convolution fusion | flops 1904446080 | bytes 21849120 | tf_op jit(solution)/shard_map/mul | solution.py:953
  581.8 11.8 %fusion.44 = (f32[8]{0:T(128)}, f32[2,8,64,680]{3,2,1,0:T(8,128)}) fusion(f32[2,680,8,64]{1,3,2,0:T(8,128)S(1)} %bitcast.329, f32[2,680,8]{1,2,0:T(8,128)} %add_rsqrt_fusion.1, f32[8,64]{1,0:T(8,128)S(1)} %copy-done.23, bf16[2,8,680,680]{2,3,1,0:T(8,128)(2,1)} %multiply_convert_fusion, f32[2,680,8,64]{1,3,2,0:T(8,128)} %bitcast.334, ...), kind=kOutput, calls=%fused_computation.87 | convolution fusion | flops 951173120 | bytes 23241760 | tf_op jit(solution)/shard_map/shqk,skhe->sqhe/dot_general | solution.py:945
  627.3 9.7 %fusion.41 = bf16[3,1024,512]{1,2,0:T(8,128)(2,1)} fusion(bf16[1,2,680,512]{3,2,0,1:T(8,128)(2,1)S(1)} %copy-done.19, bf16[1,2,680,512]{3,2,0,1:T(8,128)(2,1)} %copy.293, bf16[1,2,680,512]{3,2,0,1:T(8,128)(2,1)S(1)} %copy.292, f32[2,680,1024]{2,1,0:T(8,128)} %copy-done.10, f32[2,1024]{1,0:T(2,128)S(1)} %copy-done.51, f32[2,1024]{1,0:T(2,128)S(1)} %copy-done.41), kind=kOutput, calls=%fused_computation.78 | convolution fusion | flops 4288118784 | bytes 12910592 | tf_op jit(solution)/shard_map/sld,jslc->jdc/dot_general | solution.py:959
  653.6 9.9 %pad_maximum_fusion.full_ref = bf16[12,4,2,2,64,512]{5,4,3,2,1,0:T(8,128)(2,1)} fusion(bf16[4,4,2,2,64,512]{5,4,3,2,1,0:T(8,128)(2,1)S(1)} %bitcast.335, bf16[4,4,2,2,64,512]{5,4,3,2,1,0:T(8,128)(2,1)S(1)} %bitcast.336, bf16[1,4,2,2,64,512]{5,4,3,2,1,0:T(8,128)(2,1)S(1)} %bitcast.354, bf16[3,4,2,2,64,512]{5,4,3,2,1,0:T(8,128)(2,1)S(1)} %bitcast.337), kind=kLoop, calls=%fused_computation.14 | loop fusion | flops 18874368 | bytes 25165824 | tf_op jit(solution)/shard_map/concatenate | solution.py:1031
  663.6 120.9 %reduce_weights.1 = f32[12,64,512]{2,1,0:T(8,128)S(1)} custom-call(bf16[12,4,2,2,64,512]{5,4,3,2,1,0:T(8,128)(2,1)} %pad_maximum_fusion.full_ref), custom_call_target="tpu_custom_call" | custom-call | tf_op jit(solution)/shard_map/reduce_weights/pallas_call | solution.py:767
  788.1 8.2 fusion.36
  797.9 11.9 %swap_grads.1 = f32[32,16,128]{2,1,0:T(8,128)} custom-call(f32[32,16,128]{2,1,0:T(8,128)} %bitcast.357), custom_call_target="tpu_custom_call" | custom-call | tf_op jit(solution)/shard_map/swap_grads/pallas_call | solution.py:531
  812.9 12.5 %swap_condition.1 = f32[32,16,128]{2,1,0:T(8,128)} custom-call(f32[32,16,128]{2,1,0:T(8,128)} %pad_maximum_fusion.5.src_ref), custom_call_target="tpu_custom_call" | custom-call | tf_op jit(solution)/shard_map/swap_condition/pallas_call | solution.py:531
  (332 shorter events, 209.6 us)
Async XLA Ops:
  0.6 247.5 %copy-start = (bf16[512,6,64]{0,2,1:T(8,128)(2,1)S(1)}, bf16[512,6,64]{0,2,1:T(8,128)(2,1)}, u32[]{:S(2)}) copy-start(bf16[512,6,64]{0,2,1:T(8,128)(2,1)} %param.19) | copy-start | bytes 1179652
  22.0 203.9 %copy-start.24 = (bf16[16,2,4096]{2,1,0:T(2,128)(2,1)}, bf16[16,2,4096]{2,1,0:T(2,128)(2,1)S(1)}, u32[]{:S(2)}) copy-start(bf16[16,2,4096]{2,1,0:T(2,128)(2,1)S(1)} %reshape.362) | copy-start | bytes 786436
  27.2 203.2 %copy-start.56 = (f32[8]{0:T(128)S(1)}, f32[8]{0:T(128)}, u32[]{:S(2)}) copy-start(f32[8]{0:T(128)} %param.24) | copy-start | bytes 100
  230.3 57.9 %copy-start.14 = (bf16[3,4,2,2,64,512]{5,4,3,2,1,0:T(8,128)(2,1)}, bf16[3,4,2,2,64,512]{5,4,3,2,1,0:T(8,128)(2,1)S(1)}, u32[]{:S(2)}) copy-start(bf16[3,4,2,2,64,512]{5,4,3,2,1,0:T(8,128)(2,1)S(1)} %slice.166) | copy-start | bytes 9437188
  240.9 70.5 %copy-start.22 = (f32[8,64]{1,0:T(8,128)}, f32[8,64]{1,0:T(8,128)S(1)}, u32[]{:S(2)}) copy-start(f32[8,64]{1,0:T(8,128)S(1)} %copy.277) | copy-start | bytes 6148
  286.4 65.1 %copy-start.28 = (f32[2,680]{1,0:T(2,128)}, f32[2,680]{1,0:T(2,128)S(1)}, u32[]{:S(2)}) copy-start(f32[2,680]{1,0:T(2,128)S(1)} %add_rsqrt_fusion.3) | copy-start | bytes 16324
  306.3 22.3 %copy-start.3 = (f32[1,2,680,512]{2,3,1,0:T(8,128)}, f32[1,2,680,512]{2,3,1,0:T(8,128)S(1)}, u32[]{:S(2)}) copy-start(f32[1,2,680,512]{2,3,1,0:T(8,128)S(1)} %copy.273) | copy-start | bytes 8355844
  344.6 16.7 %slice-start = ((s8[5570560]{0:T(1024)(128)(4,1)}), s8[1376256]{0:T(1024)(128)(4,1)S(1)}, s32[]{:S(2)}) async-start(s8[5570560]{0:T(1024)(128)(4,1)} %bitcast.320), calls=%async_computation | async-start | bytes 2752512
  349.6 11.7 %collective-permute-start = (bf16[2,680,1024]{2,1,0:T(8,128)(2,1)}, bf16[2,680,1024]{2,1,0:T(8,128)(2,1)}, u32[]{:S(2)}, u32[]{:S(2)}) collective-permute-start(bf16[2,680,1024]{2,1,0:T(8,128)(2,1)} %convolution_convert_fusion), channel_id=1, source_target_pairs={{0,1},{1,0},{2,3},{3,2},{4,5},{5,4},{6,7},{7,6},{8,9},{9,8},{10,11... | collective-permute-start | bytes 8355848 | tf_op jit(solution)/shard_map/ppermute | solution.py:795
  361.2 36.4 %copy-start.6 = (f32[680,2,1024]{2,1,0:T(2,128)}, f32[680,2,1024]{2,1,0:T(2,128)S(1)}, u32[]{:S(2)}) copy-start(f32[680,2,1024]{2,1,0:T(2,128)S(1)} %bitcast_convert_fusion.7) | copy-start | bytes 16711684
  432.6 30.5 %collective-permute-start.2 = (bf16[2,680,1024]{2,1,0:T(8,128)(2,1)}, bf16[2,680,1024]{2,1,0:T(8,128)(2,1)}, u32[]{:S(2)}, u32[]{:S(2)}) collective-permute-start(bf16[2,680,1024]{2,1,0:T(8,128)(2,1)} %bitcast_convert_fusion.4), channel_id=1, source_target_pairs={{0,1},{1,0},{2,3},{3,2},{4,5},{5,4},{6,7},{7,6},{8,9},{9,8},{10,11... | collective-permute-start | bytes 8355848 | tf_op jit(solution)/shard_map/ppermute | solution.py:795
  445.6 24.7 %collective-permute-start.1 = (bf16[2,680,1024]{2,1,0:T(8,128)(2,1)}, bf16[2,680,1024]{2,1,0:T(8,128)(2,1)}, u32[]{:S(2)}, u32[]{:S(2)}) collective-permute-start(bf16[2,680,1024]{2,1,0:T(8,128)(2,1)} %bitcast_convert_fusion.5), channel_id=1, source_target_pairs={{0,1},{1,0},{2,3},{3,2},{4,5},{5,4},{6,7},{7,6},{8,9},{9,8},{10,11... | collective-permute-start | bytes 8355848 | tf_op jit(solution)/shard_map/ppermute | solution.py:795
  532.0 28.5 %copy-start.4 = (f32[1,2,680,512]{2,3,1,0:T(8,128)S(1)}, f32[1,2,680,512]{2,3,1,0:T(8,128)}, u32[]{:S(2)}) copy-start(f32[1,2,680,512]{2,3,1,0:T(8,128)} %copy-done.3) | copy-start | bytes 8355844
  532.0 28.5 %copy-start.23 = (f32[8,64]{1,0:T(8,128)S(1)}, f32[8,64]{1,0:T(8,128)}, u32[]{:S(2)}) copy-start(f32[8,64]{1,0:T(8,128)} %copy-done.22) | copy-start | bytes 6148
  643.3 144.8 %collective-permute-start.3 = (bf16[2,680,1024]{2,1,0:T(8,128)(2,1)}, bf16[2,680,1024]{2,1,0:T(8,128)(2,1)}, u32[]{:S(2)}, u32[]{:S(2)}) collective-permute-start(bf16[2,680,1024]{2,1,0:T(8,128)(2,1)} %bitcast_convert_fusion.3), channel_id=1, source_target_pairs={{0,1},{1,0},{2,3},{3,2},{4,5},{5,4},{6,7},{7,6},{8,9},{9,8},{10,11... | collective-permute-start | bytes 8355848 | tf_op jit(solution)/shard_map/ppermute | solution.py:795
  663.6 121.0 %copy-start.54 = (f32[8,64]{1,0:T(8,128)S(1)}, f32[8,64]{1,0:T(8,128)}, u32[]{:S(2)}) copy-start(f32[8,64]{1,0:T(8,128)} %get-tuple-element.121) | copy-start | bytes 6148
  663.6 123.8 %copy-start.36 = (f32[2,1,16,64]{3,2,0,1:T(8,128)S(1)}, f32[2,1,16,64]{3,2,0,1:T(8,128)}, u32[]{:S(2)}) copy-start(f32[2,1,16,64]{3,2,0,1:T(8,128)} %stack.37) | copy-start | bytes 24580
  663.6 123.8 %copy-start.37 = (f32[2,1,16,64]{3,2,0,1:T(8,128)S(1)}, f32[2,1,16,64]{3,2,0,1:T(8,128)}, u32[]{:S(2)}) copy-start(f32[2,1,16,64]{3,2,0,1:T(8,128)} %stack.38) | copy-start | bytes 24580
  663.6 123.8 %copy-start.55 = (f32[8]{0:T(128)S(1)}, f32[8]{0:T(128)}, u32[]{:S(2)}) copy-start(f32[8]{0:T(128)} %get-tuple-element.148) | copy-start | bytes 100
  663.6 123.8 %copy-start.57 = (f32[8]{0:T(128)S(1)}, f32[8]{0:T(128)}, u32[]{:S(2)}) copy-start(f32[8]{0:T(128)} %param.24) | copy-start | bytes 100
  663.6 124.5 %copy-start.27 = (f32[2,680]{1,0:T(2,128)S(1)}, f32[2,680]{1,0:T(2,128)}, u32[]{:S(2)}) copy-start(f32[2,680]{1,0:T(2,128)} %copy-done.26) | copy-start | bytes 16324
  663.6 124.5 %copy-start.29 = (f32[2,680]{1,0:T(2,128)S(1)}, f32[2,680]{1,0:T(2,128)}, u32[]{:S(2)}) copy-start(f32[2,680]{1,0:T(2,128)} %copy-done.28) | copy-start | bytes 16324
  796.4 30.4 %copy-start.25 = (f32[32,1024]{1,0:T(8,128)S(1)}, f32[32,1024]{1,0:T(8,128)}, u32[]{:S(2)}) copy-start(f32[32,1024]{1,0:T(8,128)} %reshape.392) | copy-start | bytes 393220
  796.4 31.7 %copy-start.47 = (f32[2,340]{1,0:T(2,128)S(1)}, f32[2,340]{1,0:T(2,128)}, u32[]{:S(2)}) copy-start(f32[2,340]{1,0:T(2,128)} %constant_dynamic-slice_fusion.2) | copy-start | bytes 8164
  (44 other events, 345.6 us)

commit v2 on v1

--- a/solution.py
+++ b/solution.py
@@ -470,6 +470,8 @@
 ANY = pl.ANY
 F32 = jnp.float32
 BF16 = jnp.bfloat16
+SCALES = 10
+MASK = -16384.0
 
 
 def place():
@@ -559,9 +561,9 @@
     greet_all(nz * ny * nx * 2)
     swaps = []
     for i, (src, dst) in enumerate(((tok_ref, tok_out), (grad_ref, grad_out))):
-        own = pltpu.make_async_copy(src, dst.at[core], local_sem.at[chunks + i])
+        own = pltpu.make_async_copy(src, dst.at[:, core], local_sem.at[chunks + i])
         own.start()
-        copy = remote(src, dst.at[core], t_send.at[i], t_recv.at[i], sibling)
+        copy = remote(src, dst.at[:, core], t_send.at[i], t_recv.at[i], sibling)
         copy.start()
         swaps += [own, copy]
 
@@ -631,10 +633,10 @@
         functools.partial(gather_kernel, grid, chunks),
         out_shape=[
             jax.ShapeDtypeStruct((chunks, nz, ny, nx) + shard.shape[1:], shard.dtype),
-            jax.ShapeDtypeStruct((2,) + tok.shape, tok.dtype),
-            jax.ShapeDtypeStruct((2,) + grad.shape, grad.dtype),
+            jax.ShapeDtypeStruct((tok.shape[0], 2) + tok.shape[1:], tok.dtype),
+            jax.ShapeDtypeStruct((grad.shape[0], 2) + grad.shape[1:], grad.dtype),
         ],
-        in_specs=[pl.BlockSpec(memory_space=ANY)] * 3,
+        in_specs=[pl.BlockSpec(memory_space=ANY)] + [pl.BlockSpec(memory_space=pltpu.VMEM)] * 2,
         out_specs=[pl.BlockSpec(memory_space=ANY)] * 3,
         scratch_shapes=[
             pltpu.SemaphoreType.DMA((chunks + 2,)),
@@ -791,6 +793,343 @@
     )(full)
 
 
+def dot(a, b):
+    return jnp.dot(a, b, preferred_element_type=F32)
+
+
+def dot_nt(a, b):
+    return lax.dot_general(a, b, (((1,), (1,)), ((), ())), preferred_element_type=F32)
+
+
+def dot_tn(a, b):
+    return lax.dot_general(a, b, (((0,), (0,)), ((), ())), preferred_element_type=F32)
+
+
+def lane_code(rows):
+    lane = lax.broadcasted_iota(jnp.int32, (rows, 128), 1)
+    return lane < 64, lane & 63
+
+
+def both_heads(pair, spare):
+    first, unused = lane_code(pair.shape[0])
+    pair = pair.astype(F32)
+    if not isinstance(spare, float):
+        spare = spare.astype(F32)
+    return (
+        jnp.where(first, pair, spare).astype(BF16),
+        jnp.where(first, spare, pair).astype(BF16),
+    )
+
+
+def column_sum(values):
+    return jnp.sum(values, axis=0, keepdims=True)
+
+
+def transpose_into(dst, src):
+    def step(i, carry):
+        at = pl.multiple_of(i * 128, 128)
+        dst[:, pl.ds(at, 128)] = src[pl.ds(at, 128), :].T
+        return carry
+
+    lax.fori_loop(0, src.shape[0] // 128, step, 0)
+
+
+def for_blocks(count, rows, body):
+    def step(a, carry):
+        body(a, pl.ds(pl.multiple_of(a * rows, 16), rows))
+        return carry
+
+    lax.fori_loop(0, count, step, 0)
+
+
+def split_kernel(tok_ref, grad_ref, tok_out, grad_out):
+    length = tok_ref.shape[0]
+    for src, dst in ((tok_ref, tok_out), (grad_ref, grad_out)):
+        dst[...] = jnp.zeros_like(dst)
+        for s in range(src.shape[1]):
+            dst[s, 0:length] = src[:, s, :].astype(F32).astype(BF16)
+
+
+def attn_forward(sizes, x, mod, scale, w, query_bias, value_bias, key_scale, ones, mixed, qaug, keys, values_low, key_spare, rq, rk, att, part):
+    seqs, pad = sizes
+    width = x.shape[1]
+    pairs = att.shape[1] // 128
+
+    def project(a, rows):
+        s = a // 2
+        normed, unused = normalize(x[rows, :].astype(F32))
+        m = (normed * (1.0 + mod[s, 2:3, :]) + mod[s, 4:5, :]).astype(BF16)
+        mixed[rows, :] = m
+        first, code = lane_code(pad)
+        level = scale[rows, :]
+        q_spare = jnp.where(code == level, 1.0, 0.0)
+        k_spare = jnp.where(
+            code < SCALES, jnp.where(level > code, MASK, 0.0), jnp.where(code < SCALES + 3, 1.0, 0.0)
+        )
+        key_spare[rows, :] = k_spare.astype(BF16)
+        values = dot(m, w[0]) + query_bias[...]
+        inv = lax.rsqrt(dot((values * values).astype(BF16), ones[...]) + HEAD_EPS)
+        rq[rows, :] = inv.astype(BF16)
+        values = values * inv * key_scale[...]
+        for p in range(pairs):
+            piece = values[:, p * 128 : p * 128 + 128]
+            qaug[2 * p, rows, :] = jnp.where(first, piece, q_spare).astype(BF16)
+            qaug[2 * p + 1, rows, :] = jnp.where(first, q_spare, piece).astype(BF16)
+        values = dot(m, w[1])
+        inv = lax.rsqrt(dot((values * values).astype(BF16), ones[...]) + HEAD_EPS)
+        rk[rows, :] = inv.astype(BF16)
+        keys[rows, :] = (values * inv).astype(BF16)
+        values_low[rows, :] = (dot(m, w[2]) + value_bias[...]).astype(BF16)
+
+    for_blocks(seqs * 2, pad, project)
+
+    def attend(i, carry):
+        p = i // (seqs * 2)
+        block = i % (seqs * 2)
+        s = block // 2
+        rows = pl.ds(pl.multiple_of(block * pad, 16), pad)
+        all_rows = pl.ds(pl.multiple_of(s * 2 * pad, 16), 2 * pad)
+        lanes = pl.ds(pl.multiple_of(p * 128, 128), 128)
+        first, code = lane_code(pad)
+        k_sides = both_heads(keys[all_rows, lanes], key_spare[all_rows, :])
+        v_sides = both_heads(values_low[all_rows, lanes], 1.0)
+        outs = []
+        for side in range(2):
+            h = 2 * p + side
+            q = qaug[h, rows, :]
+            prob = jnp.exp2(dot_nt(q, k_sides[side])).astype(BF16)
+            o = dot(prob, v_sides[side])
+            outs.append(o / pltpu.roll(o, 64, 1))
+            norm = -jnp.log2(o)
+            high = norm.astype(BF16)
+            rest = norm - high.astype(F32)
+            middle = rest.astype(BF16)
+            low = (rest - middle.astype(F32)).astype(BF16)
+            spare = jnp.logical_not(first) if side == 0 else first
+            q = q.astype(F32)
+            for at, piece in enumerate((high, middle, low)):
+                q = jnp.where(spare & (code == SCALES + at), piece.astype(F32), q)
+            qaug[h, rows, :] = q.astype(BF16)
+        att[rows, lanes] = jnp.where(first, outs[0], outs[1]).astype(BF16)
+        return carry
+
+    lax.fori_loop(0, pairs * seqs * 2, attend, 0)
+
+    def out_project(a, rows):
+        part[rows, :] = dot_nt(att[rows, :], w[3]).astype(BF16)
+
+    for_blocks(seqs * 2, pad, out_project)
+
+
+def mlp_forward(sizes, x, part, part_other, grad, mod, up, up_bias, down, branch, mlp, slope, mlp_part, dm, grad_down, act, turned):
+    seqs, pad = sizes
+    chunks = up.shape[0]
+
+    def mix(a, rows):
+        s = a // 2
+        b = part[rows, :].astype(F32) + part_other[rows, :].astype(F32) + mod[s, 6:7, :]
+        branch[rows, :] = b.astype(BF16)
+        normed, unused = normalize(x[rows, :].astype(F32) + mod[s, 0:1, :] * b)
+        mlp[rows, :] = (normed * (1.0 + mod[s, 3:4, :]) + mod[s, 5:6, :]).astype(BF16)
+        dm[rows, :] = (grad[rows, :].astype(F32) * mod[s, 1:2, :]).astype(BF16)
+
+    for_blocks(seqs * 2, pad, mix)
+    transpose_into(turned, dm)
+    for c in range(chunks):
+
+        def raise_rows(a, rows):
+            h = dot(mlp[rows, :], up[c]) + up_bias[c]
+            square = h * h
+            t = jnp.tanh(h * (GELU_COEF + GELU_COEF * GELU_CUBE * square))
+            act[c, rows, :] = (0.5 * h * (1.0 + t)).astype(BF16)
+            slope[c, rows, :] = (
+                0.5 * (1.0 + t)
+                + h * (1.0 - t * t) * (0.5 * GELU_COEF + 1.5 * GELU_COEF * GELU_CUBE * square)
+            ).astype(BF16)
+
+        for_blocks(seqs * 2, pad, raise_rows)
+        grad_down[c] = dot(turned[...], act[c]).astype(BF16)
+
+    def lower(a, rows):
+        total = dot_nt(act[0, rows, :], down[0])
+        for c in range(1, chunks):
+            total = total + dot_nt(act[c, rows, :], down[c])
+        mlp_part[rows, :] = total.astype(BF16)
+
+    for_blocks(seqs * 2, pad, lower)
+
+
+def mlp_backward(sizes, dm, down, slope, mlp, up, grad_part, grad_up, bias_sum, turned, low):
+    seqs, pad = sizes
+    chunks = up.shape[0]
+    transpose_into(turned, mlp)
+    bias_sum[...] = jnp.zeros_like(bias_sum)
+    for c in range(chunks):
+
+        def back(a, rows):
+            gh = dot(dm[rows, :], down[c]) * slope[c, rows, :].astype(F32)
+            bias_sum[c] += column_sum(gh)
+            low[c, rows, :] = gh.astype(BF16)
+
+        for_blocks(seqs * 2, pad, back)
+        grad_up[c] = dot(turned[...], low[c]).astype(BF16)
+
+    def gather(a, rows):
+        total = dot_nt(low[0, rows, :], up[0])
+        for c in range(1, chunks):
+            total = total + dot_nt(low[c, rows, :], up[c])
+        grad_part[rows, :] = total.astype(BF16)
+
+    for_blocks(seqs * 2, pad, gather)
+
+
+def middle_backward(sizes, x, grad, branch, grad_part, grad_other, mod, proj, att, grad_mid, grad_att, grad_proj, stats, da, turned):
+    seqs, pad = sizes
+    stats[...] = jnp.zeros_like(stats)
+
+    def back(a, rows):
+        s = a // 2
+        b = branch[rows, :].astype(F32)
+        gm = grad_part[rows, :].astype(F32) + grad_other[rows, :].astype(F32)
+        normed, inverse = normalize(x[rows, :].astype(F32) + mod[s, 0:1, :] * b)
+        stats[s, 1:2, :] += 0.5 * column_sum(gm * normed)
+        stats[s, 2:3, :] += 0.5 * column_sum(gm)
+        mid = grad[rows, :].astype(F32) + norm_back(gm * (1.0 + mod[s, 3:4, :]), normed, inverse)
+        grad_mid[rows, :] = mid.astype(BF16)
+        stats[s, 0:1, :] += 0.5 * column_sum(mid * b)
+        branch_grad = mid * mod[s, 0:1, :]
+        stats[s, 3:4, :] += 0.5 * column_sum(branch_grad)
+        low = branch_grad.astype(BF16)
+        da[rows, :] = low
+        grad_att[rows, :] = dot(low, proj[...]).astype(BF16)
+
+    for_blocks(seqs * 2, pad, back)
+    transpose_into(turned, da)
+    grad_proj[...] = dot(turned[...], att[...]).astype(BF16)
+
+
+def attn_backward(
+    sizes, mixed, w, qaug, keys, values_low, key_spare, grad_att, rq, rk, key_scale, ones, grad_qkv, grad_part, bias_sum, low, turned
+):
+    seqs, pad = sizes
+    pairs = rq.shape[1] // 128
+    bias_sum[...] = jnp.zeros_like(bias_sum)
+    transpose_into(turned, mixed)
+    ln2 = 0.6931471805599453
+
+    def attend(i, carry):
+        p = i // seqs
+        s = i % seqs
+        start = pl.multiple_of(s * 2 * pad, 16)
+        all_rows = pl.ds(start, 2 * pad)
+        lanes = pl.ds(pl.multiple_of(p * 128, 128), 128)
+        first, code = lane_code(pad)
+        first_all, unused = lane_code(2 * pad)
+        k_sides = both_heads(keys[all_rows, lanes], key_spare[all_rows, :])
+        v_sides = both_heads(values_low[all_rows, lanes], 0.0)
+        g_sides = both_heads(grad_att[all_rows, lanes], 0.0)
+        grads_k, grads_v, grads_q = [], [], [[], []]
+        for side in range(2):
+            h = 2 * p + side
+            k = k_sides[side]
+            v = v_sides[side]
+            sum_k = sum_v = None
+            for t in range(2):
+                rows = pl.ds(pl.multiple_of(start + t * pad, 16), pad)
+                q = qaug[h, rows, :]
+                g = g_sides[side][t * pad : t * pad + pad]
+                prob = jnp.exp2(dot_nt(k, q))
+                grad_prob = dot_nt(v, g)
+                ds = (prob * (grad_prob - column_sum(prob * grad_prob))).astype(BF16)
+                gv = dot(prob.astype(BF16), g)
+                gk = dot(ds, q)
+                sum_v = gv if t == 0 else sum_v + gv
+                sum_k = gk if t == 0 else sum_k + gk
+                grads_q[t].append(dot_tn(ds, k))
+            grads_k.append(sum_k)
+            grads_v.append(sum_v)
+        for t in range(2):
+            rows = pl.ds(pl.multiple_of(start + t * pad, 16), pad)
+            gq = jnp.where(first, grads_q[t][0], grads_q[t][1])
+            q = jnp.where(first, qaug[2 * p, rows, :].astype(F32), qaug[2 * p + 1, rows, :].astype(F32))
+            bias_sum[2:3, lanes] += ln2 * column_sum(gq * q)
+            low[0, rows, lanes] = gq.astype(BF16)
+        low[1, all_rows, lanes] = (ln2 * jnp.where(first_all, grads_k[0], grads_k[1])).astype(BF16)
+        low[2, all_rows, lanes] = jnp.where(first_all, grads_v[0], grads_v[1]).astype(BF16)
+        return carry
+
+    lax.fori_loop(0, pairs * seqs, attend, 0)
+
+    def finish(a, rows):
+        first, code = lane_code(pad)
+
+        scale = key_scale[...]
+        unit = jnp.concatenate(
+            [
+                jnp.where(first, qaug[2 * p, rows, :].astype(F32), qaug[2 * p + 1, rows, :].astype(F32))
+                for p in range(pairs)
+            ],
+            axis=1,
+        )
+        unit = unit / scale
+        f = low[0, rows, :].astype(F32) * (scale * ln2)
+        product = f * unit
+        gq = rq[rows, :].astype(F32) * (f - unit * dot(product.astype(BF16), ones[...]))
+        bias_sum[0:1, :] += column_sum(gq)
+        low[0, rows, :] = gq.astype(BF16)
+        unit = keys[rows, :].astype(F32)
+        f = low[1, rows, :].astype(F32)
+        gk = rk[rows, :].astype(F32) * (f - unit * dot((f * unit).astype(BF16), ones[...]))
+        low[1, rows, :] = gk.astype(BF16)
+        bias_sum[1:2, :] += column_sum(low[2, rows, :].astype(F32))
+        total = dot_nt(low[0, rows, :], w[0])
+        for j in range(1, 3):
+            total = total + dot_nt(low[j, rows, :], w[j])
+        grad_part[rows, :] = total.astype(BF16)
+
+    for_blocks(seqs * 2, pad, finish)
+    for j in range(3):
+        grad_qkv[j] = dot(turned[...], low[j]).astype(BF16)
+
+
+def finish_rows(sizes, x, grad, branch, mlp_part, mlp_other, grad_mid, grad_part, grad_other, mod, output, grad_tokens, stats):
+    seqs, pad = sizes
+    core = lax.axis_index("tensor")
+    length = output.shape[0]
+    for s in range(seqs):
+        rows = pl.ds(pl.multiple_of((s * 2 + core) * pad, 16), pad)
+        b = mlp_part[rows, :].astype(F32) + mlp_other[rows, :].astype(F32) + mod[s, 7:8, :]
+        g = grad[rows, :].astype(F32)
+        xs = x[rows, :].astype(F32)
+        middle = xs + mod[s, 0:1, :] * branch[rows, :].astype(F32)
+        out = middle + mod[s, 1:2, :] * b
+        output[:, s, :] = out[0:length]
+        stats[s, 0:1, :] = column_sum(g * b)
+        stats[s, 1:2, :] = column_sum(g * mod[s, 1:2, :])
+        normed, inverse = normalize(xs)
+        gm = grad_part[rows, :].astype(F32) + grad_other[rows, :].astype(F32)
+        stats[s, 2:3, :] = column_sum(gm * normed)
+        stats[s, 3:4, :] = column_sum(gm)
+        gt = grad_mid[rows, :].astype(F32) + norm_back(gm * (1.0 + mod[s, 2:3, :]), normed, inverse)
+        grad_tokens[:, s, :] = gt[0:length]
+        stats[s, 4:8, :] = jnp.zeros_like(stats[s, 4:8, :])
+
+
+def run(body, sizes, operands, outs, scratch=(), name=None):
+    def kernel(*refs):
+        body(sizes, *refs)
+
+    return pl.pallas_call(
+        kernel,
+        out_shape=[jax.ShapeDtypeStruct(shape, dtype) for shape, dtype in outs],
+        in_specs=[pl.BlockSpec(memory_space=pltpu.VMEM)] * len(operands),
+        out_specs=[pl.BlockSpec(memory_space=pltpu.VMEM)] * len(outs),
+        scratch_shapes=[pltpu.VMEM(shape, dtype) for shape, dtype in scratch],
+        compiler_params=pltpu.CompilerParams(vmem_limit_bytes=60 * 2**20),
+        name=name,
+    )(*operands)
+
+
 def sibling_swap(values):
     return lax.ppermute(values, "tensor", [(0, 1), (1, 0)])
 
@@ -840,12 +1179,20 @@
         ],
         axis=0,
     )
-    full, tok_all, grad_all = gather_weights(
-        grid, shard, tokens.transpose(1, 0, 2), out_grad.transpose(1, 0, 2), 0
-    )
+    pad = -(-own_len // 16) * 16
+    total = seqs * 2 * pad
+    sizes = (seqs, pad)
+    tok_own, grad_own = run(
+        lambda unused, *refs: split_kernel(*refs),
+        sizes,
+        (tokens.transpose(1, 0, 2), out_grad.transpose(1, 0, 2)),
+        [((seqs, pad, width), BF16)] * 2,
+        name="split_rows",
+    )
+    full, x, grad = gather_weights(grid, shard, tok_own, grad_own, 0)
     full = full.reshape(-1, width, part)
-    inputs = tok_all.reshape(seq_len, seqs, width).transpose(1, 0, 2).astype(F32)
-    grad_rows = grad_all.reshape(seq_len, seqs, width).transpose(1, 0, 2).astype(F32)
+    x = x.reshape(total, width)
+    grad = grad.reshape(total, width)
 
     pieces = [condition, ada_bias, query_bias, value_bias, proj_bias, up_bias, down_bias]
     small = jnp.concatenate([piece.reshape(1, -1) for piece in pieces], axis=1)
@@ -876,106 +1223,86 @@
     mod_got = mod_got.reshape(dp, 2, -1)[:, :, : seqs * 6 * cols].sum(axis=1)
     modulation = mod_got.reshape(dp, seqs, 6, cols).transpose(1, 2, 0, 3).reshape(seqs, 6, width)
     modulation = modulation + ada_bias_full
-    mod = [modulation[:, j][:, None, :] for j in range(6)]
-
-    normed_attn, inverse_attn = normalize(inputs)
-    mixed_attn = (normed_attn * (1.0 + mod[2]) + mod[4]).astype(BF16)
-    projected = jnp.einsum("sld,jdc->jslc", mixed_attn, full[:3], preferred_element_type=F32)
-    split = lambda values: values.reshape(seqs, seq_len, heads, head_dim)
-    queries = split(projected[0] + query_bias_own)
-    keys_raw = split(projected[1])
-    values_low = split((projected[2] + value_bias_own).astype(BF16))
-    query_inverse = lax.rsqrt(jnp.sum(queries * queries, axis=-1, keepdims=True) + HEAD_EPS)
-    key_inverse = lax.rsqrt(jnp.sum(keys_raw * keys_raw, axis=-1, keepdims=True) + HEAD_EPS)
-    query_unit = queries * query_inverse
-    key_unit = keys_raw * key_inverse
-    scale_factor = jnp.exp(head_scale)[:, None]
-    query_low = (query_unit * scale_factor).astype(BF16)
-    key_low = key_unit.astype(BF16)
-    scores = jnp.einsum("sqhe,skhe->shqk", query_low, key_low, preferred_element_type=F32)
-    allowed = (scale_index[:, None, :] <= scale_index[:, :, None])[:, None]
-    scores = jnp.where(allowed, scores, -1e30)
-    row_max = jnp.max(scores, axis=-1, keepdims=True)
-    weights_exp = jnp.exp(scores - row_max)
-    attn_prob = weights_exp / jnp.sum(weights_exp, axis=-1, keepdims=True)
-    prob_low = attn_prob.astype(BF16)
-    attended = jnp.einsum("shqk,skhe->sqhe", prob_low, values_low, preferred_element_type=F32)
-    attended = attended.reshape(seqs, seq_len, part).astype(BF16)
-    branch_part = jnp.einsum("slc,dc->sld", attended, full[3], preferred_element_type=F32).astype(BF16)
-    branch_attn = branch_part.astype(F32) + sibling_swap(branch_part).astype(F32) + proj_bias_full
-    middle = inputs + mod[0] * branch_attn
-    normed_mlp, inverse_mlp = normalize(middle)
-    mixed_mlp = (normed_mlp * (1.0 + mod[3]) + mod[5]).astype(BF16)
+    ends = jnp.stack([proj_bias_full, down_bias_full])
+    mod = jnp.concatenate([modulation, jnp.broadcast_to(ends, (seqs,) + ends.shape)], axis=1)
+
+    level = jnp.pad(
+        scale_index.reshape(seqs, 2, own_len), ((0, 0), (0, 0), (0, pad - own_len)), constant_values=100
+    ).reshape(total, 1)
+    key_scale = jnp.repeat(jnp.exp(head_scale) * 1.4426950408889634, head_dim).reshape(1, part)
+    head_at = jnp.arange(part) // head_dim
+    ones = (head_at[:, None] == head_at[None, :]).astype(BF16)
+    wide_rows = ((total, width), BF16)
+    part_rows = ((total, part), BF16)
+    head_rows = ((heads, total, 2 * head_dim), BF16)
     up = full[4 : 4 + ff_chunks]
     down = full[4 + ff_chunks :]
-    hidden = jnp.einsum("sld,jdf->jslf", mixed_mlp, up, preferred_element_type=F32)
-    hidden = hidden + up_bias_own.reshape(ff_chunks, 1, 1, part)
-    activated = jax.nn.gelu(hidden, approximate=True).astype(BF16)
-    mlp_part = jnp.einsum("jslf,jdf->sld", activated, down, preferred_element_type=F32).astype(BF16)
-    branch_mlp = mlp_part.astype(F32) + sibling_swap(mlp_part).astype(F32) + down_bias_full
-    output = middle + mod[1] * branch_mlp
-
-    grad_gamma_mlp = jnp.sum(grad_rows * branch_mlp, axis=1)
-    grad_branch_mlp = grad_rows * mod[1]
-    grad_down_bias = jnp.sum(grad_branch_mlp, axis=(0, 1))
-    dm_low = grad_branch_mlp.astype(BF16)
-    grad_down = jnp.einsum("sld,jslf->jdf", dm_low, activated, preferred_element_type=F32).astype(BF16)
-    grad_act = jnp.einsum("sld,jdf->jslf", dm_low, down, preferred_element_type=F32)
-    grad_hidden = grad_act * gelu_slope(hidden)
-    grad_up_bias = jnp.sum(grad_hidden, axis=(1, 2)).reshape(-1)
-    hidden_low = grad_hidden.astype(BF16)
-    grad_up = jnp.einsum("sld,jslf->jdf", mixed_mlp, hidden_low, preferred_element_type=F32).astype(BF16)
-    gm_part = jnp.einsum("jslf,jdf->sld", hidden_low, up, preferred_element_type=F32).astype(BF16)
-    grad_mixed_mlp = gm_part.astype(F32) + sibling_swap(gm_part).astype(F32)
-    grad_scale_mlp = jnp.sum(grad_mixed_mlp * normed_mlp, axis=1)
-    grad_shift_mlp = jnp.sum(grad_mixed_mlp, axis=1)
-    grad_middle = grad_rows + norm_back(grad_mixed_mlp * (1.0 + mod[3]), normed_mlp, inverse_mlp)
-    grad_gamma_attn = jnp.sum(grad_middle * branch_attn, axis=1)
-    grad_branch_attn = grad_middle * mod[0]
-    grad_proj_bias = jnp.sum(grad_branch_attn, axis=(0, 1))
-    da_low = grad_branch_attn.astype(BF16)
-    grad_proj = jnp.einsum("sld,slc->dc", da_low, attended, preferred_element_type=F32).astype(BF16)
-    grad_attended = split(
-        jnp.einsum("sld,dc->slc", da_low, full[3], preferred_element_type=F32).astype(BF16)
-    )
-    grad_prob = jnp.einsum("sqhe,skhe->shqk", grad_attended, values_low, preferred_element_type=F32)
-    row_dot = jnp.sum(attn_prob * grad_prob, axis=-1, keepdims=True)
-    grad_scores = (attn_prob * (grad_prob - row_dot)).astype(BF16)
-    grad_values = jnp.einsum("shqk,sqhe->skhe", prob_low, grad_attended, preferred_element_type=F32)
-    grad_query_scaled = jnp.einsum("shqk,skhe->sqhe", grad_scores, key_low, preferred_element_type=F32)
-    grad_key_unit = jnp.einsum("shqk,sqhe->skhe", grad_scores, query_low, preferred_element_type=F32)
-    grad_head_scale = jnp.sum(grad_query_scaled * query_unit, axis=(0, 1, 3)) * jnp.exp(head_scale)
-    grad_query_unit = grad_query_scaled * scale_factor
-    grad_queries = query_inverse * (
-        grad_query_unit - query_unit * jnp.sum(grad_query_unit * query_unit, axis=-1, keepdims=True)
-    )
-    grad_keys = key_inverse * (
-        grad_key_unit - key_unit * jnp.sum(grad_key_unit * key_unit, axis=-1, keepdims=True)
-    )
-    grad_query_bias = jnp.sum(grad_queries, axis=(0, 1)).reshape(-1)
-    grad_value_bias = jnp.sum(grad_values, axis=(0, 1)).reshape(-1)
-    qkv_low = jnp.stack([grad_queries, grad_keys, grad_values]).reshape(3, seqs, seq_len, part)
-    qkv_low = qkv_low.astype(BF16)
-    grad_qkv = jnp.einsum("sld,jslc->jdc", mixed_attn, qkv_low, preferred_element_type=F32).astype(BF16)
-    ga_part = jnp.einsum("jslc,jdc->sld", qkv_low, full[:3], preferred_element_type=F32).astype(BF16)
-    grad_mixed_attn = ga_part.astype(F32) + sibling_swap(ga_part).astype(F32)
-    grad_scale_attn = jnp.sum(grad_mixed_attn * normed_attn, axis=1)
-    grad_shift_attn = jnp.sum(grad_mixed_attn, axis=1)
-    grad_inputs = grad_middle + norm_back(
-        grad_mixed_attn * (1.0 + mod[2]), normed_attn, inverse_attn
-    )
+    ff_rows = ((ff_chunks, total, part), BF16)
+    weight_rows = ((width, part), BF16)
+    turned = ((width, total), BF16)
+
+    mixed, qaug, keys, values_low, key_spare, rq, rk, att, attn_part = run(
+        attn_forward,
+        sizes,
+        (x, mod, level, full[:4], query_bias_own[None], value_bias_own[None], key_scale, ones),
+        [wide_rows, head_rows, part_rows, part_rows, ((total, 128), BF16), part_rows, part_rows, part_rows, wide_rows],
+        name="attn_forward",
+    )
+    branch, mlp, slope, mlp_part, dm, grad_down = run(
+        mlp_forward,
+        sizes,
+        (x, attn_part, sibling_swap(attn_part), grad, mod, up, up_bias_own.reshape(ff_chunks, 1, part), down),
+        [wide_rows, wide_rows, ff_rows, wide_rows, wide_rows, ((ff_chunks, width, part), BF16)],
+        [ff_rows, turned],
+        name="mlp_forward",
+    )
+    mlp_other = sibling_swap(mlp_part)
+    gm_part, grad_up, up_sum = run(
+        mlp_backward,
+        sizes,
+        (dm, down, slope, mlp, up),
+        [wide_rows, ((ff_chunks, width, part), BF16), ((ff_chunks, 1, part), F32)],
+        [turned, ff_rows],
+        name="mlp_backward",
+    )
+    grad_mid, grad_att, grad_proj, mid_stats = run(
+        middle_backward,
+        sizes,
+        (x, grad, branch, gm_part, sibling_swap(gm_part), mod, full[3], att),
+        [wide_rows, part_rows, weight_rows, ((seqs, 4, width), F32)],
+        [wide_rows, turned],
+        name="middle_backward",
+    )
+    grad_qkv, ga_part, qkv_sum = run(
+        attn_backward,
+        sizes,
+        (mixed, full[:3], qaug, keys, values_low, key_spare, grad_att, rq, rk, key_scale, ones),
+        [((3, width, part), BF16), wide_rows, ((8, part), F32)],
+        [((3, total, part), BF16), turned],
+        name="attn_backward",
+    )
+    output, grad_inputs, end_stats = run(
+        finish_rows,
+        sizes,
+        (x, grad, branch, mlp_part, mlp_other, grad_mid, ga_part, sibling_swap(ga_part), mod),
+        [((own_len, seqs, width), F32), ((own_len, seqs, width), F32), ((seqs, 8, width), F32)],
+        name="finish_rows",
+    )
+    grad_head_scale = jnp.sum(qkv_sum[2].reshape(heads, head_dim), axis=1)
 
     grad_mod = jnp.stack(
         [
-            grad_gamma_attn,
-            grad_gamma_mlp,
-            grad_scale_attn,
-            grad_scale_mlp,
-            grad_shift_attn,
-            grad_shift_mlp,
+            mid_stats[:, 0],
+            end_stats[:, 0],
+            end_stats[:, 2],
+            mid_stats[:, 1],
+            end_stats[:, 3],
+            mid_stats[:, 2],
         ],
         axis=1,
     )
+    grad_proj_bias = jnp.sum(mid_stats[:, 3], axis=0)
+    grad_down_bias = jnp.sum(end_stats[:, 1], axis=0)
     twice = lambda values: jnp.repeat(values[:, None], 2, axis=1)
     to_owner = lambda values: values.reshape(heads, dp, -1).transpose(1, 0, 2).reshape(dp, -1)
     to_both = lambda values: (
@@ -984,29 +1311,35 @@
     send = jnp.concatenate(
         [
             twice(grad_mod.reshape(seqs, 6, dp, cols).transpose(2, 0, 1, 3).reshape(dp, -1)),
-            twice(to_owner(grad_query_bias)),
-            twice(to_owner(grad_value_bias)),
-            twice(to_owner(grad_up_bias)),
+            twice(to_owner(qkv_sum[0])),
+            twice(to_owner(qkv_sum[1])),
+            twice(to_owner(up_sum)),
+            jnp.broadcast_to(grad_head_scale, (dp, 2, heads)),
             to_both(grad_proj_bias),
             to_both(grad_down_bias),
-            jnp.broadcast_to(grad_head_scale, (dp, 2, heads)),
         ],
         axis=2,
     )
     rows = -(-send.shape[2] // (8 * 128)) * 8
     got = swap(pad_rows(send.reshape(count, -1), rows), count, False, 3, "swap_grads")
-    got = own_of(got.reshape(dp, 2, -1))
+    got = got.reshape(dp, 2, -1)
     n_mod = seqs * 6 * cols
-    mod_low = got[:, :n_mod].reshape(dp * seqs, 6, cols)
+    mod_low = jnp.sum(got[:, :, :n_mod], axis=1).reshape(dp * seqs, 6, cols)
     grad_ada_bias_cols = jnp.sum(mod_low, axis=0)
     mod_low = mod_low.astype(BF16)
-    sums = jnp.sum(got[:, n_mod:], axis=0)
-    owned, at = [], 0
-    for shape in (query_bias.shape, value_bias.shape, up_bias.shape, proj_bias.shape, down_bias.shape):
-        size = shape[0] * shape[1]
-        owned.append(sums[at : at + size].reshape(shape))
-        at += size
-    scale_total = sums[at : at + heads]
+    own_sums = jnp.sum(own_of(got), axis=0)
+    all_sums = jnp.sum(got, axis=(0, 1))
+    owned, at = [], n_mod
+    for piece, sums in (
+        (query_bias, own_sums),
+        (value_bias, own_sums),
+        (up_bias, own_sums),
+        (head_scale, own_sums),
+        (proj_bias, all_sums),
+        (down_bias, all_sums),
+    ):
+        owned.append(sums[at : at + piece.size].reshape(piece.shape))
+        at += piece.size
     grad_ada = jnp.einsum("sr,sjc->rjc", silu_half, mod_low, preferred_element_type=F32)
     cond_part = jnp.einsum("sjc,rjc->sr", mod_low, ada_weight, preferred_element_type=F32)
     return_send = jnp.repeat(cond_part.reshape(dp, seqs * part // 128, 128), 2, axis=0)
@@ -1034,23 +1367,22 @@
         5,
     )
     wide = lambda values: values.transpose(1, 0, 2).reshape(own_rows, -1)
-    own_half = lambda values: lax.dynamic_slice_in_dim(values, core * own_len, own_len, 1)
     return (
-        own_half(output),
-        own_half(grad_inputs),
+        output.transpose(1, 0, 2),
+        grad_inputs.transpose(1, 0, 2),
         grad_condition,
         grad_ada,
         grad_ada_bias,
         reduced[:3],
         owned[0],
         owned[1],
-        scale_total,
+        owned[3],
         reduced[3].T,
-        owned[3],
+        owned[4],
         wide(reduced[4 : 4 + ff_chunks]),
         owned[2],
         wide(reduced[4 + ff_chunks :]).T,
-        owned[4],
+        owned[5],
     )
 
 

time: 848 us -> 586 us (0.69)
  matrix products: 221 us -> 1.65 us
  Pallas kernels: 368 us -> 504 us
  other arithmetic: 116 us -> 18.5 us
  local copies, waits for them, and re-layouts: 134 us -> 50.8 us
    pallas_call x0 -> x7, Pallas kernels: none -> 207 us  [run(): pl.pallas_call(kernel, out_shape=[jax.ShapeDtypeStruct(shape, dtype) for...]
    dot_general x16 -> x0, matrix products: 180 us -> none  [the longest x1 25.9 us: fast_device(): jnp.einsum('sqhe,skhe->shqk', grad_attended, values_low, preferred_elemen...]
    pallas_call x1, Pallas kernels: 199 us -> 124 us  [gather_weights(): pl.pallas_call(functools.partial(gather_kernel, grid, chunks), out_shape=...]
    reduce_sum x11 -> x6, other arithmetic: 40.9 us -> 2.43 us  [the longest x1 1.02 us: fast_device(): grad_down_bias = jnp.sum(end_stats[:, 1], axis=0)]
    convert_element_type x3 -> x1, other arithmetic: 34.3 us -> 0.95 us  [fast_device(): ones = (head_at[:, None] == head_at[None, :]).astype(BF16)]
    mul x1 -> x0, matrix products: 21.4 us -> none  [fast_device(): key_unit * jnp.sum(grad_key_unit * key_unit, axis=-1, keepdims=True)]
    unnamed x158 -> x49, local copies, waits for them, and re-layouts: 30.5 us -> 12.5 us
    convert_element_type x4 -> x0, local copies, waits for them, and re-layouts: 17.6 us -> none  [the longest x1 6.59 us: fast_device(): jnp.einsum('sld,jslf->jdf', dm_low, activated, preferred_element_type=F32)]
  transfers between devices with their start and end apart: 4 -> 4, of which waited for: 0 -> 1; matrix products, arithmetic and copies ran while one was open for 8% -> 4% of each run, Pallas kernels for 14% -> 33%
where the time goes in v2:
time: 586 us; the launch traced here: 582 us
  Pallas kernels  504 us (86%)
  local copies, waits for them, and re-layouts  50.8 us (9%)
  other arithmetic  18.5 us (3%)
    pallas_call x7, Pallas kernels, run(): pl.pallas_call(kernel, out_shape=[jax.ShapeDtypeStruct(shape, dtype) for...  207 us
    pallas_call x1, Pallas kernels, gather_weights(): pl.pallas_call(functools.partial(gather_kernel, grid, chunks), out_shape=...  124 us
    pallas_call x1, Pallas kernels, reduce_weights(): pl.pallas_call(functools.partial(reduce_kernel, grid, chunks), out_shape=...  124 us
    pallas_call x4, Pallas kernels, swap(): pl.pallas_call(functools.partial(swap_kernel, count, to_all), out_shape=j...  50.2 us
    unnamed x49, local copies, waits for them, and re-layouts  12.5 us
  transfers between devices with their start and end apart: 4, of which 1 were waited for; matrix products, arithmetic and copies ran while one was open for 4% of the time, Pallas kernels for 33%

profile of v2, /device:TPU:0, one launch (start us, length us, event | category | flops | bytes accessed | tf_op | source)
XLA Modules:
  0.0 582.2 jit_solution(16073644887522404007)
XLA Ops:
  7.3 13.7 %gather_small.1 = bf16[32,32,128]{2,1,0:T(8,128)(2,1)} custom-call(bf16[32,128]{1,0:T(8,128)(2,1)} %bitcast.180), custom_call_target="tpu_custom_call" | custom-call | tf_op jit(solution)/shard_map/gather_small/pallas_call | solution.py:533
  28.7 12.2 %swap_modulation.1 = f32[32,8,128]{2,1,0:T(8,128)} custom-call(f32[32,8,128]{2,1,0:T(8,128)} %bitcast.153), custom_call_target="tpu_custom_call" | custom-call | tf_op jit(solution)/shard_map/swap_modulation/pallas_call | solution.py:533
  44.2 1.5 reshape.312.refs_2_
  45.8 10.1 %split_rows.1 = (bf16[2,352,1024]{2,1,0:T(8,128)(2,1)}, bf16[2,352,1024]{2,1,0:T(8,128)(2,1)}) custom-call(bf16[340,2,1024]{2,1,0:T(2,128)(2,1)} %bitcast.146, bf16[340,2,1024]{2,1,0:T(2,128)(2,1)} %bitcast.147), custom_call_target="tpu_custom_call" | custom-call | tf_op jit(solution)/shard_map/split_rows/pallas_call | solution.py:1122
  56.9 123.8 %gather_weights.1 = (bf16[12,4,2,2,64,512]{5,4,3,2,1,0:T(8,128)(2,1)}, bf16[2,2,352,1024]{3,2,1,0:T(8,128)(2,1)}, bf16[2,2,352,1024]{3,2,1,0:T(8,128)(2,1)}) custom-call(bf16[12,64,512]{2,1,0:T(8,128)(2,1)} %pad_maximum_fusion.1.shard_ref, bf16[2,352,1024]{2,1,0:T(8,128)(2,1)} %get-tuple-element.48.tok_ref, bf16[2,352,1024]{2,1,0:T(8,128)(2,1)} %get-tuple-element.49.grad_ref), custom_call_target="tpu_custom_call" | custom-call | tf_op jit(solution)/shard_map/gather_weights/pallas_call | solution.py:632
  180.7 8.9 %fusion.13 = (bf16[4,4,2,2,64,512]{5,4,3,2,1,0:T(8,128)(2,1)}, bf16[4,4,2,2,64,512]{5,4,3,2,1,0:T(8,128)(2,1)}, bf16[4,4,2,2,64,512]{5,4,3,2,1,0:T(8,128)(2,1)}) fusion(bf16[12,4,2,2,64,512]{5,4,3,2,1,0:T(8,128)(2,1)} %get-tuple-element.52), kind=kLoop, calls=%fused_computation.58 | loop fusion | bytes 25165824 | tf_op jit(solution)/shard_map/slice | solution.py:1239
  190.3 34.6 %attn_forward.1 = (bf16[1408,1024]{1,0:T(8,128)(2,1)}, bf16[8,1408,128]{2,1,0:T(8,128)(2,1)}, bf16[1408,512]{1,0:T(8,128)(2,1)}, bf16[1408,512]{1,0:T(8,128)(2,1...) custom-call(bf16[1408,1024]{1,0:T(8,128)(2,1)} %bitcast.129, ...), custom_call_target="tpu_custom_call" | custom-call | tf_op jit(solution)/shard_map/attn_forward/pallas_call | solution.py:1122
  225.8 4.6 collective-permute-done.refs_2_
  230.4 1.5 copy-done.1
  231.9 45.5 %mlp_forward.1 = (bf16[1408,1024]{1,0:T(8,128)(2,1)}, bf16[1408,1024]{1,0:T(8,128)(2,1)}, bf16[4,1408,512]{2,1,0:T(8,128)(2,1)}, bf16[1408,1024]{1,0:T(8,128)(2,...) custom-call(bf16[1408,1024]{1,0:T(8,128)(2,1)} %bitcast.130, ...), custom_call_target="tpu_custom_call" | custom-call | tf_op jit(solution)/shard_map/mlp_forward/pallas_call | solution.py:1122
  277.4 32.7 %mlp_backward.1 = (bf16[1408,1024]{1,0:T(8,128)(2,1)}, bf16[4,1024,512]{2,1,0:T(8,128)(2,1)}, f32[4,1,512]{2,1,0:T(1,128)}) custom-call(bf16[1408,1024]{1,0:T(8,128)(2,1)} %get-tuple-element.56.refs_0_, bf16[4,1024,512]{2,1,0:T(8,128)(2,1)} %bitcast.134, bf16[4,1408,512]{2,1,0:T(8,128)(2,1)} %get-tuple-element.57.refs_2_, ...), custom_call_target="tpu_custom_call" | custom-call | tf_op jit(solution)/shard_map/mlp_backward/pallas_call | solution.py:1122
  310.3 2.3 slice.177
  312.6 3.9 slice.178
  316.9 1.6 copy-done.2
  318.5 17.3 %middle_backward.1 = (bf16[1408,1024]{1,0:T(8,128)(2,1)}, bf16[1408,512]{1,0:T(8,128)(2,1)}, bf16[1024,512]{1,0:T(8,128)(2,1)}, f32[2,4,1024]{2,1,0:T(4,128)}) custom-call(bf16[1408,1024]{1,0:T(8,128)(2,1)} %bitcast.131, bf16[1408,1024]{1,0:T(8,128)(2,1)} %bitcast.138, bf16[1408,1024]{1,0:T(8,128)(2,1)} %get-tuple-element.54.refs_2_, ...), custom_call_target="tpu_custom_call" | custom-call | tf_op jit(solution)/shard_map/middle_backward/pallas_call | solution.py:1122
  335.8 52.6 %attn_backward.1 = (bf16[3,1024,512]{2,1,0:T(8,128)(2,1)}, bf16[1408,1024]{1,0:T(8,128)(2,1)}, f32[8,512]{1,0:T(8,128)}) custom-call(bf16[1408,1024]{1,0:T(8,128)(2,1)} %get-tuple-element.62.refs_0_, bf16[3,1024,512]{2,1,0:T(8,128)(2,1)} %bitcast.141, bf16[8,1408,128]{2,1,0:T(8,128)(2,1)} %get-tuple-element.63.refs_2_, ...), custom_call_target="tpu_custom_call" | custom-call | tf_op jit(solution)/shard_map/attn_backward/pallas_call | solution.py:1122
  388.8 11.2 %pad_maximum_fusion.full_ref = bf16[12,4,2,2,64,512]{5,4,3,2,1,0:T(8,128)(2,1)} fusion(bf16[4,4,2,2,64,512]{5,4,3,2,1,0:T(8,128)(2,1)} %bitcast.143, bf16[4,4,2,2,64,512]{5,4,3,2,1,0:T(8,128)(2,1)} %bitcast.144, bf16[1,4,2,2,64,512]{5,4,3,2,1,0:T(8,128)(2,1)S(1)} %bitcast.148, bf16[3,4,2,2,64,512]{5,4,3,2,1,0:T(8,128)(2,1)} %bitcast.145), kind=kLoop, calls=%fused_computation | loop fusion | flops 18874368 | bytes 25165824 | tf_op jit(solution)/shard_map/concatenate | solution.py:1364
  399.9 123.8 %reduce_weights.1 = f32[12,64,512]{2,1,0:T(8,128)S(1)} custom-call(bf16[12,4,2,2,64,512]{5,4,3,2,1,0:T(8,128)(2,1)} %pad_maximum_fusion.full_ref), custom_call_target="tpu_custom_call" | custom-call | tf_op jit(solution)/shard_map/reduce_weights/pallas_call | solution.py:769
  529.0 13.9 %finish_rows.1 = (f32[340,2,1024]{2,1,0:T(2,128)}, f32[340,2,1024]{2,1,0:T(2,128)}, f32[2,8,1024]{2,1,0:T(8,128)}) custom-call(bf16[1408,1024]{1,0:T(8,128)(2,1)} %bitcast.132, bf16[1408,1024]{1,0:T(8,128)(2,1)} %bitcast.139, bf16[1408,1024]{1,0:T(8,128)(2,1)} %get-tuple-element.54.refs_2_, bf16[1408,1024]{1,0:T(8,128)(2,1)} %get-tuple-element.55.refs_3_, ...), custom_call_target="tpu_custom_call" | custom-call | tf_op jit(solution)/shard_map/finish_rows/pallas_call | solution.py:1122
  545.6 10.8 %swap_grads.1 = f32[32,16,128]{2,1,0:T(8,128)} custom-call(f32[32,16,128]{2,1,0:T(8,128)} %bitcast.149), custom_call_target="tpu_custom_call" | custom-call | tf_op jit(solution)/shard_map/swap_grads/pallas_call | solution.py:533
  557.4 1.1 reshape.293
  560.7 13.5 %swap_condition.1 = f32[32,16,128]{2,1,0:T(8,128)} custom-call(f32[32,16,128]{2,1,0:T(8,128)} %pad_maximum_fusion.2.src_ref), custom_call_target="tpu_custom_call" | custom-call | tf_op jit(solution)/shard_map/swap_condition/pallas_call | solution.py:533
  574.2 1.1 reshape.298
  575.5 1.2 fusion.1
  (171 shorter events, 37.4 us)
Async XLA Ops:
  0.6 26.9 %copy-start = (bf16[512,6,64]{0,2,1:T(8,128)(2,1)S(1)}, bf16[512,6,64]{0,2,1:T(8,128)(2,1)}, u32[]{:S(2)}) copy-start(bf16[512,6,64]{0,2,1:T(8,128)(2,1)} %param.19) | copy-start | bytes 1179652
  24.7 17.4 %copy-start.4 = (f32[32,1024]{1,0:T(8,128)}, f32[32,1024]{1,0:T(8,128)S(1)}, u32[]{:S(2)}) copy-start(f32[32,1024]{1,0:T(8,128)S(1)} %reshape.303) | copy-start | bytes 393220
  27.5 18.2 %copy-start.6 = (bf16[2048,64]{0,1:T(8,128)(2,1)S(1)}, bf16[2048,64]{0,1:T(8,128)(2,1)}, u32[]{:S(2)}) copy-start(bf16[2048,64]{0,1:T(8,128)(2,1)} %param.29) | copy-start | bytes 786436
  27.5 18.2 %copy-start.7 = (bf16[64,2048]{1,0:T(8,128)(2,1)S(1)}, bf16[64,2048]{1,0:T(8,128)(2,1)}, u32[]{:S(2)}) copy-start(bf16[64,2048]{1,0:T(8,128)(2,1)} %param.27) | copy-start | bytes 786436
  43.8 12.1 %copy-start.8 = (bf16[3,64,512]{2,1,0:T(8,128)(2,1)S(1)}, bf16[3,64,512]{2,1,0:T(8,128)(2,1)}, u32[]{:S(2)}) copy-start(bf16[3,64,512]{2,1,0:T(8,128)(2,1)} %param.21) | copy-start | bytes 589828
  43.8 12.1 %copy-start.9 = (bf16[512,64]{0,1:T(8,128)(2,1)S(1)}, bf16[512,64]{0,1:T(8,128)(2,1)}, u32[]{:S(2)}) copy-start(bf16[512,64]{0,1:T(8,128)(2,1)} %param.25) | copy-start | bytes 196612
  224.9 5.5 collective-permute-start
  230.4 1.5 copy-start.1
  310.1 6.7 %collective-permute-start.2 = (bf16[1408,1024]{1,0:T(8,128)(2,1)}, bf16[1408,1024]{1,0:T(8,128)(2,1)S(1)}, u32[]{:S(2)}, u32[]{:S(2)}) collective-permute-start(bf16[1408,1024]{1,0:T(8,128)(2,1)} %get-tuple-element.59.refs_3_), channel_id=1, source_target_pairs={{0,1},{1,0},{2,3},{3,2},{4,5},{5,4},{6,7},{7,6},{8,9},{9,8},{10,11... | collective-permute-start | bytes 8650760 | tf_op jit(solution)/shard_map/ppermute | solution.py:1134
  316.5 212.4 %collective-permute-start.1 = (bf16[1408,1024]{1,0:T(8,128)(2,1)}, bf16[1408,1024]{1,0:T(8,128)(2,1)}, u32[]{:S(2)}, u32[]{:S(2)}) collective-permute-start(bf16[1408,1024]{1,0:T(8,128)(2,1)} %get-tuple-element.55.refs_3_), channel_id=1, source_target_pairs={{0,1},{1,0},{2,3},{3,2},{4,5},{5,4},{6,7},{7,6},{8,9},{9,8},{10,11... | collective-permute-start | bytes 8650760 | tf_op jit(solution)/shard_map/ppermute | solution.py:1134
  316.9 1.6 copy-start.2
  335.8 52.8 %copy-start.12 = (f32[4,1,512]{2,1,0:T(1,128)S(1)}, f32[4,1,512]{2,1,0:T(1,128)}, u32[]{:S(2)}) copy-start(f32[4,1,512]{2,1,0:T(1,128)} %get-tuple-element.76) | copy-start | bytes 24580
  335.8 53.0 %copy-start.3 = (bf16[1024,512]{1,0:T(8,128)(2,1)S(1)}, bf16[1024,512]{1,0:T(8,128)(2,1)}, u32[]{:S(2)}) copy-start(bf16[1024,512]{1,0:T(8,128)(2,1)} %get-tuple-element.78) | copy-start | bytes 3145732
  388.4 140.6 %collective-permute-start.3 = (bf16[1408,1024]{1,0:T(8,128)(2,1)}, bf16[1408,1024]{1,0:T(8,128)(2,1)}, u32[]{:S(2)}, u32[]{:S(2)}) collective-permute-start(bf16[1408,1024]{1,0:T(8,128)(2,1)} %get-tuple-element.70.refs_6_), channel_id=1, source_target_pairs={{0,1},{1,0},{2,3},{3,2},{4,5},{5,4},{6,7},{7,6},{8,9},{9,8},{10,11... | collective-permute-start | bytes 8650760 | tf_op jit(solution)/shard_map/ppermute | solution.py:1134
  399.9 125.3 %copy-start.10 = (f32[2,4,1024]{2,1,0:T(4,128)S(1)}, f32[2,4,1024]{2,1,0:T(4,128)}, u32[]{:S(2)}) copy-start(f32[2,4,1024]{2,1,0:T(4,128)} %get-tuple-element.73) | copy-start | bytes 98308
  544.8 30.7 %copy-start.5 = (f32[32,1024]{1,0:T(8,128)S(1)}, f32[32,1024]{1,0:T(8,128)}, u32[]{:S(2)}) copy-start(f32[32,1024]{1,0:T(8,128)} %copy-done.4) | copy-start | bytes 393220
  556.4 22.5 %copy-start.11 = (bf16[2,1024]{1,0:T(2,128)(2,1)S(1)}, bf16[2,1024]{1,0:T(2,128)(2,1)}, u32[]{:S(2)}) copy-start(bf16[2,1024]{1,0:T(2,128)(2,1)} %param.17) | copy-start | bytes 12292

commit v3 on v2

--- a/solution.py
+++ b/solution.py
@@ -544,112 +544,434 @@
         name=name,
     )(values)
 
-
-def gather_kernel(
-    grid, chunks, shard_ref, tok_ref, grad_ref, full_ref, tok_out, grad_out, local_sem, z_send, z_recv, p_send, p_recv, t_send, t_recv
+def greet(peers):
+    barrier = pltpu.get_barrier_semaphore()
+    for peer in peers:
+        pl.semaphore_signal(barrier, inc=1, device_id=peer, device_id_type=MESH_ID)
+    pl.semaphore_wait(barrier, len(peers))
+
+
+def forward_kernel(
+    grid,
+    sizes,
+    chunk_counts,
+    shard,
+    tok,
+    grad_in,
+    mod,
+    query_spare,
+    key_spare,
+    query_bias,
+    value_bias,
+    key_scale,
+    up_bias,
+    ones,
+    full,
+    x_out,
+    grad_out,
+    mixed_out,
+    qaug_out,
+    kv_out,
+    inverse_out,
+    att_out,
+    branch_out,
+    mlp_out,
+    slope_out,
+    dm_out,
+    grad_down_out,
+    mlp_own,
+    mlp_other,
+    x,
+    dm,
+    mixed,
+    part,
+    other,
+    turned,
+    qaug,
+    kv,
+    inverses,
+    att,
+    w,
+    slope,
+    act,
+    grad_down,
+    local_sem,
+    z_send,
+    z_recv,
+    p_send,
+    p_recv,
+    t_send,
+    t_recv,
+    load_sem,
+    save_sem,
 ):
     nz, ny, nx = grid
     half = nz // 2
-    z, y, x, core = coords(grid)
-
-    def dev(z_at, y_at, x_at):
-        return ((z_at * ny + y_at) * nx + x_at, core)
-
-    x_peer = dev(z, y, 1 - x)
-    y_peer = dev(z, 1 - y, x)
+    seqs, pad = sizes
+    chunks = shard.shape[0]
+    ff_chunks = chunk_counts
+    z, y, x_at, core = coords(grid)
+    width = x.shape[1]
+    part_width = att.shape[1]
+    pairs = part_width // 128
+    blocks = seqs * 2
+    length = tok.shape[0]
+
+    def dev(z_to, y_to, x_to):
+        return ((z_to * ny + y_to) * nx + x_to, core)
+
+    x_peer = dev(z, y, 1 - x_at)
+    y_peer = dev(z, 1 - y, x_at)
     sibling = (place()[0], 1 - core)
-    greet_all(nz * ny * nx * 2)
-    swaps = []
-    for i, (src, dst) in enumerate(((tok_ref, tok_out), (grad_ref, grad_out))):
-        own = pltpu.make_async_copy(src, dst.at[:, core], local_sem.at[chunks + i])
-        own.start()
-        copy = remote(src, dst.at[:, core], t_send.at[i], t_recv.at[i], sibling)
-        copy.start()
-        swaps += [own, copy]
+    greet([x_peer, y_peer, sibling] + [dev((z + k) % nz, y, x_at) for k in range(1, nz)])
 
     def own_copy(c):
-        return pltpu.make_async_copy(shard_ref.at[c], full_ref.at[c, z, y, x], local_sem.at[c])
+        return pltpu.make_async_copy(shard.at[c], full.at[c, z, y, x_at], local_sem.at[c])
 
     def z_copies(c):
         return [
             remote(
-                shard_ref.at[c],
-                full_ref.at[c, z, y, x],
+                shard.at[c],
+                full.at[c, z, y, x_at],
                 z_send.at[c, k - 1],
                 z_recv.at[c, k - 1],
-                dev((z + k) % nz, y, x),
+                dev((z + k) % nz, y, x_at),
             )
             for k in range(1, nz)
         ]
 
     def first_copies(c):
-        low = full_ref.at[c, pl.ds(0, half), y, x]
-        high = full_ref.at[c, pl.ds(half, half), y, x]
+        low = full.at[c, pl.ds(0, half), y, x_at]
+        high = full.at[c, pl.ds(half, half), y, x_at]
         return [
             remote(low, low, p_send.at[c, 0], p_recv.at[c, 0], x_peer),
             remote(high, high, p_send.at[c, 1], p_recv.at[c, 1], y_peer),
         ]
 
     def second_copies(c):
-        low = full_ref.at[c, pl.ds(0, half), y]
-        high = full_ref.at[c, pl.ds(half, half), :, x]
+        low = full.at[c, pl.ds(0, half), y]
+        high = full.at[c, pl.ds(half, half), :, x_at]
         return [
             remote(low, low, p_send.at[c, 2], p_recv.at[c, 2], y_peer),
             remote(high, high, p_send.at[c, 3], p_recv.at[c, 3], x_peer),
         ]
 
     ahead = 2
-    for t in range(-ahead, chunks + 2):
-        if 0 <= t + ahead < chunks:
-            c = t + ahead
-            own_copy(c).start()
-            for copy in z_copies(c):
-                copy.start()
-        if 0 <= t < chunks:
-            own_copy(t).wait()
-            for copy in z_copies(t):
-                copy.wait_recv()
-            for copy in first_copies(t):
-                copy.start()
-        if 0 <= t - 1 < chunks:
-            for copy in first_copies(t - 1):
-                copy.wait_recv()
-            for copy in second_copies(t - 1):
-                copy.start()
-        if 0 <= t - 2 < chunks:
-            for copy in second_copies(t - 2):
-                copy.wait_recv()
+    progress = [-ahead]
+
+    def advance(upto):
+        while progress[0] <= upto:
+            t = progress[0]
+            if 0 <= t + ahead < chunks:
+                own_copy(t + ahead).start()
+                for copy in z_copies(t + ahead):
+                    copy.start()
+            if 0 <= t < chunks:
+                own_copy(t).wait()
+                for copy in z_copies(t):
+                    copy.wait_recv()
+                for copy in first_copies(t):
+                    copy.start()
+            if 0 <= t - 1 < chunks:
+                for copy in first_copies(t - 1):
+                    copy.wait_recv()
+                for copy in second_copies(t - 1):
+                    copy.start()
+            if 0 <= t - 2 < chunks:
+                for copy in second_copies(t - 2):
+                    copy.wait_recv()
+            progress[0] += 1
+
+    def load(c):
+        return pltpu.make_async_copy(full.at[c], w.at[c % 4], load_sem.at[c])
+
+    def weight(c):
+        return w[c % 4].reshape(width, part_width)
+
+    saves = []
+
+    def save(src, dst):
+        copy = pltpu.make_async_copy(src, dst, save_sem.at[len(saves)])
+        copy.start()
+        saves.append(copy)
+        return copy
+
+    def block_rows(a):
+        return pl.ds(pl.multiple_of(a * pad, 16), pad)
+
+    advance(-1)
+
+    def own_rows(s, which):
+        return block_rows(s * 2 + which)
+
+    swaps = []
+    for i, (src, dst) in enumerate(((tok, x), (grad_in, dm))):
+        for s in range(seqs):
+            values = src[:, s, :].astype(F32).astype(BF16)
+            start = pl.multiple_of((s * 2 + core) * pad, 16)
+            dst[pl.ds(start + length // 16 * 16, pad - length // 16 * 16), :] = jnp.zeros(
+                (pad - length // 16 * 16, width), BF16
+            )
+            dst[pl.ds(start, length), :] = values
+            piece = dst.at[own_rows(s, core), :]
+            copy = remote(piece, piece, t_send.at[i * seqs + s], t_recv.at[i * seqs + s], sibling)
+            copy.start()
+            swaps.append(copy)
+    for copy in swaps[:seqs]:
+        copy.wait()
+    save(x, x_out)
+
+    def mix_attn(a, rows):
+        s = a // 2
+        normed, unused = normalize(x[rows, :].astype(F32))
+        mixed[rows, :] = (normed * (1.0 + mod[s, 2:3, :]) + mod[s, 4:5, :]).astype(BF16)
+
+    for_blocks(blocks, pad, mix_attn)
+    mixed_saved = save(mixed, mixed_out)
+    advance(0)
+    for copy in swaps[seqs:]:
+        copy.wait()
+    grad_saved = save(dm, grad_out)
+    advance(1)
+    grad_saved.wait()
+
+    def scale_grad(a, rows):
+        dm[rows, :] = (dm[rows, :].astype(F32) * mod[a // 2, 1:2, :]).astype(BF16)
+
+    for_blocks(blocks, pad, scale_grad)
+    save(dm, dm_out)
+    advance(2)
+    load(0).start()
+    transpose_into(turned, dm)
+    advance(3)
+    load(1).start()
+
+    load(0).wait()
+
+    def project_q(a, rows):
+        first, unused = lane_code(pad)
+        q_spare = query_spare[rows, :].astype(F32)
+        values = dot(mixed[rows, :], weight(0)) + query_bias[...]
+        inv = lax.rsqrt(dot((values * values).astype(BF16), ones[...]) + HEAD_EPS)
+        inverses[rows, 0:part_width] = inv.astype(BF16)
+        values = values * inv * key_scale[...]
+        for p in range(pairs):
+            piece = values[:, p * 128 : p * 128 + 128]
+            qaug[2 * p, rows, :] = jnp.where(first, piece, q_spare).astype(BF16)
+            qaug[2 * p + 1, rows, :] = jnp.where(first, q_spare, piece).astype(BF16)
+
+    for_blocks(blocks, pad, project_q)
+    advance(4)
+    load(2).start()
+    load(1).wait()
+
+    def project_k(a, rows):
+        values = dot(mixed[rows, :], weight(1))
+        inv = lax.rsqrt(dot((values * values).astype(BF16), ones[...]) + HEAD_EPS)
+        inverses[rows, part_width : 2 * part_width] = inv.astype(BF16)
+        kv[rows, 0:part_width] = (values * inv).astype(BF16)
+
+    for_blocks(blocks, pad, project_k)
+    save(inverses, inverse_out)
+    load(2).wait()
+
+    def project_v(a, rows):
+        kv[rows, part_width : 2 * part_width] = (
+            dot(mixed[rows, :], weight(2)) + value_bias[...]
+        ).astype(BF16)
+
+    for_blocks(blocks, pad, project_v)
+    save(kv, kv_out)
+    advance(5)
+    load(3).start()
+
+    def attend(i, carry):
+        p = i // blocks
+        block = i % blocks
+        rows = block_rows(block)
+        all_rows = pl.ds(pl.multiple_of((block // 2) * 2 * pad, 16), 2 * pad)
+        at = pl.multiple_of(p * 128, 128)
+        first, code = lane_code(pad)
+        k_sides = both_heads(kv[all_rows, pl.ds(at, 128)], key_spare[all_rows, :])
+        v_sides = both_heads(kv[all_rows, pl.ds(at + part_width, 128)], 1.0)
+        outs = []
+        for side in range(2):
+            h = 2 * p + side
+            q = qaug[h, rows, :]
+            prob = jnp.exp2(dot_nt(q, k_sides[side])).astype(BF16)
+            o = dot(prob, v_sides[side])
+            outs.append(o / pltpu.roll(o, 64, 1))
+            norm = -jnp.log2(o)
+            high = norm.astype(BF16)
+            rest = norm - high.astype(F32)
+            middle = rest.astype(BF16)
+            low = (rest - middle.astype(F32)).astype(BF16)
+            spare = jnp.logical_not(first) if side == 0 else first
+            q = q.astype(F32)
+            for where, piece in enumerate((high, middle, low)):
+                q = jnp.where(spare & (code == SCALES + where), piece.astype(F32), q)
+            qaug[h, rows, :] = q.astype(BF16)
+        att[rows, pl.ds(at, 128)] = jnp.where(first, outs[0], outs[1]).astype(BF16)
+        return carry
+
+    count = pairs * blocks
+    for quarter in range(2):
+        lax.fori_loop(quarter * count // 2, (quarter + 1) * count // 2, attend, 0)
+        advance(6 + quarter)
+        load(4 + quarter).start()
+    save(qaug, qaug_out)
+    save(att, att_out)
+    load(3).wait()
+    part_copies = []
+    for a in range(blocks):
+        rows = block_rows(a)
+        part[rows, :] = dot_nt(att[rows, :], weight(3)).astype(BF16)
+        copy = remote(
+            part.at[rows, :], other.at[rows, :], t_send.at[2 * seqs + a], t_recv.at[2 * seqs + a], sibling
+        )
+        copy.start()
+        part_copies.append(copy)
+    mixed_saved.wait()
+    mlp = mixed
+    for a in range(blocks):
+        rows = block_rows(a)
+        s = a // 2
+        part_copies[a].wait()
+        b = part[rows, :].astype(F32) + other[rows, :].astype(F32) + mod[s, 6:7, :]
+        other[rows, :] = b.astype(BF16)
+        normed, unused = normalize(x[rows, :].astype(F32) + mod[s, 0:1, :] * b)
+        mlp[rows, :] = (normed * (1.0 + mod[s, 3:4, :]) + mod[s, 5:6, :]).astype(BF16)
+    save(other, branch_out)
+    save(mlp, mlp_out)
+    for c in range(ff_chunks):
+        advance(6 + c)
+        if c >= 2:
+            load(4 + c).start()
+        load(4 + c).wait()
+
+        def raise_rows(a, rows):
+            h = dot(mlp[rows, :], weight(4 + c)) + up_bias[c]
+            square = h * h
+            t = jnp.tanh(h * (GELU_COEF + GELU_COEF * GELU_CUBE * square))
+            act[c, rows, :] = (0.5 * h * (1.0 + t)).astype(BF16)
+            slope[c, rows, :] = (
+                0.5 * (1.0 + t)
+                + h * (1.0 - t * t) * (0.5 * GELU_COEF + 1.5 * GELU_COEF * GELU_CUBE * square)
+            ).astype(BF16)
+
+        for_blocks(blocks, pad, raise_rows)
+        save(slope.at[c], slope_out.at[c])
+    down_saved = []
+    for c in range(ff_chunks):
+        advance(10 + c)
+        load(8 + c).start()
+        if c >= 2:
+            down_saved[c - 2].wait()
+        grad_down[c % 2] = dot(turned[...], act[c]).astype(BF16).reshape(grad_down.shape[1:])
+        down_saved.append(save(grad_down.at[c % 2], grad_down_out.at[c]))
+    for c in range(ff_chunks):
+        load(8 + c).wait()
+    end_copies = []
+    for step in range(blocks):
+        s = step % seqs
+        which = 1 - core if step < seqs else core
+        rows = own_rows(s, which)
+        total = dot_nt(act[0, rows, :], weight(8))
+        for c in range(1, ff_chunks):
+            total = total + dot_nt(act[c, rows, :], weight(8 + c))
+        part[rows, :] = total.astype(BF16)
+        if step < seqs:
+            copy = remote(
+                part.at[rows, :],
+                mlp_other.at[s],
+                t_send.at[2 * seqs + blocks + s],
+                t_recv.at[2 * seqs + blocks + s],
+                sibling,
+            )
+            copy.start()
+            end_copies.append(copy)
+        else:
+            save(part.at[rows, :], mlp_own.at[s])
+    for copy in end_copies:
+        copy.wait()
+    done = [mixed_saved, grad_saved] + down_saved[:-2]
+    for copy in saves:
+        if all(copy is not other_copy for other_copy in done):
+            copy.wait()
     for c in range(chunks):
         for copy in z_copies(c) + first_copies(c) + second_copies(c):
             copy.wait_send()
-    for copy in swaps:
-        copy.wait()
-
-
-def gather_weights(grid, shard, tok, grad, collective_id):
+
+
+def forward_pass(grid, sizes, shard, tok, grad_in, mod, query_spare, key_spare, query_bias, value_bias, key_scale, up_bias, ones, collective_id):
     nz, ny, nx = grid
-    chunks = shard.shape[0]
+    seqs, pad = sizes
+    chunks, own_rows, part = shard.shape
+    ff_chunks = up_bias.shape[0]
+    width = tok.shape[2]
+    total = seqs * 2 * pad
+    heads = part // 64
+    wide = ((total, width), BF16)
+    narrow = ((total, part), BF16)
+    chunk = (nz, ny, nx, own_rows, part)
+    outs = [
+        ((chunks,) + chunk, BF16),
+        wide,
+        wide,
+        wide,
+        ((heads, total, 128), BF16),
+        wide,
+        wide,
+        narrow,
+        wide,
+        wide,
+        ((ff_chunks, total, part), BF16),
+        wide,
+        ((ff_chunks,) + chunk, BF16),
+        ((seqs, pad, width), BF16),
+        ((seqs, pad, width), BF16),
+    ]
+    scratch = [
+        wide,
+        wide,
+        wide,
+        wide,
+        wide,
+        ((width, total), BF16),
+        ((heads, total, 128), BF16),
+        wide,
+        wide,
+        narrow,
+        ((4,) + chunk, BF16),
+        ((ff_chunks, total, part), BF16),
+        ((ff_chunks, total, part), BF16),
+        ((2,) + chunk, BF16),
+    ]
+    swaps = 3 * seqs + seqs * 2
+    vmem = pl.BlockSpec(memory_space=pltpu.VMEM)
+    hbm = pl.BlockSpec(memory_space=ANY)
     return pl.pallas_call(
-        functools.partial(gather_kernel, grid, chunks),
-        out_shape=[
-            jax.ShapeDtypeStruct((chunks, nz, ny, nx) + shard.shape[1:], shard.dtype),
-            jax.ShapeDtypeStruct((tok.shape[0], 2) + tok.shape[1:], tok.dtype),
-            jax.ShapeDtypeStruct((grad.shape[0], 2) + grad.shape[1:], grad.dtype),
-        ],
-        in_specs=[pl.BlockSpec(memory_space=ANY)] + [pl.BlockSpec(memory_space=pltpu.VMEM)] * 2,
-        out_specs=[pl.BlockSpec(memory_space=ANY)] * 3,
-        scratch_shapes=[
-            pltpu.SemaphoreType.DMA((chunks + 2,)),
+        functools.partial(forward_kernel, grid, sizes, ff_chunks),
+        out_shape=[jax.ShapeDtypeStruct(shape, dtype) for shape, dtype in outs],
+        in_specs=[hbm] + [vmem] * 10,
+        out_specs=[hbm] * len(outs),
+        scratch_shapes=[pltpu.VMEM(shape, dtype) for shape, dtype in scratch]
+        + [
+            pltpu.SemaphoreType.DMA((chunks,)),
             pltpu.SemaphoreType.DMA((chunks, nz - 1)),
             pltpu.SemaphoreType.DMA((chunks, nz - 1)),
             pltpu.SemaphoreType.DMA((chunks, 4)),
             pltpu.SemaphoreType.DMA((chunks, 4)),
-            pltpu.SemaphoreType.DMA((2,)),
-            pltpu.SemaphoreType.DMA((2,)),
+            pltpu.SemaphoreType.DMA((swaps,)),
+            pltpu.SemaphoreType.DMA((swaps,)),
+            pltpu.SemaphoreType.DMA((chunks,)),
+            pltpu.SemaphoreType.DMA((24,)),
         ],
-        compiler_params=pltpu.CompilerParams(collective_id=collective_id, has_side_effects=True),
-        name="gather_weights",
-    )(shard, tok, grad)
+        compiler_params=pltpu.CompilerParams(
+            collective_id=collective_id, has_side_effects=True, vmem_limit_bytes=60 * 2**20
+        ),
+        name="forward_pass",
+    )(shard, tok, grad_in, mod, query_spare, key_spare, query_bias, value_bias, key_scale, up_bias, ones)
 
 
 def reduce_kernel(
@@ -842,123 +1164,6 @@
     lax.fori_loop(0, count, step, 0)
 
 
-def split_kernel(tok_ref, grad_ref, tok_out, grad_out):
-    length = tok_ref.shape[0]
-    for src, dst in ((tok_ref, tok_out), (grad_ref, grad_out)):
-        dst[...] = jnp.zeros_like(dst)
-        for s in range(src.shape[1]):
-            dst[s, 0:length] = src[:, s, :].astype(F32).astype(BF16)
-
-
-def attn_forward(sizes, x, mod, scale, w, query_bias, value_bias, key_scale, ones, mixed, qaug, keys, values_low, key_spare, rq, rk, att, part):
-    seqs, pad = sizes
-    width = x.shape[1]
-    pairs = att.shape[1] // 128
-
-    def project(a, rows):
-        s = a // 2
-        normed, unused = normalize(x[rows, :].astype(F32))
-        m = (normed * (1.0 + mod[s, 2:3, :]) + mod[s, 4:5, :]).astype(BF16)
-        mixed[rows, :] = m
-        first, code = lane_code(pad)
-        level = scale[rows, :]
-        q_spare = jnp.where(code == level, 1.0, 0.0)
-        k_spare = jnp.where(
-            code < SCALES, jnp.where(level > code, MASK, 0.0), jnp.where(code < SCALES + 3, 1.0, 0.0)
-        )
-        key_spare[rows, :] = k_spare.astype(BF16)
-        values = dot(m, w[0]) + query_bias[...]
-        inv = lax.rsqrt(dot((values * values).astype(BF16), ones[...]) + HEAD_EPS)
-        rq[rows, :] = inv.astype(BF16)
-        values = values * inv * key_scale[...]
-        for p in range(pairs):
-            piece = values[:, p * 128 : p * 128 + 128]
-            qaug[2 * p, rows, :] = jnp.where(first, piece, q_spare).astype(BF16)
-            qaug[2 * p + 1, rows, :] = jnp.where(first, q_spare, piece).astype(BF16)
-        values = dot(m, w[1])
-        inv = lax.rsqrt(dot((values * values).astype(BF16), ones[...]) + HEAD_EPS)
-        rk[rows, :] = inv.astype(BF16)
-        keys[rows, :] = (values * inv).astype(BF16)
-        values_low[rows, :] = (dot(m, w[2]) + value_bias[...]).astype(BF16)
-
-    for_blocks(seqs * 2, pad, project)
-
-    def attend(i, carry):
-        p = i // (seqs * 2)
-        block = i % (seqs * 2)
-        s = block // 2
-        rows = pl.ds(pl.multiple_of(block * pad, 16), pad)
-        all_rows = pl.ds(pl.multiple_of(s * 2 * pad, 16), 2 * pad)
-        lanes = pl.ds(pl.multiple_of(p * 128, 128), 128)
-        first, code = lane_code(pad)
-        k_sides = both_heads(keys[all_rows, lanes], key_spare[all_rows, :])
-        v_sides = both_heads(values_low[all_rows, lanes], 1.0)
-        outs = []
-        for side in range(2):
-            h = 2 * p + side
-            q = qaug[h, rows, :]
-            prob = jnp.exp2(dot_nt(q, k_sides[side])).astype(BF16)
-            o = dot(prob, v_sides[side])
-            outs.append(o / pltpu.roll(o, 64, 1))
-            norm = -jnp.log2(o)
-            high = norm.astype(BF16)
-            rest = norm - high.astype(F32)
-            middle = rest.astype(BF16)
-            low = (rest - middle.astype(F32)).astype(BF16)
-            spare = jnp.logical_not(first) if side == 0 else first
-            q = q.astype(F32)
-            for at, piece in enumerate((high, middle, low)):
-                q = jnp.where(spare & (code == SCALES + at), piece.astype(F32), q)
-            qaug[h, rows, :] = q.astype(BF16)
-        att[rows, lanes] = jnp.where(first, outs[0], outs[1]).astype(BF16)
-        return carry
-
-    lax.fori_loop(0, pairs * seqs * 2, attend, 0)
-
-    def out_project(a, rows):
-        part[rows, :] = dot_nt(att[rows, :], w[3]).astype(BF16)
-
-    for_blocks(seqs * 2, pad, out_project)
-
-
-def mlp_forward(sizes, x, part, part_other, grad, mod, up, up_bias, down, branch, mlp, slope, mlp_part, dm, grad_down, act, turned):
-    seqs, pad = sizes
-    chunks = up.shape[0]
-
-    def mix(a, rows):
-        s = a // 2
-        b = part[rows, :].astype(F32) + part_other[rows, :].astype(F32) + mod[s, 6:7, :]
-        branch[rows, :] = b.astype(BF16)
-        normed, unused = normalize(x[rows, :].astype(F32) + mod[s, 0:1, :] * b)
-        mlp[rows, :] = (normed * (1.0 + mod[s, 3:4, :]) + mod[s, 5:6, :]).astype(BF16)
-        dm[rows, :] = (grad[rows, :].astype(F32) * mod[s, 1:2, :]).astype(BF16)
-
-    for_blocks(seqs * 2, pad, mix)
-    transpose_into(turned, dm)
-    for c in range(chunks):
-
-        def raise_rows(a, rows):
-            h = dot(mlp[rows, :], up[c]) + up_bias[c]
-            square = h * h
-            t = jnp.tanh(h * (GELU_COEF + GELU_COEF * GELU_CUBE * square))
-            act[c, rows, :] = (0.5 * h * (1.0 + t)).astype(BF16)
-            slope[c, rows, :] = (
-                0.5 * (1.0 + t)
-                + h * (1.0 - t * t) * (0.5 * GELU_COEF + 1.5 * GELU_COEF * GELU_CUBE * square)
-            ).astype(BF16)
-
-        for_blocks(seqs * 2, pad, raise_rows)
-        grad_down[c] = dot(turned[...], act[c]).astype(BF16)
-
-    def lower(a, rows):
-        total = dot_nt(act[0, rows, :], down[0])
-        for c in range(1, chunks):
-            total = total + dot_nt(act[c, rows, :], down[c])
-        mlp_part[rows, :] = total.astype(BF16)
-
-    for_blocks(seqs * 2, pad, lower)
-
-
 def mlp_backward(sizes, dm, down, slope, mlp, up, grad_part, grad_up, bias_sum, turned, low):
     seqs, pad = sizes
     chunks = up.shape[0]
@@ -1009,10 +1214,11 @@
 
 
 def attn_backward(
-    sizes, mixed, w, qaug, keys, values_low, key_spare, grad_att, rq, rk, key_scale, ones, grad_qkv, grad_part, bias_sum, low, turned
+    sizes, mixed, w, qaug, kv, key_spare, grad_att, inverses, key_scale, ones, grad_qkv, grad_part, bias_sum, low, turned
 ):
     seqs, pad = sizes
-    pairs = rq.shape[1] // 128
+    part_width = grad_att.shape[1]
+    pairs = part_width // 128
     bias_sum[...] = jnp.zeros_like(bias_sum)
     transpose_into(turned, mixed)
     ln2 = 0.6931471805599453
@@ -1022,11 +1228,12 @@
         s = i % seqs
         start = pl.multiple_of(s * 2 * pad, 16)
         all_rows = pl.ds(start, 2 * pad)
-        lanes = pl.ds(pl.multiple_of(p * 128, 128), 128)
+        at = pl.multiple_of(p * 128, 128)
+        lanes = pl.ds(at, 128)
         first, code = lane_code(pad)
         first_all, unused = lane_code(2 * pad)
-        k_sides = both_heads(keys[all_rows, lanes], key_spare[all_rows, :])
-        v_sides = both_heads(values_low[all_rows, lanes], 0.0)
+        k_sides = both_heads(kv[all_rows, lanes], key_spare[all_rows, :])
+        v_sides = both_heads(kv[all_rows, pl.ds(at + part_width, 128)], 0.0)
         g_sides = both_heads(grad_att[all_rows, lanes], 0.0)
         grads_k, grads_v, grads_q = [], [], [[], []]
         for side in range(2):
@@ -1074,12 +1281,12 @@
         unit = unit / scale
         f = low[0, rows, :].astype(F32) * (scale * ln2)
         product = f * unit
-        gq = rq[rows, :].astype(F32) * (f - unit * dot(product.astype(BF16), ones[...]))
+        gq = inverses[rows, 0:part_width].astype(F32) * (f - unit * dot(product.astype(BF16), ones[...]))
         bias_sum[0:1, :] += column_sum(gq)
         low[0, rows, :] = gq.astype(BF16)
-        unit = keys[rows, :].astype(F32)
+        unit = kv[rows, 0:part_width].astype(F32)
         f = low[1, rows, :].astype(F32)
-        gk = rk[rows, :].astype(F32) * (f - unit * dot((f * unit).astype(BF16), ones[...]))
+        gk = inverses[rows, part_width : 2 * part_width].astype(F32) * (f - unit * dot((f * unit).astype(BF16), ones[...]))
         low[1, rows, :] = gk.astype(BF16)
         bias_sum[1:2, :] += column_sum(low[2, rows, :].astype(F32))
         total = dot_nt(low[0, rows, :], w[0])
@@ -1098,7 +1305,7 @@
     length = output.shape[0]
     for s in range(seqs):
         rows = pl.ds(pl.multiple_of((s * 2 + core) * pad, 16), pad)
-        b = mlp_part[rows, :].astype(F32) + mlp_other[rows, :].astype(F32) + mod[s, 7:8, :]
+        b = mlp_part[s].astype(F32) + mlp_other[s].astype(F32) + mod[s, 7:8, :]
         g = grad[rows, :].astype(F32)
         xs = x[rows, :].astype(F32)
         middle = xs + mod[s, 0:1, :] * branch[rows, :].astype(F32)
@@ -1182,18 +1389,6 @@
     pad = -(-own_len // 16) * 16
     total = seqs * 2 * pad
     sizes = (seqs, pad)
-    tok_own, grad_own = run(
-        lambda unused, *refs: split_kernel(*refs),
-        sizes,
-        (tokens.transpose(1, 0, 2), out_grad.transpose(1, 0, 2)),
-        [((seqs, pad, width), BF16)] * 2,
-        name="split_rows",
-    )
-    full, x, grad = gather_weights(grid, shard, tok_own, grad_own, 0)
-    full = full.reshape(-1, width, part)
-    x = x.reshape(total, width)
-    grad = grad.reshape(total, width)
-
     pieces = [condition, ada_bias, query_bias, value_bias, proj_bias, up_bias, down_bias]
     small = jnp.concatenate([piece.reshape(1, -1) for piece in pieces], axis=1)
     small_rows = -(-small.shape[1] // (16 * 128)) * 16
@@ -1229,34 +1424,57 @@
     level = jnp.pad(
         scale_index.reshape(seqs, 2, own_len), ((0, 0), (0, 0), (0, pad - own_len)), constant_values=100
     ).reshape(total, 1)
+    code = jnp.arange(128)[None] % 64
+    query_spare = jnp.where(code == level, 1.0, 0.0).astype(BF16)
+    key_spare = jnp.where(
+        code < SCALES, jnp.where(level > code, MASK, 0.0), jnp.where(code < SCALES + 3, 1.0, 0.0)
+    ).astype(BF16)
     key_scale = jnp.repeat(jnp.exp(head_scale) * 1.4426950408889634, head_dim).reshape(1, part)
     head_at = jnp.arange(part) // head_dim
     ones = (head_at[:, None] == head_at[None, :]).astype(BF16)
     wide_rows = ((total, width), BF16)
     part_rows = ((total, part), BF16)
     head_rows = ((heads, total, 2 * head_dim), BF16)
-    up = full[4 : 4 + ff_chunks]
-    down = full[4 + ff_chunks :]
     ff_rows = ((ff_chunks, total, part), BF16)
     weight_rows = ((width, part), BF16)
     turned = ((width, total), BF16)
 
-    mixed, qaug, keys, values_low, key_spare, rq, rk, att, attn_part = run(
-        attn_forward,
+    (
+        full,
+        x,
+        grad,
+        mixed,
+        qaug,
+        kv,
+        inverses,
+        att,
+        branch,
+        mlp,
+        slope,
+        dm,
+        grad_down,
+        mlp_part,
+        mlp_other,
+    ) = forward_pass(
+        grid,
         sizes,
-        (x, mod, level, full[:4], query_bias_own[None], value_bias_own[None], key_scale, ones),
-        [wide_rows, head_rows, part_rows, part_rows, ((total, 128), BF16), part_rows, part_rows, part_rows, wide_rows],
-        name="attn_forward",
-    )
-    branch, mlp, slope, mlp_part, dm, grad_down = run(
-        mlp_forward,
-        sizes,
-        (x, attn_part, sibling_swap(attn_part), grad, mod, up, up_bias_own.reshape(ff_chunks, 1, part), down),
-        [wide_rows, wide_rows, ff_rows, wide_rows, wide_rows, ((ff_chunks, width, part), BF16)],
-        [ff_rows, turned],
-        name="mlp_forward",
-    )
-    mlp_other = sibling_swap(mlp_part)
+        shard,
+        tokens.transpose(1, 0, 2),
+        out_grad.transpose(1, 0, 2),
+        mod,
+        query_spare,
+        key_spare,
+        query_bias_own[None],
+        value_bias_own[None],
+        key_scale,
+        up_bias_own.reshape(ff_chunks, 1, part),
+        ones,
+        0,
+    )
+    full = full.reshape(-1, width, part)
+    grad_down = grad_down.reshape(-1, width, part)
+    up = full[4 : 4 + ff_chunks]
+    down = full[4 + ff_chunks :]
     gm_part, grad_up, up_sum = run(
         mlp_backward,
         sizes,
@@ -1276,7 +1494,7 @@
     grad_qkv, ga_part, qkv_sum = run(
         attn_backward,
         sizes,
-        (mixed, full[:3], qaug, keys, values_low, key_spare, grad_att, rq, rk, key_scale, ones),
+        (mixed, full[:3], qaug, kv, key_spare, grad_att, inverses, key_scale, ones),
         [((3, width, part), BF16), wide_rows, ((8, part), F32)],
         [((3, total, part), BF16), turned],
         name="attn_backward",

time: 586 us -> 504 us (0.86)
  Pallas kernels: 504 us -> 430 us
  local copies, waits for them, and re-layouts: 50.8 us -> 44.9 us
    pallas_call x7 -> x4, Pallas kernels: 207 us -> 115 us  [run(): pl.pallas_call(kernel, out_shape=[jax.ShapeDtypeStruct(shape, dtype) for...]
    pallas_call x1, Pallas kernels: 124 us -> 141 us  [forward_pass(): pl.pallas_call(functools.partial(forward_kernel, grid, sizes, ff_chunks),...]
    unnamed x49 -> x43, local copies, waits for them, and re-layouts: 12.5 us -> 11 us
  transfers between devices with their start and end apart: 4 -> 2, of which waited for: 1 -> 0; matrix products, arithmetic and copies ran while one was open for 4% -> 5% of each run, Pallas kernels for 33% -> 25%
where the time goes in v3:
time: 504 us; the launch traced here: 499 us
  Pallas kernels  430 us (85%)
  local copies, waits for them, and re-layouts  44.9 us (9%)
  other arithmetic  20.9 us (4%)
    pallas_call x1, Pallas kernels, forward_pass(): pl.pallas_call(functools.partial(forward_kernel, grid, sizes, ff_chunks),...  141 us
    pallas_call x1, Pallas kernels, reduce_weights(): pl.pallas_call(functools.partial(reduce_kernel, grid, chunks), out_shape=...  123 us
    pallas_call x4, Pallas kernels, run(): pl.pallas_call(kernel, out_shape=[jax.ShapeDtypeStruct(shape, dtype) for...  115 us
    pallas_call x4, Pallas kernels, swap(): pl.pallas_call(functools.partial(swap_kernel, count, to_all), out_shape=j...  50.3 us
    concatenate x1, other arithmetic, fast_device(): jnp.concatenate([grad_qkv, grad_proj[None], grad_up, grad_down], axis=0)  11.5 us
    unnamed x43, local copies, waits for them, and re-layouts  11 us
  transfers between devices with their start and end apart: 2, of which 0 were waited for; matrix products, arithmetic and copies ran while one was open for 5% of the time, Pallas kernels for 25%

profile of v3, /device:TPU:0, one launch (start us, length us, event | category | flops | bytes accessed | tf_op | source)
XLA Modules:
  0.0 499.5 jit_solution(6298156503709849403)
XLA Ops:
  7.3 13.7 %gather_small.1 = bf16[32,32,128]{2,1,0:T(8,128)(2,1)} custom-call(bf16[32,128]{1,0:T(8,128)(2,1)} %bitcast.165), custom_call_target="tpu_custom_call" | custom-call | tf_op jit(solution)/shard_map/gather_small/pallas_call | solution.py:533
  21.0 1.0 reshape.290
  28.9 12.0 %swap_modulation.1 = f32[32,8,128]{2,1,0:T(8,128)} custom-call(f32[32,8,128]{2,1,0:T(8,128)} %bitcast.138), custom_call_target="tpu_custom_call" | custom-call | tf_op jit(solution)/shard_map/swap_modulation/pallas_call | solution.py:533
  40.8 1.0 reshape.294
  45.0 1.0 select_convert_fusion.1.query_spare
  46.0 1.0 select_convert_fusion.key_spare.refs_4_
  48.7 141.4 %forward_pass.1 = (bf16[12,4,2,2,64,512]{5,4,3,2,1,0:T(8,128)(2,1)}, bf16[1408,1024]{1,0:T(8,128)(2,1)}, bf16[1408,1024]{1,0:T(8,128)(2,1)}, bf16[1408,1024]{1,0...) custom-call(bf16[12,64,512]{2,1,0:T(8,128)(2,1)} %pad_maximum_fusion, ...), custom_call_target="tpu_custom_call" | custom-call | tf_op jit(solution)/shard_map/forward_pass/pallas_call | solution.py:953
  190.1 6.0 %fusion.13 = (bf16[4,4,2,2,64,512]{5,4,3,2,1,0:T(8,128)(2,1)}, bf16[4,4,2,2,64,512]{5,4,3,2,1,0:T(8,128)(2,1)}) fusion(bf16[12,4,2,2,64,512]{5,4,3,2,1,0:T(8,128)(2,1)} %get-tuple-element.49), kind=kLoop, calls=%fused_computation.63 | loop fusion | bytes 16777216 | tf_op jit(solution)/shard_map/slice | solution.py:1476
  196.1 32.7 %mlp_backward.1 = (bf16[1408,1024]{1,0:T(8,128)(2,1)}, bf16[4,1024,512]{2,1,0:T(8,128)(2,1)}, f32[4,1,512]{2,1,0:T(1,128)}) custom-call(bf16[1408,1024]{1,0:T(8,128)(2,1)} %get-tuple-element.48.refs_0_, bf16[4,1024,512]{2,1,0:T(8,128)(2,1)} %bitcast.126, bf16[4,1408,512]{2,1,0:T(8,128)(2,1)} %get-tuple-element.50.refs_2_, ...), custom_call_target="tpu_custom_call" | custom-call | tf_op jit(solution)/shard_map/mlp_backward/pallas_call | solution.py:1329
  228.8 2.3 slice.169
  231.1 3.9 slice.170
  235.0 1.6 copy-done.1
  236.6 17.3 %middle_backward.1 = (bf16[1408,1024]{1,0:T(8,128)(2,1)}, bf16[1408,512]{1,0:T(8,128)(2,1)}, bf16[1024,512]{1,0:T(8,128)(2,1)}, f32[2,4,1024]{2,1,0:T(4,128)}) custom-call(bf16[1408,1024]{1,0:T(8,128)(2,1)} %get-tuple-element.43.refs_0_, bf16[1408,1024]{1,0:T(8,128)(2,1)} %get-tuple-element.44.refs_1_, bf16[1408,1024]{1,0:T(8,128)(2,1)} %get-tuple-element.45.refs_2_, ...), custom_call_target="tpu_custom_call" | custom-call | tf_op jit(solution)/shard_map/middle_backward/pallas_call | solution.py:1329
  253.9 51.9 %attn_backward.1 = (bf16[3,1024,512]{2,1,0:T(8,128)(2,1)}, bf16[1408,1024]{1,0:T(8,128)(2,1)}, f32[8,512]{1,0:T(8,128)}) custom-call(bf16[1408,1024]{1,0:T(8,128)(2,1)} %get-tuple-element.55.refs_0_, bf16[3,1024,512]{2,1,0:T(8,128)(2,1)} %bitcast.127, bf16[8,1408,128]{2,1,0:T(8,128)(2,1)} %get-tuple-element.56.refs_2_, ...), custom_call_target="tpu_custom_call" | custom-call | tf_op jit(solution)/shard_map/attn_backward/pallas_call | solution.py:1329
  306.6 11.5 %pad_maximum_fusion.full_ref = bf16[12,4,2,2,64,512]{5,4,3,2,1,0:T(8,128)(2,1)} fusion(bf16[4,4,2,2,64,512]{5,4,3,2,1,0:T(8,128)(2,1)} %get-tuple-element.70, bf16[4,4,2,2,64,512]{5,4,3,2,1,0:T(8,128)(2,1)} %bitcast.129, bf16[1,4,2,2,64,512]{5,4,3,2,1,0:T(8,128)(2,1)S(1)} %bitcast.133, bf16[3,4,2,2,64,512]{5,4,3,2,1,0:T(8,128)(2,1)} %bitcast.130), kind=kLoop, calls=%fused_computation | loop fusion | flops 18874368 | bytes 25165824 | tf_op jit(solution)/shard_map/concatenate | solution.py:1582
  318.1 123.4 %reduce_weights.1 = f32[12,64,512]{2,1,0:T(8,128)S(1)} custom-call(bf16[12,4,2,2,64,512]{5,4,3,2,1,0:T(8,128)(2,1)} %pad_maximum_fusion.full_ref), custom_call_target="tpu_custom_call" | custom-call | tf_op jit(solution)/shard_map/reduce_weights/pallas_call | solution.py:1091
  446.8 13.0 %finish_rows.1 = (f32[340,2,1024]{2,1,0:T(2,128)}, f32[340,2,1024]{2,1,0:T(2,128)}, f32[2,8,1024]{2,1,0:T(8,128)}) custom-call(bf16[1408,1024]{1,0:T(8,128)(2,1)} %get-tuple-element.43.refs_0_, bf16[1408,1024]{1,0:T(8,128)(2,1)} %get-tuple-element.44.refs_1_, bf16[1408,1024]{1,0:T(8,128)(2,1)} %get-tuple-element.45.refs_2_, ...), custom_call_target="tpu_custom_call" | custom-call | tf_op jit(solution)/shard_map/finish_rows/pallas_call | solution.py:1329
  459.8 1.0 slice_reduce_fusion.3
  462.5 10.9 %swap_grads.1 = f32[32,16,128]{2,1,0:T(8,128)} custom-call(f32[32,16,128]{2,1,0:T(8,128)} %bitcast.134), custom_call_target="tpu_custom_call" | custom-call | tf_op jit(solution)/shard_map/swap_grads/pallas_call | solution.py:533
  473.4 1.0 reduce_sum.89
  474.4 1.1 reshape.307
  477.7 13.8 %swap_condition.1 = f32[32,16,128]{2,1,0:T(8,128)} custom-call(f32[32,16,128]{2,1,0:T(8,128)} %pad_maximum_fusion.2.src_ref), custom_call_target="tpu_custom_call" | custom-call | tf_op jit(solution)/shard_map/swap_condition/pallas_call | solution.py:533
  491.5 1.1 reshape.312
  492.8 1.2 fusion.1
  (163 shorter events, 33.3 us)
Async XLA Ops:
  0.6 27.1 %copy-start = (bf16[512,6,64]{0,2,1:T(8,128)(2,1)S(1)}, bf16[512,6,64]{0,2,1:T(8,128)(2,1)}, u32[]{:S(2)}) copy-start(bf16[512,6,64]{0,2,1:T(8,128)(2,1)} %param.19) | copy-start | bytes 1179652
  28.0 19.0 %copy-start.3 = (bf16[2048,64]{0,1:T(8,128)(2,1)S(1)}, bf16[2048,64]{0,1:T(8,128)(2,1)}, u32[]{:S(2)}) copy-start(bf16[2048,64]{0,1:T(8,128)(2,1)} %param.29) | copy-start | bytes 786436
  28.0 19.0 %copy-start.4 = (bf16[64,2048]{1,0:T(8,128)(2,1)S(1)}, bf16[64,2048]{1,0:T(8,128)(2,1)}, u32[]{:S(2)}) copy-start(bf16[64,2048]{1,0:T(8,128)(2,1)} %param.27) | copy-start | bytes 786436
  41.8 5.9 %copy-start.5 = (bf16[3,64,512]{2,1,0:T(8,128)(2,1)S(1)}, bf16[3,64,512]{2,1,0:T(8,128)(2,1)}, u32[]{:S(2)}) copy-start(bf16[3,64,512]{2,1,0:T(8,128)(2,1)} %param.21) | copy-start | bytes 589828
  41.8 5.9 %copy-start.6 = (bf16[512,64]{0,1:T(8,128)(2,1)S(1)}, bf16[512,64]{0,1:T(8,128)(2,1)}, u32[]{:S(2)}) copy-start(bf16[512,64]{0,1:T(8,128)(2,1)} %param.25) | copy-start | bytes 196612
  228.8 6.2 %collective-permute-start = (bf16[1408,1024]{1,0:T(8,128)(2,1)}, bf16[1408,1024]{1,0:T(8,128)(2,1)S(1)}, u32[]{:S(2)}, u32[]{:S(2)}) collective-permute-start(bf16[1408,1024]{1,0:T(8,128)(2,1)} %get-tuple-element.52.refs_3_), channel_id=1, source_target_pairs={{0,1},{1,0},{2,3},{3,2},{4,5},{5,4},{6,7},{7,6},{8,9},{9,8},{10,11... | collective-permute-start | bytes 8650760 | tf_op jit(solution)/shard_map/ppermute | solution.py:1341
  235.0 1.6 copy-start.1
  253.9 52.4 %copy-start.9 = (f32[4,1,512]{2,1,0:T(1,128)S(1)}, f32[4,1,512]{2,1,0:T(1,128)}, u32[]{:S(2)}) copy-start(f32[4,1,512]{2,1,0:T(1,128)} %get-tuple-element.66) | copy-start | bytes 24580
  253.9 52.7 %copy-start.2 = (bf16[1024,512]{1,0:T(8,128)(2,1)S(1)}, bf16[1024,512]{1,0:T(8,128)(2,1)}, u32[]{:S(2)}) copy-start(bf16[1024,512]{1,0:T(8,128)(2,1)} %get-tuple-element.68) | copy-start | bytes 3145732
  305.8 140.9 %collective-permute-start.1 = (bf16[1408,1024]{1,0:T(8,128)(2,1)}, bf16[1408,1024]{1,0:T(8,128)(2,1)}, u32[]{:S(2)}, u32[]{:S(2)}) collective-permute-start(bf16[1408,1024]{1,0:T(8,128)(2,1)} %get-tuple-element.60.refs_6_), channel_id=1, source_target_pairs={{0,1},{1,0},{2,3},{3,2},{4,5},{5,4},{6,7},{7,6},{8,9},{9,8},{10,11... | collective-permute-start | bytes 8650760 | tf_op jit(solution)/shard_map/ppermute | solution.py:1341
  318.1 124.9 %copy-start.7 = (f32[2,4,1024]{2,1,0:T(4,128)S(1)}, f32[2,4,1024]{2,1,0:T(4,128)}, u32[]{:S(2)}) copy-start(f32[2,4,1024]{2,1,0:T(4,128)} %get-tuple-element.63) | copy-start | bytes 98308
  473.4 22.8 %copy-start.8 = (bf16[2,1024]{1,0:T(2,128)(2,1)S(1)}, bf16[2,1024]{1,0:T(2,128)(2,1)}, u32[]{:S(2)}) copy-start(bf16[2,1024]{1,0:T(2,128)(2,1)} %param.17) | copy-start | bytes 12292

commit v4 on v3

--- a/solution.py
+++ b/solution.py
@@ -867,7 +867,7 @@
         load(8 + c).start()
         if c >= 2:
             down_saved[c - 2].wait()
-        grad_down[c % 2] = dot(turned[...], act[c]).astype(BF16).reshape(grad_down.shape[1:])
+        weight_grad(grad_down.at[c % 2], turned, act.at[c])
         down_saved.append(save(grad_down.at[c % 2], grad_down_out.at[c]))
     for c in range(ff_chunks):
         load(8 + c).wait()
@@ -974,147 +974,6 @@
     )(shard, tok, grad_in, mod, query_spare, key_spare, query_bias, value_bias, key_scale, up_bias, ones)
 
 
-def reduce_kernel(
-    grid,
-    chunks,
-    full_ref,
-    out_ref,
-    keep_low,
-    keep_high,
-    got_low,
-    got_high,
-    next_low,
-    next_high,
-    column,
-    got_z,
-    local_sem,
-    p_send,
-    p_recv,
-    z_send,
-    z_recv,
-):
-    nz, ny, nx = grid
-    half = nz // 2
-    z, y, x, core = coords(grid)
-
-    def dev(z_at, y_at, x_at):
-        return ((z_at * ny + y_at) * nx + x_at, core)
-
-    x_peer = dev(z, y, 1 - x)
-    y_peer = dev(z, 1 - y, x)
-    greet_all(nz * ny * nx * 2)
-
-    def own_copies(c):
-        return [
-            pltpu.make_async_copy(full_ref.at[c, pl.ds(0, half), y], keep_low.at[c], local_sem.at[c, 0]),
-            pltpu.make_async_copy(
-                full_ref.at[c, pl.ds(half, half), :, x], keep_high.at[c], local_sem.at[c, 1]
-            ),
-        ]
-
-    def first_copies(c):
-        return [
-            remote(
-                full_ref.at[c, pl.ds(0, half), 1 - y], got_low.at[c], p_send.at[c, 0], p_recv.at[c, 0], y_peer
-            ),
-            remote(
-                full_ref.at[c, pl.ds(half, half), :, 1 - x],
-                got_high.at[c],
-                p_send.at[c, 1],
-                p_recv.at[c, 1],
-                x_peer,
-            ),
-        ]
-
-    def second_copies(c):
-        return [
-            remote(keep_low.at[c, :, 1 - x], next_low.at[c], p_send.at[c, 2], p_recv.at[c, 2], x_peer),
-            remote(keep_high.at[c, :, 1 - y], next_high.at[c], p_send.at[c, 3], p_recv.at[c, 3], y_peer),
-        ]
-
-    def z_copies(c):
-        return [
-            remote(
-                column.at[c, (z + k) % nz],
-                got_z.at[c, k - 1],
-                z_send.at[c, k - 1],
-                z_recv.at[c, k - 1],
-                dev((z + k) % nz, y, x),
-            )
-            for k in range(1, nz)
-        ]
-
-    def add(a, b):
-        return (a.astype(F32) + b.astype(F32)).astype(BF16)
-
-    ahead = 2
-    for t in range(-ahead, chunks + 2):
-        if 0 <= t + ahead < chunks:
-            c = t + ahead
-            for copy in first_copies(c) + own_copies(c):
-                copy.start()
-        if 0 <= t < chunks:
-            for copy in own_copies(t):
-                copy.wait()
-            for copy in first_copies(t):
-                copy.wait_recv()
-            keep_low[t] = add(keep_low[t], got_low[t])
-            keep_high[t] = add(keep_high[t], got_high[t])
-            for copy in second_copies(t):
-                copy.start()
-        if 0 <= t - 1 < chunks:
-            c = t - 1
-            for copy in second_copies(c):
-                copy.wait_recv()
-            column[c, 0:half] = add(keep_low[c, :, x], next_low[c])
-            column[c, half:nz] = add(keep_high[c, :, y], next_high[c])
-            for copy in z_copies(c):
-                copy.start()
-        if 0 <= t - 2 < chunks:
-            c = t - 2
-            for copy in z_copies(c):
-                copy.wait_recv()
-            total = column[c, z].astype(F32)
-            for k in range(nz - 1):
-                total = total + got_z[c, k].astype(F32)
-            out_ref[c] = total
-    for c in range(chunks):
-        for copy in first_copies(c) + second_copies(c) + z_copies(c):
-            copy.wait_send()
-
-
-def reduce_weights(grid, full, collective_id):
-    nz, ny, nx = grid
-    half = nz // 2
-    chunks = full.shape[0]
-    block = full.shape[4:]
-    return pl.pallas_call(
-        functools.partial(reduce_kernel, grid, chunks),
-        out_shape=jax.ShapeDtypeStruct((chunks,) + block, F32),
-        in_specs=[pl.BlockSpec(memory_space=ANY)],
-        out_specs=pl.BlockSpec(memory_space=pltpu.VMEM),
-        scratch_shapes=[
-            pltpu.VMEM((chunks, half, nx) + block, BF16),
-            pltpu.VMEM((chunks, half, ny) + block, BF16),
-            pltpu.VMEM((chunks, half, nx) + block, BF16),
-            pltpu.VMEM((chunks, half, ny) + block, BF16),
-            pltpu.VMEM((chunks, half) + block, BF16),
-            pltpu.VMEM((chunks, half) + block, BF16),
-            pltpu.VMEM((chunks, nz) + block, BF16),
-            pltpu.VMEM((chunks, nz - 1) + block, BF16),
-            pltpu.SemaphoreType.DMA((chunks, 2)),
-            pltpu.SemaphoreType.DMA((chunks, 4)),
-            pltpu.SemaphoreType.DMA((chunks, 4)),
-            pltpu.SemaphoreType.DMA((chunks, nz - 1)),
-            pltpu.SemaphoreType.DMA((chunks, nz - 1)),
-        ],
-        compiler_params=pltpu.CompilerParams(
-            collective_id=collective_id, has_side_effects=True, vmem_limit_bytes=48 * 2**20
-        ),
-        name="reduce_weights",
-    )(full)
-
-
 def dot(a, b):
     return jnp.dot(a, b, preferred_element_type=F32)
 
@@ -1156,6 +1015,17 @@
     lax.fori_loop(0, src.shape[0] // 128, step, 0)
 
 
+def weight_grad(dst, turned, right):
+    rows = turned.shape[0] // dst.shape[0]
+
+    def step(i, carry):
+        at = pl.ds(pl.multiple_of(i * rows, rows), rows)
+        dst[i] = dot(turned[at, :], right[...]).astype(BF16).reshape(dst.shape[1:])
+        return carry
+
+    lax.fori_loop(0, dst.shape[0], step, 0)
+
+
 def for_blocks(count, rows, body):
     def step(a, carry):
         body(a, pl.ds(pl.multiple_of(a * rows, 16), rows))
@@ -1163,65 +1033,277 @@
 
     lax.fori_loop(0, count, step, 0)
 
-
-def mlp_backward(sizes, dm, down, slope, mlp, up, grad_part, grad_up, bias_sum, turned, low):
+def backward_kernel(
+    grid,
+    sizes,
+    full,
+    x_in,
+    grad_in,
+    mixed_in,
+    qaug_in,
+    kv_in,
+    inverse_in,
+    att_in,
+    branch_in,
+    mlp_in,
+    slope_in,
+    dm_in,
+    grad_down_in,
+    mod,
+    key_spare,
+    key_scale,
+    ones,
+    out,
+    mid_own,
+    ga_own,
+    ga_other,
+    stats,
+    up_sum,
+    qkv_sum,
+    b0,
+    b1,
+    b2,
+    b3,
+    b4,
+    turned,
+    pool,
+    qaug,
+    w,
+    work,
+    got_low,
+    got_high,
+    next_low,
+    next_high,
+    got_z,
+    p_send,
+    p_recv,
+    z_send,
+    z_recv,
+    t_send,
+    t_recv,
+    load_sem,
+):
+    nz, ny, nx = grid
+    half = nz // 2
     seqs, pad = sizes
-    chunks = up.shape[0]
-    transpose_into(turned, mlp)
-    bias_sum[...] = jnp.zeros_like(bias_sum)
-    for c in range(chunks):
+    chunks = out.shape[0]
+    slots = work.shape[0]
+    ff_chunks = slope_in.shape[0]
+    z, y, x_at, core = coords(grid)
+    width = b0.shape[1]
+    part_width = pool.shape[2]
+    pairs = part_width // 128
+    blocks = seqs * 2
+    ln2 = 0.6931471805599453
+
+    def dev(z_to, y_to, x_to):
+        return ((z_to * ny + y_to) * nx + x_to, core)
+
+    x_peer = dev(z, y, 1 - x_at)
+    y_peer = dev(z, 1 - y, x_at)
+    sibling = (place()[0], 1 - core)
+    greet([x_peer, y_peer, sibling] + [dev((z + k) % nz, y, x_at) for k in range(1, nz)])
+
+    def block_rows(a):
+        return pl.ds(pl.multiple_of(a * pad, 16), pad)
+
+    loads = []
+
+    def load(src, dst):
+        copy = pltpu.make_async_copy(src, dst, load_sem.at[len(loads)])
+        copy.start()
+        loads.append(copy)
+        return copy
+
+    def first_copies(c):
+        s = c % slots
+        return [
+            remote(
+                work.at[s, pl.ds(0, half), 1 - y], got_low.at[c], p_send.at[c, 0], p_recv.at[c, 0], y_peer
+            ),
+            remote(
+                work.at[s, pl.ds(half, half), :, 1 - x_at],
+                got_high.at[c],
+                p_send.at[c, 1],
+                p_recv.at[c, 1],
+                x_peer,
+            ),
+        ]
+
+    def second_copies(c):
+        s = c % slots
+        return [
+            remote(
+                work.at[s, pl.ds(0, half), y, 1 - x_at],
+                next_low.at[c],
+                p_send.at[c, 2],
+                p_recv.at[c, 2],
+                x_peer,
+            ),
+            remote(
+                work.at[s, pl.ds(half, half), 1 - y, x_at],
+                next_high.at[c],
+                p_send.at[c, 3],
+                p_recv.at[c, 3],
+                y_peer,
+            ),
+        ]
+
+    def z_copies(c):
+        s = c % slots
+        return [
+            remote(
+                work.at[s, (z + k) % nz, y, x_at],
+                got_z.at[c, k - 1],
+                z_send.at[c, k - 1],
+                z_recv.at[c, k - 1],
+                dev((z + k) % nz, y, x_at),
+            )
+            for k in range(1, nz)
+        ]
+
+    def add(a, b):
+        return (a.astype(F32) + b.astype(F32)).astype(BF16)
+
+    def begin(c):
+        for copy in first_copies(c):
+            copy.start()
+
+    def second(c):
+        s = c % slots
+        for copy in first_copies(c):
+            copy.wait_recv()
+        work[s, 0:half, y] = add(work[s, 0:half, y], got_low[c])
+        work[s, half:nz, :, x_at] = add(work[s, half:nz, :, x_at], got_high[c])
+        for copy in second_copies(c):
+            copy.start()
+
+    def third(c):
+        s = c % slots
+        for copy in second_copies(c):
+            copy.wait_recv()
+        work[s, 0:half, y, x_at] = add(work[s, 0:half, y, x_at], next_low[c])
+        work[s, half:nz, y, x_at] = add(work[s, half:nz, y, x_at], next_high[c])
+        for copy in z_copies(c):
+            copy.start()
+
+    def last(c):
+        s = c % slots
+        for copy in z_copies(c):
+            copy.wait_recv()
+        total = work[s, z, y, x_at].astype(F32)
+        for k in range(nz - 1):
+            total = total + got_z[c, k].astype(F32)
+        out[c] = total
+
+    def sent(c):
+        for copy in first_copies(c) + second_copies(c) + z_copies(c):
+            copy.wait_send()
+
+    def put(c, right):
+        if c >= slots:
+            sent(c - slots)
+        weight_grad(work.at[c % slots], turned, right)
+
+    def step(t, start=True):
+        if start and t < chunks:
+            begin(t)
+        if 0 <= t - 2 < chunks:
+            second(t - 2)
+        if 0 <= t - 3 < chunks:
+            third(t - 3)
+        if 0 <= t - 4 < chunks:
+            last(t - 4)
+
+    def weight(slot):
+        return w[slot].reshape(width, part_width)
+
+    down_grads = [load(grad_down_in.at[c], work.at[c]) for c in range(ff_chunks)]
+    mlp_load = load(mlp_in, b1)
+    dm_load = load(dm_in, b0)
+    down_loads = [
+        (load(full.at[chunks - ff_chunks + c], w.at[c]), load(slope_in.at[c], pool.at[c]))
+        for c in range(ff_chunks)
+    ]
+    branch_load = load(branch_in, b4)
+    qaug_load = load(qaug_in, qaug)
+    for c in range(2):
+        down_grads[c].wait()
+        step(c)
+    for c in range(2, ff_chunks):
+        down_grads[c].wait()
+    mlp_load.wait()
+    transpose_into(turned, b1)
+    grad_load = load(grad_in, b1)
+    dm_load.wait()
+    up_sum[...] = jnp.zeros_like(up_sum)
+    up_loads = []
+    for c in range(ff_chunks):
+        for copy in down_loads[c]:
+            copy.wait()
 
         def back(a, rows):
-            gh = dot(dm[rows, :], down[c]) * slope[c, rows, :].astype(F32)
-            bias_sum[c] += column_sum(gh)
-            low[c, rows, :] = gh.astype(BF16)
-
-        for_blocks(seqs * 2, pad, back)
-        grad_up[c] = dot(turned[...], low[c]).astype(BF16)
-
-    def gather(a, rows):
-        total = dot_nt(low[0, rows, :], up[0])
-        for c in range(1, chunks):
-            total = total + dot_nt(low[c, rows, :], up[c])
-        grad_part[rows, :] = total.astype(BF16)
-
-    for_blocks(seqs * 2, pad, gather)
-
-
-def middle_backward(sizes, x, grad, branch, grad_part, grad_other, mod, proj, att, grad_mid, grad_att, grad_proj, stats, da, turned):
-    seqs, pad = sizes
+            gh = dot(b0[rows, :], weight(c)) * pool[c, rows, :].astype(F32)
+            up_sum[c] += column_sum(gh)
+            pool[c, rows, :] = gh.astype(BF16)
+
+        for_blocks(blocks, pad, back)
+        up_loads.append(load(full.at[4 + c], w.at[c]))
+        put(ff_chunks + c, pool.at[c])
+        if c != 1:
+            step(2 + (c + 1) // 2)
+    x_load = load(x_in, b0)
+    for copy in up_loads:
+        copy.wait()
+    swaps = []
+    for a in range(blocks):
+        rows = block_rows(a)
+        total = dot_nt(pool[0, rows, :], weight(0))
+        for c in range(1, ff_chunks):
+            total = total + dot_nt(pool[c, rows, :], weight(c))
+        b2[rows, :] = total.astype(BF16)
+        copy = remote(b2.at[rows, :], b3.at[rows, :], t_send.at[a], t_recv.at[a], sibling)
+        copy.start()
+        swaps.append(copy)
+    proj_load = load(full.at[3], w.at[3])
+    qkv_loads = [load(full.at[j], w.at[j]) for j in range(3)]
+    step(5)
+    for copy in (x_load, grad_load, branch_load, proj_load):
+        copy.wait()
     stats[...] = jnp.zeros_like(stats)
-
-    def back(a, rows):
+    grad_att = pool.at[3]
+    for a in range(blocks):
+        rows = block_rows(a)
         s = a // 2
-        b = branch[rows, :].astype(F32)
-        gm = grad_part[rows, :].astype(F32) + grad_other[rows, :].astype(F32)
-        normed, inverse = normalize(x[rows, :].astype(F32) + mod[s, 0:1, :] * b)
+        swaps[a].wait()
+        b = b4[rows, :].astype(F32)
+        gm = b2[rows, :].astype(F32) + b3[rows, :].astype(F32)
+        normed, inverse = normalize(b0[rows, :].astype(F32) + mod[s, 0:1, :] * b)
         stats[s, 1:2, :] += 0.5 * column_sum(gm * normed)
         stats[s, 2:3, :] += 0.5 * column_sum(gm)
-        mid = grad[rows, :].astype(F32) + norm_back(gm * (1.0 + mod[s, 3:4, :]), normed, inverse)
-        grad_mid[rows, :] = mid.astype(BF16)
+        mid = b1[rows, :].astype(F32) + norm_back(gm * (1.0 + mod[s, 3:4, :]), normed, inverse)
+        b1[rows, :] = mid.astype(BF16)
         stats[s, 0:1, :] += 0.5 * column_sum(mid * b)
         branch_grad = mid * mod[s, 0:1, :]
         stats[s, 3:4, :] += 0.5 * column_sum(branch_grad)
         low = branch_grad.astype(BF16)
-        da[rows, :] = low
-        grad_att[rows, :] = dot(low, proj[...]).astype(BF16)
-
-    for_blocks(seqs * 2, pad, back)
-    transpose_into(turned, da)
-    grad_proj[...] = dot(turned[...], att[...]).astype(BF16)
-
-
-def attn_backward(
-    sizes, mixed, w, qaug, kv, key_spare, grad_att, inverses, key_scale, ones, grad_qkv, grad_part, bias_sum, low, turned
-):
-    seqs, pad = sizes
-    part_width = grad_att.shape[1]
-    pairs = part_width // 128
-    bias_sum[...] = jnp.zeros_like(bias_sum)
-    transpose_into(turned, mixed)
-    ln2 = 0.6931471805599453
+        b4[rows, :] = low
+        grad_att[rows, :] = dot(low, weight(3)).astype(BF16)
+        if a == 1:
+            step(6)
+    mid_saves = [load(b1.at[block_rows(s * 2 + core), :], mid_own.at[s]) for s in range(seqs)]
+    att = b2.at[:, pl.ds(0, part_width)]
+    att_load = load(att_in, att)
+    kv_load = load(kv_in, b3)
+    transpose_into(turned, b4)
+    step(7)
+    mixed_load = load(mixed_in, b4)
+    att_load.wait()
+    put(8, att)
+    inverse_load = load(inverse_in, b2)
+    kv_load.wait()
+    qaug_load.wait()
+    qkv_sum[...] = jnp.zeros_like(qkv_sum)
 
     def attend(i, carry):
         p = i // seqs
@@ -1230,11 +1312,11 @@
         all_rows = pl.ds(start, 2 * pad)
         at = pl.multiple_of(p * 128, 128)
         lanes = pl.ds(at, 128)
-        first, code = lane_code(pad)
+        first, unused = lane_code(pad)
         first_all, unused = lane_code(2 * pad)
-        k_sides = both_heads(kv[all_rows, lanes], key_spare[all_rows, :])
-        v_sides = both_heads(kv[all_rows, pl.ds(at + part_width, 128)], 0.0)
-        g_sides = both_heads(grad_att[all_rows, lanes], 0.0)
+        k_sides = both_heads(b3[all_rows, lanes], key_spare[all_rows, :])
+        v_sides = both_heads(b3[all_rows, pl.ds(at + part_width, 128)], 0.0)
+        g_sides = both_heads(pool[3, all_rows, lanes], 0.0)
         grads_k, grads_v, grads_q = [], [], [[], []]
         for side in range(2):
             h = 2 * p + side
@@ -1259,17 +1341,31 @@
             rows = pl.ds(pl.multiple_of(start + t * pad, 16), pad)
             gq = jnp.where(first, grads_q[t][0], grads_q[t][1])
             q = jnp.where(first, qaug[2 * p, rows, :].astype(F32), qaug[2 * p + 1, rows, :].astype(F32))
-            bias_sum[2:3, lanes] += ln2 * column_sum(gq * q)
-            low[0, rows, lanes] = gq.astype(BF16)
-        low[1, all_rows, lanes] = (ln2 * jnp.where(first_all, grads_k[0], grads_k[1])).astype(BF16)
-        low[2, all_rows, lanes] = jnp.where(first_all, grads_v[0], grads_v[1]).astype(BF16)
+            qkv_sum[2:3, lanes] += ln2 * column_sum(gq * q)
+            pool[0, rows, lanes] = gq.astype(BF16)
+        pool[1, all_rows, lanes] = (ln2 * jnp.where(first_all, grads_k[0], grads_k[1])).astype(BF16)
+        gv = jnp.where(first_all, grads_v[0], grads_v[1])
+        qkv_sum[1:2, lanes] += column_sum(gv)
+        pool[2, all_rows, lanes] = gv.astype(BF16)
         return carry
 
-    lax.fori_loop(0, pairs * seqs, attend, 0)
-
-    def finish(a, rows):
-        first, code = lane_code(pad)
-
+    count = pairs * seqs
+    for quarter in range(4):
+        lax.fori_loop(quarter * count // 4, (quarter + 1) * count // 4, attend, 0)
+        if quarter == 0:
+            step(8)
+        elif quarter < 3:
+            step(8 + quarter, start=False)
+    third(8)
+    last(7)
+    mixed_load.wait()
+    transpose_into(turned, b4)
+    put(9, pool.at[2])
+    begin(9)
+    inverse_load.wait()
+
+    def finish_q(a, rows):
+        first, unused = lane_code(pad)
         scale = key_scale[...]
         unit = jnp.concatenate(
             [
@@ -1279,24 +1375,119 @@
             axis=1,
         )
         unit = unit / scale
-        f = low[0, rows, :].astype(F32) * (scale * ln2)
-        product = f * unit
-        gq = inverses[rows, 0:part_width].astype(F32) * (f - unit * dot(product.astype(BF16), ones[...]))
-        bias_sum[0:1, :] += column_sum(gq)
-        low[0, rows, :] = gq.astype(BF16)
-        unit = kv[rows, 0:part_width].astype(F32)
-        f = low[1, rows, :].astype(F32)
-        gk = inverses[rows, part_width : 2 * part_width].astype(F32) * (f - unit * dot((f * unit).astype(BF16), ones[...]))
-        low[1, rows, :] = gk.astype(BF16)
-        bias_sum[1:2, :] += column_sum(low[2, rows, :].astype(F32))
-        total = dot_nt(low[0, rows, :], w[0])
+        f = pool[0, rows, :].astype(F32) * (scale * ln2)
+        gq = b2[rows, 0:part_width].astype(F32) * (f - unit * dot((f * unit).astype(BF16), ones[...]))
+        qkv_sum[0:1, :] += column_sum(gq)
+        pool[0, rows, :] = gq.astype(BF16)
+
+    def finish_k(a, rows):
+        unit = b3[rows, 0:part_width].astype(F32)
+        f = pool[1, rows, :].astype(F32)
+        gk = b2[rows, part_width : 2 * part_width].astype(F32) * (
+            f - unit * dot((f * unit).astype(BF16), ones[...])
+        )
+        pool[1, rows, :] = gk.astype(BF16)
+
+    for_blocks(blocks, pad, finish_q)
+    put(10, pool.at[0])
+    begin(10)
+    last(8)
+    for_blocks(blocks, pad, finish_k)
+    put(11, pool.at[1])
+    begin(11)
+    second(9)
+    for copy in qkv_loads:
+        copy.wait()
+    end_copies = []
+    end_saves = []
+    for i in range(blocks):
+        s = i % seqs
+        which = 1 - core if i < seqs else core
+        rows = block_rows(s * 2 + which)
+        total = dot_nt(pool[0, rows, :], weight(0))
         for j in range(1, 3):
-            total = total + dot_nt(low[j, rows, :], w[j])
-        grad_part[rows, :] = total.astype(BF16)
-
-    for_blocks(seqs * 2, pad, finish)
-    for j in range(3):
-        grad_qkv[j] = dot(turned[...], low[j]).astype(BF16)
+            total = total + dot_nt(pool[j, rows, :], weight(j))
+        b0[rows, :] = total.astype(BF16)
+        if i < seqs:
+            copy = remote(b0.at[rows, :], ga_other.at[s], t_send.at[blocks + s], t_recv.at[blocks + s], sibling)
+            copy.start()
+            end_copies.append(copy)
+        else:
+            end_saves.append(load(b0.at[rows, :], ga_own.at[s]))
+        if i == 1:
+            second(10)
+            third(9)
+    second(11)
+    third(10)
+    last(9)
+    third(11)
+    last(10)
+    last(11)
+    for copy in end_copies + end_saves + mid_saves:
+        copy.wait()
+    for c in range(chunks - slots, chunks):
+        sent(c)
+
+
+def backward_pass(grid, sizes, operands, mod, key_spare, key_scale, ones, collective_id):
+    nz, ny, nx = grid
+    half = nz // 2
+    seqs, pad = sizes
+    full, slope = operands[0], operands[10]
+    chunks = full.shape[0]
+    own_rows, part = full.shape[4:]
+    ff_chunks = slope.shape[0]
+    total = seqs * 2 * pad
+    width = nz * ny * nx * own_rows
+    heads = part // 64
+    wide = ((total, width), BF16)
+    chunk = (nz, ny, nx, own_rows, part)
+    block = (own_rows, part)
+    slots = 8
+    outs = [
+        ((chunks,) + block, F32),
+        ((seqs, pad, width), BF16),
+        ((seqs, pad, width), BF16),
+        ((seqs, pad, width), BF16),
+        ((seqs, 4, width), F32),
+        ((ff_chunks, 1, part), F32),
+        ((8, part), F32),
+    ]
+    scratch = [wide] * 5 + [
+        ((width, total), BF16),
+        ((ff_chunks, total, part), BF16),
+        ((heads, total, 128), BF16),
+        ((4,) + chunk, BF16),
+        ((slots,) + chunk, BF16),
+        ((chunks, half, nx) + block, BF16),
+        ((chunks, half, ny) + block, BF16),
+        ((chunks, half) + block, BF16),
+        ((chunks, half) + block, BF16),
+        ((chunks, nz - 1) + block, BF16),
+    ]
+    vmem = pl.BlockSpec(memory_space=pltpu.VMEM)
+    hbm = pl.BlockSpec(memory_space=ANY)
+    swaps = seqs * 2 + seqs
+    return pl.pallas_call(
+        functools.partial(backward_kernel, grid, sizes),
+        out_shape=[jax.ShapeDtypeStruct(shape, dtype) for shape, dtype in outs],
+        in_specs=[hbm] * 13 + [vmem] * 4,
+        out_specs=[vmem] + [hbm] * 3 + [vmem] * 3,
+        scratch_shapes=[pltpu.VMEM(shape, dtype) for shape, dtype in scratch]
+        + [
+            pltpu.SemaphoreType.DMA((chunks, 4)),
+            pltpu.SemaphoreType.DMA((chunks, 4)),
+            pltpu.SemaphoreType.DMA((chunks, nz - 1)),
+            pltpu.SemaphoreType.DMA((chunks, nz - 1)),
+            pltpu.SemaphoreType.DMA((swaps,)),
+            pltpu.SemaphoreType.DMA((swaps,)),
+            pltpu.SemaphoreType.DMA((40,)),
+        ],
+        compiler_params=pltpu.CompilerParams(
+            collective_id=collective_id, has_side_effects=True, vmem_limit_bytes=60 * 2**20
+        ),
+        name="backward_pass",
+    )(*operands, mod, key_spare, key_scale, ones)
 
 
 def finish_rows(sizes, x, grad, branch, mlp_part, mlp_other, grad_mid, grad_part, grad_other, mod, output, grad_tokens, stats):
@@ -1314,10 +1505,10 @@
         stats[s, 0:1, :] = column_sum(g * b)
         stats[s, 1:2, :] = column_sum(g * mod[s, 1:2, :])
         normed, inverse = normalize(xs)
-        gm = grad_part[rows, :].astype(F32) + grad_other[rows, :].astype(F32)
+        gm = grad_part[s].astype(F32) + grad_other[s].astype(F32)
         stats[s, 2:3, :] = column_sum(gm * normed)
         stats[s, 3:4, :] = column_sum(gm)
-        gt = grad_mid[rows, :].astype(F32) + norm_back(gm * (1.0 + mod[s, 2:3, :]), normed, inverse)
+        gt = grad_mid[s].astype(F32) + norm_back(gm * (1.0 + mod[s, 2:3, :]), normed, inverse)
         grad_tokens[:, s, :] = gt[0:length]
         stats[s, 4:8, :] = jnp.zeros_like(stats[s, 4:8, :])
 
@@ -1335,10 +1526,6 @@
         compiler_params=pltpu.CompilerParams(vmem_limit_bytes=60 * 2**20),
         name=name,
     )(*operands)
-
-
-def sibling_swap(values):
-    return lax.ppermute(values, "tensor", [(0, 1), (1, 0)])
 
 
 def pad_rows(values, rows):
@@ -1432,13 +1619,6 @@
     key_scale = jnp.repeat(jnp.exp(head_scale) * 1.4426950408889634, head_dim).reshape(1, part)
     head_at = jnp.arange(part) // head_dim
     ones = (head_at[:, None] == head_at[None, :]).astype(BF16)
-    wide_rows = ((total, width), BF16)
-    part_rows = ((total, part), BF16)
-    head_rows = ((heads, total, 2 * head_dim), BF16)
-    ff_rows = ((ff_chunks, total, part), BF16)
-    weight_rows = ((width, part), BF16)
-    turned = ((width, total), BF16)
-
     (
         full,
         x,
@@ -1471,38 +1651,20 @@
         ones,
         0,
     )
-    full = full.reshape(-1, width, part)
-    grad_down = grad_down.reshape(-1, width, part)
-    up = full[4 : 4 + ff_chunks]
-    down = full[4 + ff_chunks :]
-    gm_part, grad_up, up_sum = run(
-        mlp_backward,
+    reduced, grad_mid, ga_part, ga_other, mid_stats, up_sum, qkv_sum = backward_pass(
+        grid,
         sizes,
-        (dm, down, slope, mlp, up),
-        [wide_rows, ((ff_chunks, width, part), BF16), ((ff_chunks, 1, part), F32)],
-        [turned, ff_rows],
-        name="mlp_backward",
-    )
-    grad_mid, grad_att, grad_proj, mid_stats = run(
-        middle_backward,
-        sizes,
-        (x, grad, branch, gm_part, sibling_swap(gm_part), mod, full[3], att),
-        [wide_rows, part_rows, weight_rows, ((seqs, 4, width), F32)],
-        [wide_rows, turned],
-        name="middle_backward",
-    )
-    grad_qkv, ga_part, qkv_sum = run(
-        attn_backward,
-        sizes,
-        (mixed, full[:3], qaug, kv, key_spare, grad_att, inverses, key_scale, ones),
-        [((3, width, part), BF16), wide_rows, ((8, part), F32)],
-        [((3, total, part), BF16), turned],
-        name="attn_backward",
+        (full, x, grad, mixed, qaug, kv, inverses, att, branch, mlp, slope, dm, grad_down),
+        mod,
+        key_spare,
+        key_scale,
+        ones,
+        5,
     )
     output, grad_inputs, end_stats = run(
         finish_rows,
         sizes,
-        (x, grad, branch, mlp_part, mlp_other, grad_mid, ga_part, sibling_swap(ga_part), mod),
+        (x, grad, branch, mlp_part, mlp_other, grad_mid, ga_part, ga_other, mod),
         [((own_len, seqs, width), F32), ((own_len, seqs, width), F32), ((seqs, 8, width), F32)],
         name="finish_rows",
     )
@@ -1577,13 +1739,7 @@
     ada_rows = lax.dynamic_slice_in_dim(ada_cols, core * heads, heads, 0).transpose(1, 0, 2)
     grad_ada_bias = lax.dynamic_slice_in_dim(ada_rows, chip * ada_bias.shape[2], ada_bias.shape[2], 2)
 
-    reduced = reduce_weights(
-        grid,
-        jnp.concatenate([grad_qkv, grad_proj[None], grad_up, grad_down], axis=0).reshape(
-            (-1,) + grid + (own_rows, part)
-        ),
-        5,
-    )
+    chunks = reduced.shape[0]
     wide = lambda values: values.transpose(1, 0, 2).reshape(own_rows, -1)
     return (
         output.transpose(1, 0, 2),
@@ -1591,15 +1747,15 @@
         grad_condition,
         grad_ada,
         grad_ada_bias,
-        reduced[:3],
+        jnp.stack([reduced[chunks - 2], reduced[chunks - 1], reduced[chunks - 3]]),
         owned[0],
         owned[1],
         owned[3],
-        reduced[3].T,
+        reduced[2 * ff_chunks].T,
         owned[4],
-        wide(reduced[4 : 4 + ff_chunks]),
+        wide(reduced[ff_chunks : 2 * ff_chunks]),
         owned[2],
-        wide(reduced[4 + ff_chunks :]).T,
+        wide(reduced[:ff_chunks]).T,
         owned[5],
     )
 

time: 504 us -> 393 us (0.78)
  Pallas kernels: 430 us -> 345 us
  local copies, waits for them, and re-layouts: 44.9 us -> 30.4 us
  other arithmetic: 20.9 us -> 10.2 us
    pallas_call x4 -> x1, Pallas kernels: 115 us -> 11.7 us  [run(): pl.pallas_call(kernel, out_shape=[jax.ShapeDtypeStruct(shape, dtype) for...]
    pallas_call x1, Pallas kernels: 123 us -> 141 us  [backward_pass(): pl.pallas_call(functools.partial(backward_kernel, grid, sizes), out_shape...]
    slice x4 -> x1, local copies, waits for them, and re-layouts: 13 us -> 0.02 us  [fast_device(): reduced[chunks - 2]]
    concatenate x1 -> x0, other arithmetic: 11.5 us -> none  [fast_device(): jnp.concatenate([grad_qkv, grad_proj[None], grad_up, grad_down], axis=0)]
    unnamed x43 -> x41, local copies, waits for them, and re-layouts: 11 us -> 9.43 us
  transfers between devices with their start and end apart: 2 -> 0, of which waited for: 0 -> 0; matrix products, arithmetic and copies ran while one was open for 5% -> 0% of each run, Pallas kernels for 25% -> 0%
where the time goes in v4:
time: 393 us; the launch traced here: 389 us
  Pallas kernels  345 us (88%)
  local copies, waits for them, and re-layouts  30.4 us (8%)
  other arithmetic  10.2 us (3%)
    pallas_call x1, Pallas kernels, forward_pass(): pl.pallas_call(functools.partial(forward_kernel, grid, sizes, ff_chunks),...  142 us
    pallas_call x1, Pallas kernels, backward_pass(): pl.pallas_call(functools.partial(backward_kernel, grid, sizes), out_shape...  141 us
    pallas_call x4, Pallas kernels, swap(): pl.pallas_call(functools.partial(swap_kernel, count, to_all), out_shape=j...  50.1 us
    pallas_call x1, Pallas kernels, run(): pl.pallas_call(kernel, out_shape=[jax.ShapeDtypeStruct(shape, dtype) for...  11.7 us
    unnamed x41, local copies, waits for them, and re-layouts  9.43 us

profile of v4, /device:TPU:0, one launch (start us, length us, event | category | flops | bytes accessed | tf_op | source)
XLA Modules:
  0.0 389.0 jit_solution(17088831681490395802)
XLA Ops:
  6.3 0.8 reshape.283
  7.9 0.8 copy.128
  9.6 13.7 %gather_small.1 = bf16[32,32,128]{2,1,0:T(8,128)(2,1)} custom-call(bf16[32,128]{1,0:T(8,128)(2,1)} %bitcast.151), custom_call_target="tpu_custom_call" | custom-call | tf_op jit(solution)/shard_map/gather_small/pallas_call | solution.py:533
  23.3 1.0 reshape.276
  28.9 11.9 %swap_modulation.1 = f32[32,8,128]{2,1,0:T(8,128)} custom-call(f32[32,8,128]{2,1,0:T(8,128)} %bitcast.124), custom_call_target="tpu_custom_call" | custom-call | tf_op jit(solution)/shard_map/swap_modulation/pallas_call | solution.py:533
  40.8 1.0 reshape.280
  43.0 1.0 select_convert_fusion.key_spare
  43.9 1.0 select_convert_fusion.1.query_spare
  44.9 0.9 compare_convert_fusion.ones
  46.0 1.0 pad_maximum_fusion.shard
  48.6 142.4 %forward_pass.1 = (bf16[12,4,2,2,64,512]{5,4,3,2,1,0:T(8,128)(2,1)}, bf16[1408,1024]{1,0:T(8,128)(2,1)}, bf16[1408,1024]{1,0:T(8,128)(2,1)}, bf16[1408,1024]{1,0...) custom-call(bf16[12,64,512]{2,1,0:T(8,128)(2,1)} %pad_maximum_fusion, ...), custom_call_target="tpu_custom_call" | custom-call | tf_op jit(solution)/shard_map/forward_pass/pallas_call | solution.py:953
  191.0 141.2 %backward_pass.1 = (f32[12,64,512]{2,1,0:T(8,128)}, bf16[2,352,1024]{2,1,0:T(8,128)(2,1)}, bf16[2,352,1024]{2,1,0:T(8,128)(2,1)}, bf16[2,352,1024]{2,1,0:T(8,128...) custom-call(bf16[12,4,2,2,64,512]{5,4,3,2,1,0:T(8,128)(2,1)} %get-tuple-element.45.full, ...), custom_call_target="tpu_custom_call" | custom-call | tf_op jit(solution)/shard_map/backward_pass/pallas_call | solution.py:1471
  332.2 11.7 %finish_rows.1 = (f32[340,2,1024]{2,1,0:T(2,128)}, f32[340,2,1024]{2,1,0:T(2,128)}, f32[2,8,1024]{2,1,0:T(8,128)}) custom-call(bf16[1408,1024]{1,0:T(8,128)(2,1)} %get-tuple-element.40.x_in.refs_0_, bf16[1408,1024]{1,0:T(8,128)(2,1)} %get-tuple-element.41.grad_in.refs_1_, bf16[1408,1024]{1,0:T(8,128)(2,1)} %get-tuple-element.42.branch_in.refs_2_, ...), custom_call_target="tpu_custom_call" | custom-call | tf_op jit(solution)/shard_map/finish_rows/pallas_call | solution.py:1520
  343.9 0.9 slice_reduce_fusion.5
  345.0 1.0 slice_reduce_fusion.3
  349.0 11.3 %swap_grads.1 = f32[32,16,128]{2,1,0:T(8,128)} custom-call(f32[32,16,128]{2,1,0:T(8,128)} %bitcast.120), custom_call_target="tpu_custom_call" | custom-call | tf_op jit(solution)/shard_map/swap_grads/pallas_call | solution.py:533
  360.3 1.0 reduce_sum.89
  361.3 1.1 reshape.293
  366.7 13.2 %swap_condition.1 = f32[32,16,128]{2,1,0:T(8,128)} custom-call(f32[32,16,128]{2,1,0:T(8,128)} %pad_maximum_fusion.2.src_ref), custom_call_target="tpu_custom_call" | custom-call | tf_op jit(solution)/shard_map/swap_condition/pallas_call | solution.py:533
  379.9 1.1 reshape.298
  385.1 0.8 copy.183
  386.0 0.8 pad_maximum_fusion.1
  386.7 1.2 fusion.1
  387.9 0.8 copy.182
  (151 shorter events, 26.0 us)
Async XLA Ops:
  0.6 27.1 %copy-start = (bf16[512,6,64]{0,2,1:T(8,128)(2,1)S(1)}, bf16[512,6,64]{0,2,1:T(8,128)(2,1)}, u32[]{:S(2)}) copy-start(bf16[512,6,64]{0,2,1:T(8,128)(2,1)} %param.19) | copy-start | bytes 1179652
  25.1 20.8 %copy-start.2 = (bf16[2048,64]{0,1:T(8,128)(2,1)S(1)}, bf16[2048,64]{0,1:T(8,128)(2,1)}, u32[]{:S(2)}) copy-start(bf16[2048,64]{0,1:T(8,128)(2,1)} %param.29) | copy-start | bytes 786436
  25.1 20.8 %copy-start.3 = (bf16[64,2048]{1,0:T(8,128)(2,1)S(1)}, bf16[64,2048]{1,0:T(8,128)(2,1)}, u32[]{:S(2)}) copy-start(bf16[64,2048]{1,0:T(8,128)(2,1)} %param.27) | copy-start | bytes 786436
  27.7 18.2 %copy-start.4 = (bf16[3,64,512]{2,1,0:T(8,128)(2,1)S(1)}, bf16[3,64,512]{2,1,0:T(8,128)(2,1)}, u32[]{:S(2)}) copy-start(bf16[3,64,512]{2,1,0:T(8,128)(2,1)} %param.21) | copy-start | bytes 589828
  27.8 18.2 %copy-start.5 = (bf16[512,64]{0,1:T(8,128)(2,1)S(1)}, bf16[512,64]{0,1:T(8,128)(2,1)}, u32[]{:S(2)}) copy-start(bf16[512,64]{0,1:T(8,128)(2,1)} %param.25) | copy-start | bytes 196612
  332.2 12.8 %copy-start.8 = (f32[4,1,512]{2,1,0:T(1,128)S(1)}, f32[4,1,512]{2,1,0:T(1,128)}, u32[]{:S(2)}) copy-start(f32[4,1,512]{2,1,0:T(1,128)} %get-tuple-element.63) | copy-start | bytes 24580
  332.2 13.9 %copy-start.6 = (f32[2,4,1024]{2,1,0:T(4,128)S(1)}, f32[2,4,1024]{2,1,0:T(4,128)}, u32[]{:S(2)}) copy-start(f32[2,4,1024]{2,1,0:T(4,128)} %get-tuple-element.60) | copy-start | bytes 98308
  348.2 33.0 %copy-start.7 = (bf16[2,1024]{1,0:T(2,128)(2,1)S(1)}, bf16[2,1024]{1,0:T(2,128)(2,1)}, u32[]{:S(2)}) copy-start(bf16[2,1024]{1,0:T(2,128)(2,1)} %param.17) | copy-start | bytes 12292
  349.0 35.4 %copy-start.1 = (f32[12,64,512]{2,1,0:T(8,128)S(1)}, f32[12,64,512]{2,1,0:T(8,128)}, u32[]{:S(2)}) copy-start(f32[12,64,512]{2,1,0:T(8,128)} %get-tuple-element.64) | copy-start | bytes 4718596
